TPU v7x, 32 devices: a whole 2x2x4 slice. The times are simulated.
32 devices in a mesh: theta: 8 (over y, x, core), phi: 4 (over z).
Axes of the slice: x: 2, y: 2, z: 4, core: 2. Of those that a mesh axis runs over, the one named last changes fastest.
Arguments:
- child_out: float32 [8, 192, 384, 128], P(None, 'theta', 'phi'), may hold values from -6 to 6
- child_slot: int32 [128], replicated, may hold values from 0 to 127, each once
- sources_child: int32 [128, 12], replicated, may hold values from 0 to 127
- kinds_child: int32 [128, 12], replicated, may hold values from 0 to 127
- table_child: float32 [2, 192, 384, 128], P(None, 'theta', 'phi'), may hold values from -4 to 4
- sources_parent: int32 [16, 12], replicated, may hold values from 0 to 15
- kinds_parent: int32 [16, 12], replicated, may hold values from 0 to 127
- table_parent: float32 [2, 352, 704, 128], P(None, 'theta', 'phi'), may hold values from -1.5 to 1.5
Outputs:
- child_in: float32 [8, 192, 384, 128], P(None, 'theta', 'phi')
Inputs may be any that keep to these rules, and one draw needn't show every extreme that they name: Each value occurs once; child b belongs to parent child_slot[b] % 16 as octant child_slot[b] // 16.
All inputs are finite; a program needn't handle non-finite values.
Results may differ from a plain program's by a relative error of at most 0.00012.
Values sent between devices are 32-bit elements; how exact they have to be, the bound alone decides.
No kernel may reach another device: no remote copies, remote signals or barrier semaphores. Data moves between devices by JAX's collectives and lax.ppermute only.
A program may use at most 256 MiB of HBM per device.

v0:
```python
import math

import jax
import jax.numpy as jnp
import numpy as np
from jax import lax
from jax.sharding import PartitionSpec as P

TH1 = 192
PH1 = 384
TH2 = 352
PH2 = 704
BAND1 = 180


def with_halo(block, sides, width, periodic):
    for axis, dim in sides:
        count = lax.axis_size(axis)
        forward = [(i, i + 1) for i in range(count - 1)]
        if periodic:
            forward.append((count - 1, 0))
        backward = [(target, source) for source, target in forward]
        low = lax.ppermute(
            lax.slice_in_dim(block, block.shape[dim] - width, None, axis=dim), axis, forward
        )
        high = lax.ppermute(lax.slice_in_dim(block, 0, width, axis=dim), axis, backward)
        block = jnp.concatenate([low, block, high], axis=dim)
    return block


def stencil_entries(count_out, count_in, centered, out_rows):
    entries = []
    for row_out in out_rows:
        if centered:
            numerator = (2 * row_out + 1) * count_in - count_out
        else:
            numerator = 2 * row_out * count_in
        denominator = 2 * count_out
        base_index = numerator // denominator
        fraction = (numerator - base_index * denominator) / denominator
        for offset_a in range(-2, 4):
            weight = 1.0
            for offset_b in range(-2, 4):
                if offset_b != offset_a:
                    weight = weight * (fraction - offset_b) / (offset_a - offset_b)
            entries.append((row_out, base_index + offset_a, weight))
    return entries


def local_up(count_out, count_in, centered, rows_out, rows_in):
    matrix = np.zeros((rows_out, rows_in + 6))
    for row_out, column, weight in stencil_entries(count_out, count_in, centered, range(rows_out)):
        matrix[row_out, column + 3] += weight
    return jnp.asarray(matrix, jnp.float32)


def local_down(count_out, count_in, centered, rows_out, rows_in, margin):
    matrix = np.zeros((rows_in, rows_out + 2 * margin))
    for row_out, column, weight in stencil_entries(
        count_out, count_in, centered, range(-margin, rows_out + margin)
    ):
        if 0 <= column < rows_in:
            matrix[column, row_out + margin] += weight
    return jnp.asarray(matrix, jnp.float32)


def phase_table(count_polar, count_azimuth, polar_first, azimuth_first, rows_here, columns_here):
    polar = ((jnp.arange(rows_here, dtype=jnp.int32) + polar_first).astype(jnp.float32) + 0.5) * (
        math.pi / count_polar
    )
    azimuth = (jnp.arange(columns_here, dtype=jnp.int32) + azimuth_first).astype(jnp.float32) * (
        2.0 * math.pi / count_azimuth
    )
    octant = jnp.arange(8, dtype=jnp.int32)
    east_sign = (2 * (octant % 2) - 1).astype(jnp.float32)
    north_sign = (2 * (octant // 2 % 2) - 1).astype(jnp.float32)
    upper_sign = (2 * (octant // 4) - 1).astype(jnp.float32)
    sin_polar = jnp.sin(polar)[:, None, None]
    cos_polar = jnp.cos(polar)[:, None, None]
    cos_azimuth = jnp.cos(azimuth)[None, :, None]
    sin_azimuth = jnp.sin(azimuth)[None, :, None]
    phase_angle = (
        BAND1
        / (2.0 * math.sqrt(3.0))
        * (
            sin_polar * cos_azimuth * east_sign
            + sin_polar * sin_azimuth * north_sign
            + cos_polar * upper_sign
        )
    )
    return jnp.stack([jnp.cos(phase_angle), jnp.sin(phase_angle)])


def complex_times(pattern, factor):
    halves = pattern.reshape((2, 4) + pattern.shape[1:])
    cosine = factor[0][None]
    sine_part = factor[1][None]
    real_out = halves[0] * cosine - halves[1] * sine_part
    imag_out = halves[0] * sine_part + halves[1] * cosine
    return jnp.concatenate([real_out, imag_out], axis=0)


def aggregate(grouped, phase):
    halves = grouped.reshape((2, 4) + grouped.shape[1:])
    cosine = phase[0][None, :, :, :, None]
    sine_part = phase[1][None, :, :, :, None]
    real_out = jnp.sum(halves[0] * cosine - halves[1] * sine_part, axis=3)
    imag_out = jnp.sum(halves[0] * sine_part + halves[1] * cosine, axis=3)
    return jnp.concatenate([real_out, imag_out], axis=0)


def translate(pattern, sources, kinds, table):

    def accumulate(summed, columns):
        source_column, kind_column = columns
        gathered = jnp.take(pattern, source_column, axis=3)
        factor = jnp.take(table, kind_column, axis=3)
        return (summed + complex_times(gathered, factor), None)

    start = jnp.zeros(pattern.shape[:3] + (sources.shape[0],), jnp.float32)
    summed, unused = lax.scan(accumulate, start, (sources.T, kinds.T))
    return summed


def per_device(
    child_out,
    child_slot,
    sources_child,
    kinds_child,
    table_child,
    sources_parent,
    kinds_parent,
    table_parent,
):
    exact_mode = lax.Precision.HIGHEST
    rows_child = child_out.shape[1]
    columns_child = child_out.shape[2]
    boxes_child = child_out.shape[3]
    rows_parent = table_parent.shape[1]
    columns_parent = table_parent.shape[2]
    boxes_parent = boxes_child // 8
    polar_up = local_up(TH2, TH1, True, rows_parent, rows_child)
    azimuth_up = local_up(PH2, PH1, False, columns_parent, columns_child)
    polar_index = lax.axis_index("theta")
    azimuth_index = lax.axis_index("phi")
    margin_columns = (3 * columns_parent + columns_child - 1) // columns_child + 1
    margin_rows = (3 * rows_parent + rows_child - 1) // rows_child + 1
    azimuth_down = local_down(PH2, PH1, False, columns_parent, columns_child, margin_columns)
    polar_down = local_down(TH2, TH1, True, rows_parent, rows_child, margin_rows)
    inverse = (
        jnp.zeros((boxes_child,), jnp.int32)
        .at[child_slot]
        .set(jnp.arange(boxes_child, dtype=jnp.int32))
    )
    padded = with_halo(child_out, (("theta", 1),), 3, False)
    row_pass = jnp.einsum("pt,ctfb->cpfb", polar_up, padded, precision=exact_mode)
    padded = with_halo(row_pass, (("phi", 2),), 3, True)
    upward = jnp.einsum("qf,cpfb->cpqb", azimuth_up, padded, precision=exact_mode)
    grouped = jnp.take(upward, inverse, axis=3).reshape(
        8, rows_parent, columns_parent, 8, boxes_parent
    )
    phase_up = phase_table(
        TH2,
        PH2,
        polar_index * rows_parent,
        azimuth_index * columns_parent,
        rows_parent,
        columns_parent,
    )
    parent_out = aggregate(grouped, phase_up)
    child_local = translate(child_out, sources_child, kinds_child, table_child)
    parent_in = translate(parent_out, sources_parent, kinds_parent, table_parent)
    widened = with_halo(parent_in, (("phi", 2),), margin_columns, True)
    columns_back = jnp.einsum("fq,cpqb->cpfb", azimuth_down, widened, precision=exact_mode)
    heightened = with_halo(columns_back, (("theta", 1),), margin_rows, False)
    lowered = jnp.einsum("tp,cpfb->ctfb", polar_down, heightened, precision=exact_mode)
    expanded = jnp.take(lowered, child_slot % boxes_parent, axis=3)
    phase_down = phase_table(
        TH1, PH1, polar_index * rows_child, azimuth_index * columns_child, rows_child, columns_child
    )
    octant_onehot = (
        jnp.arange(8, dtype=jnp.int32)[:, None] == (child_slot // boxes_parent)[None, :]
    ).astype(jnp.float32)
    box_phase = jnp.einsum("atfo,ob->atfb", phase_down, octant_onehot, precision=exact_mode)
    factor = jnp.stack([box_phase[0], -box_phase[1]])
    return complex_times(expanded, factor) + child_local


def solution(mesh):
    placed = (
        P(None, "theta", "phi", None),
        P(),
        P(),
        P(),
        P(None, "theta", "phi", None),
        P(),
        P(),
        P(None, "theta", "phi", None),
    )
    return jax.shard_map(
        per_device,
        mesh=mesh,
        in_specs=placed,
        out_specs=P(None, "theta", "phi", None),
        check_vma=False,
    )
```

profile of v0, /device:TPU:28, one launch (start us, length us, event | category | flops | bytes accessed | tf_op | source)
XLA Modules:
  0.0 1435.0 jit_solution(971638897615131425)
XLA Ops:
  9.7 11.7 copy.68
  28.4 604.9 %while.23 = (s32[]{:T(128)}, f32[8,24,96,128]{2,1,0,3:T(8,128)}, s32[12,128]{1,0:T(8,128)}, f32[8,24,96,128]{2,1,0,3:T(8,128)}, s32[12,128]{1,0:T(8,128)}, /*index=5*/f32[2,24,96,128]{2,1,3,0:T(8,128)}, s32[]{:T(128)}, s32[]{:T(128)}) while((s32[]{:T(128)}, f32[8,24,96,128]{2,1,0,3:T(8,128)}, s32[12,128]{1,0:T(8,128)}, ...), condition=%wide.region_6.7_spmd.clone, body=%wide.region_5.6_spmd.clone.sunk | while | flops 17109252 | bytes 101463648 | solution.py:121
  33.0 10.5 gather_fusion.2
  43.5 11.8 select_bitcast_fusion.12
  55.3 8.7 multiply_subtract_fusion.6
  64.0 12.3 maximum_add_fusion.6
  80.8 10.5 gather_fusion.2
  91.3 11.8 select_bitcast_fusion.12
  103.1 8.7 multiply_subtract_fusion.6
  111.8 15.1 %maximum_add_fusion.6 = f32[8,24,96,128]{2,1,0,3:T(8,128)} fusion(f32[4,24,96,128]{2,1,0,3:T(8,128)} %get-tuple-element.319, f32[4,24,96,128]{2,1,0,3:T(8,128)} %get-tuple-element.320, f32[8,24,96,128]{2,1,0,3:T(8,128)} %get-tuple-element.330, pred[]{:T(512)S(6)} %compare.23), kind=kLoop, calls=%fused_computation.26.clone.1 | loop fusion | flops 7077888 | bytes 28311552 | tf_op jit(solution)/shard_map/while/body/eval_jaxpr/add | solution.py:118
  131.5 10.5 gather_fusion.2
  141.9 11.8 select_bitcast_fusion.12
  153.7 8.7 multiply_subtract_fusion.6
  162.4 15.1 %maximum_add_fusion.6 = f32[8,24,96,128]{2,1,0,3:T(8,128)} fusion(f32[4,24,96,128]{2,1,0,3:T(8,128)} %get-tuple-element.319, f32[4,24,96,128]{2,1,0,3:T(8,128)} %get-tuple-element.320, f32[8,24,96,128]{2,1,0,3:T(8,128)} %get-tuple-element.330, pred[]{:T(512)S(6)} %compare.23), kind=kLoop, calls=%fused_computation.26.clone.1 | loop fusion | flops 7077888 | bytes 28311552 | tf_op jit(solution)/shard_map/while/body/eval_jaxpr/add | solution.py:118
  182.1 10.5 gather_fusion.2
  192.6 11.8 select_bitcast_fusion.12
  204.4 8.7 multiply_subtract_fusion.6
  213.1 15.1 %maximum_add_fusion.6 = f32[8,24,96,128]{2,1,0,3:T(8,128)} fusion(f32[4,24,96,128]{2,1,0,3:T(8,128)} %get-tuple-element.319, f32[4,24,96,128]{2,1,0,3:T(8,128)} %get-tuple-element.320, f32[8,24,96,128]{2,1,0,3:T(8,128)} %get-tuple-element.330, pred[]{:T(512)S(6)} %compare.23), kind=kLoop, calls=%fused_computation.26.clone.1 | loop fusion | flops 7077888 | bytes 28311552 | tf_op jit(solution)/shard_map/while/body/eval_jaxpr/add | solution.py:118
  232.8 10.5 gather_fusion.2
  243.2 11.8 select_bitcast_fusion.12
  255.0 8.7 multiply_subtract_fusion.6
  263.7 15.1 %maximum_add_fusion.6 = f32[8,24,96,128]{2,1,0,3:T(8,128)} fusion(f32[4,24,96,128]{2,1,0,3:T(8,128)} %get-tuple-element.319, f32[4,24,96,128]{2,1,0,3:T(8,128)} %get-tuple-element.320, f32[8,24,96,128]{2,1,0,3:T(8,128)} %get-tuple-element.330, pred[]{:T(512)S(6)} %compare.23), kind=kLoop, calls=%fused_computation.26.clone.1 | loop fusion | flops 7077888 | bytes 28311552 | tf_op jit(solution)/shard_map/while/body/eval_jaxpr/add | solution.py:118
  283.4 10.5 gather_fusion.2
  293.9 11.8 select_bitcast_fusion.12
  314.4 15.1 %maximum_add_fusion.6 = f32[8,24,96,128]{2,1,0,3:T(8,128)} fusion(f32[4,24,96,128]{2,1,0,3:T(8,128)} %get-tuple-element.319, f32[4,24,96,128]{2,1,0,3:T(8,128)} %get-tuple-element.320, f32[8,24,96,128]{2,1,0,3:T(8,128)} %get-tuple-element.330, pred[]{:T(512)S(6)} %compare.23), kind=kLoop, calls=%fused_computation.26.clone.1 | loop fusion | flops 7077888 | bytes 28311552 | tf_op jit(solution)/shard_map/while/body/eval_jaxpr/add | solution.py:118
  334.0 10.5 gather_fusion.2
  344.5 11.8 select_bitcast_fusion.12
  356.3 8.7 multiply_subtract_fusion.6
  365.0 15.1 %maximum_add_fusion.6 = f32[8,24,96,128]{2,1,0,3:T(8,128)} fusion(f32[4,24,96,128]{2,1,0,3:T(8,128)} %get-tuple-element.319, f32[4,24,96,128]{2,1,0,3:T(8,128)} %get-tuple-element.320, f32[8,24,96,128]{2,1,0,3:T(8,128)} %get-tuple-element.330, pred[]{:T(512)S(6)} %compare.23), kind=kLoop, calls=%fused_computation.26.clone.1 | loop fusion | flops 7077888 | bytes 28311552 | tf_op jit(solution)/shard_map/while/body/eval_jaxpr/add | solution.py:118
  384.7 10.5 gather_fusion.2
  395.2 11.8 select_bitcast_fusion.12
  407.0 8.7 multiply_subtract_fusion.6
  415.7 15.1 %maximum_add_fusion.6 = f32[8,24,96,128]{2,1,0,3:T(8,128)} fusion(f32[4,24,96,128]{2,1,0,3:T(8,128)} %get-tuple-element.319, f32[4,24,96,128]{2,1,0,3:T(8,128)} %get-tuple-element.320, f32[8,24,96,128]{2,1,0,3:T(8,128)} %get-tuple-element.330, pred[]{:T(512)S(6)} %compare.23), kind=kLoop, calls=%fused_computation.26.clone.1 | loop fusion | flops 7077888 | bytes 28311552 | tf_op jit(solution)/shard_map/while/body/eval_jaxpr/add | solution.py:118
  435.3 10.5 gather_fusion.2
  445.8 11.8 select_bitcast_fusion.12
  457.6 8.7 multiply_subtract_fusion.6
  466.3 15.1 %maximum_add_fusion.6 = f32[8,24,96,128]{2,1,0,3:T(8,128)} fusion(f32[4,24,96,128]{2,1,0,3:T(8,128)} %get-tuple-element.319, f32[4,24,96,128]{2,1,0,3:T(8,128)} %get-tuple-element.320, f32[8,24,96,128]{2,1,0,3:T(8,128)} %get-tuple-element.330, pred[]{:T(512)S(6)} %compare.23), kind=kLoop, calls=%fused_computation.26.clone.1 | loop fusion | flops 7077888 | bytes 28311552 | tf_op jit(solution)/shard_map/while/body/eval_jaxpr/add | solution.py:118
  486.0 10.5 gather_fusion.2
  496.5 11.8 select_bitcast_fusion.12
  517.0 15.1 %maximum_add_fusion.6 = f32[8,24,96,128]{2,1,0,3:T(8,128)} fusion(f32[4,24,96,128]{2,1,0,3:T(8,128)} %get-tuple-element.319, f32[4,24,96,128]{2,1,0,3:T(8,128)} %get-tuple-element.320, f32[8,24,96,128]{2,1,0,3:T(8,128)} %get-tuple-element.330, pred[]{:T(512)S(6)} %compare.23), kind=kLoop, calls=%fused_computation.26.clone.1 | loop fusion | flops 7077888 | bytes 28311552 | tf_op jit(solution)/shard_map/while/body/eval_jaxpr/add | solution.py:118
  536.6 10.5 gather_fusion.2
  547.1 11.8 select_bitcast_fusion.12
  567.6 15.1 %maximum_add_fusion.6 = f32[8,24,96,128]{2,1,0,3:T(8,128)} fusion(f32[4,24,96,128]{2,1,0,3:T(8,128)} %get-tuple-element.319, f32[4,24,96,128]{2,1,0,3:T(8,128)} %get-tuple-element.320, f32[8,24,96,128]{2,1,0,3:T(8,128)} %get-tuple-element.330, pred[]{:T(512)S(6)} %compare.23), kind=kLoop, calls=%fused_computation.26.clone.1 | loop fusion | flops 7077888 | bytes 28311552 | tf_op jit(solution)/shard_map/while/body/eval_jaxpr/add | solution.py:118
  587.3 10.5 gather_fusion.2
  597.7 11.8 select_bitcast_fusion.12
  618.2 15.1 %maximum_add_fusion.6 = f32[8,24,96,128]{2,1,0,3:T(8,128)} fusion(f32[4,24,96,128]{2,1,0,3:T(8,128)} %get-tuple-element.319, f32[4,24,96,128]{2,1,0,3:T(8,128)} %get-tuple-element.320, f32[8,24,96,128]{2,1,0,3:T(8,128)} %get-tuple-element.330, pred[]{:T(512)S(6)} %compare.23), kind=kLoop, calls=%fused_computation.26.clone.1 | loop fusion | flops 7077888 | bytes 28311552 | tf_op jit(solution)/shard_map/while/body/eval_jaxpr/add | solution.py:118
  633.3 12.7 copy.47
  646.1 12.5 copy.59
  664.5 20.3 %fusion.15 = f32[8,44,96,128]{3,1,2,0:T(8,128)S(1)} fusion(f32[44,30,1,1]{0,1,3,2:T(8,128)S(1)} %copy-done.14, f32[8,3,96,128]{3,1,2,0:T(4,128)S(1)} %copy.48, f32[8,24,96,128]{3,1,2,0:T(8,128)} %copy.47, f32[8,3,96,128]{3,1,2,0:T(4,128)S(1)} %copy.46), kind=kOutput, calls=%fused_computation.60 | convolution fusion | flops 1563033600 | bytes 29103264 | tf_op jit(solution)/shard_map/pt,ctfb->cpfb/dot_general | solution.py:156
  692.0 18.0 %collective-permute-done.2 = f32[8,44,3,128]{3,0,2,1:T(8,128)S(1)} collective-permute-done((f32[8,44,3,128]{3,0,2,1:T(8,128)S(1)}, f32[8,44,3,128]{3,0,2,1:T(8,128)S(1)}, u32[]{:S(2)}, u32[]{:S(2)}) %collective-permute-start.2) | collective-permute-done | bytes 540704 | tf_op jit(solution)/shard_map/ppermute | solution.py:23
  718.5 32.0 %fusion.12 = f32[8,44,176,128]{3,2,1,0:T(8,128)} fusion(f32[176,102,1,1]{1,0,3,2:T(8,128)S(1)} %copy-done.13, f32[8,44,102,128]{3,1,2,0:T(8,128)S(1)} %pad_maximum_fusion), kind=kOutput, calls=%fused_computation.59 | convolution fusion | flops 9706143744 | bytes 50174080 | tf_op jit(solution)/shard_map/qf,cpfb->cpqb/dot_general | solution.py:158
  750.5 47.3 %copy.54 = f32[8,44,176,128]{2,1,0,3:T(8,128)} copy(f32[8,44,176,128]{3,2,1,0:T(8,128)} %fusion.12) | data formatting | bytes 63438848 | tf_op jit(solution)/shard_map/qf,cpfb->cpqb/transpose | solution.py:158
  797.8 35.4 %gather_fusion.4 = f32[128,8,44,176]{3,2,1,0:T(8,128)} fusion(f32[8,44,176,128]{2,1,0,3:T(8,128)} %copy.54, s32[1024]{0:T(1024)} %pad_clamp_fusion.5), kind=kCustom, calls=%fused_computation.4 | custom fusion | bytes 63439360 | tf_op jit(solution)/shard_map/jit(_take)/gather | solution.py:159
  833.2 36.5 %select_bitcast_fusion.4 = f32[8,44,176,128]{2,1,0,3:T(8,128)} fusion(f32[128,8,44,176]{3,2,1,0:T(8,128)} %gather_fusion.4, pred[128]{0:T(512)(128)(4,1)S(1)} %compare_and_fusion.4), kind=kLoop, calls=%fused_computation.45 | loop fusion | flops 7929856 | bytes 63438976 | tf_op jit(solution)/shard_map/jit(_take)/select_n | solution.py:159
  869.7 34.2 %fusion.67 = (f32[4,44,176,128]{2,1,0,3:T(8,128)}, f32[4,44,176,128]{2,1,0,3:T(8,128)}) fusion(f32[8,44,176,128]{2,1,0,3:T(8,128)} %select_bitcast_fusion.4), kind=kLoop, calls=%fused_computation.147 | loop fusion | bytes 63438848 | tf_op jit(solution)/shard_map/slice | solution.py:107
  903.8 27.0 %copy.55 = f32[4,44,176,128]{2,3,1,0:T(8,128)} copy(f32[4,44,176,128]{2,1,0,3:T(8,128)} %get-tuple-element.181) | data formatting | bytes 31719424 | tf_op jit(solution)/shard_map/slice | solution.py:107
  930.8 26.5 %copy.56 = f32[4,44,176,128]{2,3,1,0:T(8,128)} copy(f32[4,44,176,128]{2,1,0,3:T(8,128)S(1)} %copy-done) | data formatting | bytes 31719424 | tf_op jit(solution)/shard_map/slice | solution.py:107
  957.3 17.8 %subtract_reduce_fusion = (f32[4,44,176,16]{2,3,1,0:T(8,128)S(1)}, f32[4,44,176,16]{2,3,1,0:T(8,128)S(1)}) fusion(f32[4,44,176,8,16]{2,4,3,1,0:T(8,128)} %bitcast.108, f32[4,44,176,8,16]{2,4,3,1,0:T(8,128)} %bitcast.107, f32[44,176,8]{1,2,0:T(8,128)S(1)} %copy-done.9, f32[44,176,8]{1,2,0:T(8,128)S(1)} %copy-done.8), kind=kLoop, calls=%fused_computation.47 | loop fusion | flops 30728192 | bytes 36179968 | tf_op jit(solution)/shard_map/reduce_sum | solution.py:107
  983.9 338.2 %while.22 = (s32[]{:T(128)}, f32[8,44,176,16]{2,0,1,3:T(8,128)}, s32[12,16]{1,0:T(8,128)}, f32[8,44,176,16]{2,0,3,1:T(8,128)}, s32[12,16]{1,0:T(8,128)}, /*index=5*/f32[2,44,176,128]{2,1,0,3:T(8,128)}, s32[]{:T(128)}, s32[]{:T(128)}) while((s32[]{:T(128)}, f32[8,44,176,16]{2,0,1,3:T(8,128)}, s32[12,16]{1,0:T(8,128)}, ...), condition=%wide.region_4.5_spmd.clone, body=%wide.region_3.4_spmd.clone.sunk | while | flops 7188771 | bytes 46596956 | solution.py:121
  1322.1 9.5 copy.60
  1358.3 8.9 fusion.26
  1393.3 12.0 select_bitcast_fusion.5
  1411.2 11.7 maximum_add_fusion.2
  1422.9 11.7 copy.70
  (390 shorter events, 532.7 us)
Async XLA Ops:
  3.2 657.1 %collective-permute-start = (f32[8,3,96,128]{3,2,1,0:T(8,128)}, f32[8,3,96,128]{3,2,1,0:T(8,128)}, u32[]{:S(2)}, u32[]{:S(2)}) collective-permute-start(f32[8,3,96,128]{3,2,1,0:T(8,128)} %get-tuple-element.189), channel_id=1, source_target_pairs={{0,4},{4,8},{8,12},{12,16},{16,20},{20,24},{24,28},{1,5},{5,9},{9,... | collective-permute-start | bytes 3538952 | tf_op jit(solution)/shard_map/ppermute | solution.py:23
  5.2 657.3 %collective-permute-start.1 = (f32[8,3,96,128]{3,2,1,0:T(8,128)}, f32[8,3,96,128]{3,2,1,0:T(8,128)}, u32[]{:S(2)}, u32[]{:S(2)}) collective-permute-start(f32[8,3,96,128]{3,2,1,0:T(8,128)} %get-tuple-element.190), channel_id=1, source_target_pairs={{4,0},{8,4},{12,8},{16,12},{20,16},{24,20},{28,24},{5,1},{9,5},{13... | collective-permute-start | bytes 3538952 | tf_op jit(solution)/shard_map/ppermute | solution.py:26
  9.7 13.0 copy-start.27
  9.7 16.3 %copy-start.7 = (f32[2,24,96,128]{3,2,1,0:T(8,128)S(1)}, f32[2,24,96,128]{3,2,1,0:T(8,128)}, u32[]{:S(2)}) copy-start(f32[2,24,96,128]{3,2,1,0:T(8,128)} %param.20) | copy-start | bytes 7077892
  24.2 4.1 copy-start.29
  646.1 12.6 copy-start.16
  646.1 13.3 copy-start.17
  646.1 13.9 copy-start.30
  646.1 13.9 copy-start.25
  646.1 14.0 copy-start.21
  646.1 14.1 copy-start.22
  646.1 14.1 copy-start.23
  646.1 14.1 copy-start.24
  646.1 14.1 copy-start.18
  646.1 14.1 copy-start.19
  646.1 14.1 copy-start.20
  646.1 18.4 %copy-start.14 = (f32[44,30,1,1]{0,1,3,2:T(8,128)S(1)}, f32[44,30,1,1]{0,1,3,2:T(8,128)}, u32[]{:S(2)}) copy-start(f32[44,30,1,1]{0,1,3,2:T(8,128)} %constant.234) | copy-start | bytes 15844
  684.9 25.2 %copy-start.1 = (f32[8,44,96,128]{3,1,2,0:T(8,128)}, f32[8,44,96,128]{3,1,2,0:T(8,128)S(1)}, u32[]{:S(2)}) copy-start(f32[8,44,96,128]{3,1,2,0:T(8,128)S(1)} %fusion.15) | copy-start | bytes 51904516
  685.2 24.8 %collective-permute-start.2 = (f32[8,44,3,128]{3,0,2,1:T(8,128)S(1)}, f32[8,44,3,128]{3,0,2,1:T(8,128)S(1)}, u32[]{:S(2)}, u32[]{:S(2)}) collective-permute-start(f32[8,44,3,128]{3,0,2,1:T(8,128)S(1)} %copy.49), channel_id=1, source_target_pairs={{0,1},{1,2},{2,3},{3,0},{4,5},{5,6},{6,7},{7,4},{8,9},{9,10},{10,1... | collective-permute-start | bytes 1622024 | tf_op jit(solution)/shard_map/ppermute | solution.py:23
  685.6 24.4 %collective-permute-start.3 = (f32[8,44,3,128]{3,0,2,1:T(8,128)S(1)}, f32[8,44,3,128]{3,0,2,1:T(8,128)S(1)}, u32[]{:S(2)}, u32[]{:S(2)}) collective-permute-start(f32[8,44,3,128]{3,0,2,1:T(8,128)S(1)} %copy.50), channel_id=1, source_target_pairs={{1,0},{2,1},{3,2},{0,3},{5,4},{6,5},{7,6},{4,7},{9,8},{10,9},{11,1... | collective-permute-start | bytes 1622024 | tf_op jit(solution)/shard_map/ppermute | solution.py:26
  710.2 8.2 copy-start.13
  903.8 27.0 %copy-start = (f32[4,44,176,128]{2,1,0,3:T(8,128)S(1)}, f32[4,44,176,128]{2,1,0,3:T(8,128)}, u32[]{:S(2)}) copy-start(f32[4,44,176,128]{2,1,0,3:T(8,128)} %get-tuple-element.182) | copy-start | bytes 47579140
  930.8 26.5 %copy-start.8 = (f32[44,176,8]{1,2,0:T(8,128)S(1)}, f32[44,176,8]{1,2,0:T(8,128)}, u32[]{:S(2)}) copy-start(f32[44,176,8]{1,2,0:T(8,128)} %get-tuple-element.195) | copy-start | bytes 743428
  930.8 26.5 %copy-start.9 = (f32[44,176,8]{1,2,0:T(8,128)S(1)}, f32[44,176,8]{1,2,0:T(8,128)}, u32[]{:S(2)}) copy-start(f32[44,176,8]{1,2,0:T(8,128)} %get-tuple-element.196) | copy-start | bytes 743428
  998.2 3.4 copy-start.2
  998.2 3.4 copy-start.3
  1024.8 3.4 copy-start.2
  1024.8 3.4 copy-start.3
  1053.2 3.4 copy-start.2
  1053.2 3.4 copy-start.3
  1081.5 3.4 copy-start.2
  1081.5 3.4 copy-start.3
  1109.9 3.4 copy-start.2
  1109.9 3.4 copy-start.3
  1138.2 3.4 copy-start.2
  1138.2 3.4 copy-start.3
  1166.6 3.4 copy-start.2
  1166.6 3.4 copy-start.3
  1194.9 3.4 copy-start.2
  1194.9 3.4 copy-start.3
  1223.2 3.4 copy-start.2
  1223.2 3.4 copy-start.3
  1251.5 3.4 copy-start.2
  1251.5 3.4 copy-start.3
  1279.7 3.4 copy-start.2
  1279.7 3.4 copy-start.3
  1308.0 3.4 copy-start.2
  1308.0 3.4 copy-start.3
  1322.1 13.1 copy-start.10
  1322.1 13.1 copy-start.11
  1322.1 13.1 copy-start.26
  1332.9 14.3 collective-permute-start.4
  1334.5 21.1 %collective-permute-start.5 = (f32[8,44,7,16]{1,3,2,0:T(8,128)S(1)}, f32[8,44,7,16]{1,3,2,0:T(8,128)S(1)}, u32[]{:S(2)}, u32[]{:S(2)}) collective-permute-start(f32[8,44,7,16]{1,3,2,0:T(8,128)S(1)} %get-tuple-element.188), channel_id=1, source_target_pairs={{1,0},{2,1},{3,2},{0,3},{5,4},{6,5},{7,6},{4,7},{9,8},{10,9},{11,1... | collective-permute-start | bytes 473096 | tf_op jit(solution)/shard_map/ppermute | solution.py:26
  1347.2 11.1 copy-start.12
  1358.3 16.5 %copy-start.4 = (f32[2,24,96,128]{3,2,1,0:T(8,128)S(1)}, f32[2,24,96,128]{3,2,1,0:T(8,128)}, u32[]{:S(2)}) copy-start(f32[2,24,96,128]{3,2,1,0:T(8,128)} %fusion.35) | copy-start | bytes 7077892
  1367.2 15.0 %copy-start.28 = (s32[128]{0:T(128)S(1)}, s32[128]{0:T(128)}, u32[]{:S(2)}) copy-start(s32[128]{0:T(128)} %param.17) | copy-start | bytes 1540
  1368.1 14.2 collective-permute-start.6
  1370.0 12.2 collective-permute-start.7
  1379.3 4.5 copy-start.15
  1393.3 12.0 copy-start.5
  1393.3 12.0 copy-start.6
where the time goes:
time: 1450 us; the launch traced here: 1430 us
  other arithmetic  735 us (51%)
  local copies, waits for them, and re-layouts  588 us (41%)
  matrix products  68.3 us (5%)
  waiting for transfers between devices  23.9 us (2%)
  starting transfers between devices  17.6 us (1%)
    add x24, other arithmetic, accumulate(): return (summed + complex_times(gathered, factor), None)  268 us
    gather x24, local copies, waits for them, and re-layouts, accumulate(): gathered = jnp.take(pattern, source_column, axis=3)  199 us
    select_n x48, other arithmetic, accumulate(): gathered = jnp.take(pattern, source_column, axis=3)  199 us
    sub x25, other arithmetic, complex_times(): real_out = halves[0] * cosine - halves[1] * sine_part  147 us
    gather x24, local copies, waits for them, and re-layouts, accumulate(): factor = jnp.take(table, kind_column, axis=3)  94.3 us
    slice x3, local copies, waits for them, and re-layouts, aggregate(): real_out = jnp.sum(halves[0] * cosine - halves[1] * sine_part, axis=3)  87.6 us
    unnamed x65, local copies, waits for them, and re-layouts  48.6 us
    transpose x1, local copies, waits for them, and re-layouts, per_device(): jnp.einsum('qf,cpfb->cpqb', azimuth_up, padded, precision=exact_mode)  47.3 us
  transfers between devices with their start and end apart: 8, of which 2 were waited for; matrix products, arithmetic and copies ran while one was open for 47% of the time, Pallas kernels for 0%

commit v1 on v0

v1 whole, which is shorter than its diff:
```python
import functools
import math

import jax
import jax.numpy as jnp
import numpy as np
from jax import lax
from jax.experimental import pallas as pl
from jax.experimental.pallas import tpu as pltpu
from jax.sharding import PartitionSpec as P

BAND1 = 180
WAVE = BAND1 / (2.0 * math.sqrt(3.0))
LANES = 128
MIB = 1 << 20
F32 = jnp.float32
BF16 = jnp.bfloat16


def round_up(count, step):
    return -(-count // step) * step


def stencil_entries(count_out, count_in, centered, out_rows):
    entries = []
    for row_out in out_rows:
        if centered:
            numerator = (2 * row_out + 1) * count_in - count_out
        else:
            numerator = 2 * row_out * count_in
        denominator = 2 * count_out
        base_index = numerator // denominator
        fraction = (numerator - base_index * denominator) / denominator
        for offset_a in range(-2, 4):
            weight = 1.0
            for offset_b in range(-2, 4):
                if offset_b != offset_a:
                    weight = weight * (fraction - offset_b) / (offset_a - offset_b)
            entries.append((row_out, base_index + offset_a, weight))
    return entries


def local_up(count_out, count_in, centered, rows_out, rows_in, below, shape):
    matrix = np.zeros(shape)
    for row_out, column, weight in stencil_entries(count_out, count_in, centered, range(rows_out)):
        assert -below <= column < rows_in + 3 or abs(weight) < 1e-12
        if column >= 0:
            matrix[row_out, column] += weight
        elif column >= -below:
            matrix[row_out, rows_in + 3 + below + column] += weight
    return matrix.astype(np.float32)


def split(x):
    high = x.astype(BF16)
    return high, (x - high.astype(F32)).astype(BF16)


def split_constant(matrix):
    high = matrix.astype(jnp.bfloat16)
    return high, (matrix - high.astype(np.float32)).astype(jnp.bfloat16)


def dot(a, b):
    return jnp.dot(a, b, preferred_element_type=F32)


def dot_transposed(a, b):
    return lax.dot_general(a, b, (((1,), (1,)), ((), ())), preferred_element_type=F32)


def local_kernel(entries, child_ref, table_ref, source_ref, kind_ref, *rest):
    out_ref = rest[-1]
    rows, columns = child_ref.shape[1], child_ref.shape[2]

    def one_tile(step, carry):
        row = step // (columns // 8)
        at = pl.ds(pl.multiple_of(step % (columns // 8) * 8, 8), 8)
        pattern = [child_ref[c, row, at, :] for c in range(8)]
        table = [table_ref[c, row, at, :] for c in range(2)]
        total = [None] * 8
        for entry in range(entries):
            source, kind = source_ref[entry], kind_ref[entry]
            real, imag = (jnp.take_along_axis(t, kind, axis=1, mode="promise_in_bounds") for t in table)
            for c in range(4):
                x = jnp.take_along_axis(pattern[c], source, axis=1, mode="promise_in_bounds")
                y = jnp.take_along_axis(pattern[4 + c], source, axis=1, mode="promise_in_bounds")
                re = x * real - y * imag
                im = x * imag + y * real
                total[c] = re if entry == 0 else total[c] + re
                total[4 + c] = im if entry == 0 else total[4 + c] + im
        for c in range(8):
            out_ref[c, row, at, :] = total[c]
        return carry

    lax.fori_loop(0, rows * (columns // 8), one_tile, 0)


def child_translate(child_out, table, sources, kinds, first, count, onto):
    _, rows, columns, boxes = child_out.shape
    entries = sources.shape[0]
    block = next(b for b in (4, 3, 2, 1) if count % b == 0 and first % b == 0)
    at = first // block

    def place(i):
        return (0, at + i, 0, 0)

    whole = pl.BlockSpec((entries, 8, boxes), lambda i: (0, 0, 0))
    in_specs = [
        pl.BlockSpec((8, block, columns, boxes), place),
        pl.BlockSpec((2, block, columns, boxes), place),
        whole,
        whole,
    ]
    operands = [child_out, table, sources, kinds]
    aliases = {}
    if onto is not None:
        in_specs.append(pl.BlockSpec(memory_space=pl.ANY))
        operands.append(onto)
        aliases = {4: 0}
    samples = count * columns * boxes
    return pl.pallas_call(
        functools.partial(local_kernel, entries),
        grid=(count // block,),
        in_specs=in_specs,
        out_specs=pl.BlockSpec((8, block, columns, boxes), place),
        out_shape=jax.ShapeDtypeStruct(child_out.shape, F32),
        input_output_aliases=aliases,
        compiler_params=pltpu.CompilerParams(vmem_limit_bytes=40 * MIB),
        cost_estimate=pl.CostEstimate(
            flops=samples * entries * 32, bytes_accessed=samples * 72, transcendentals=0
        ),
        name="child_translate",
    )(*operands)


def parent_kernel(
    sizes,
    source_ref,
    kind_ref,
    child_ref,
    next_ref,
    previous_ref,
    side_ref,
    table_ref,
    combine_ref,
    polar_cos_ref,
    polar_sin_ref,
    azimuth_up_ref,
    polar_down_ref,
    azimuth_down_ref,
    phase_ref,
    out_ref,
    wide,
    rows_done,
    table_by_kind,
    parent_out,
    in_high,
    in_low,
    lowered,
):
    (rows, columns, rows_up, columns_up, parents, entries, table_steps, table_rows) = sizes
    t_pad, p_pad, f_pad, q_pad = wide.shape[1] // 128, parent_out.shape[3], wide.shape[2], parent_out.shape[4]
    step = pl.program_id(0)
    half = 4 * parents

    @pl.when(step == 0)
    def _():
        for part in range(2):
            for t in range(rows + 6, t_pad):
                wide[part, pl.ds(t, 128, stride=t_pad), :] = jnp.zeros((128, f_pad), F32)
        for part in range(2):
            for p in range(rows_up, p_pad):
                for lane in range(0, q_pad, LANES):
                    table_by_kind[lane // LANES, pl.ds(part * p_pad + p, 128, stride=2 * p_pad), :] = jnp.zeros(
                        (128, LANES), F32
                    )

    @pl.when(step < table_steps)
    def _():
        def one_row(r, carry):
            for part in range(2):
                x = table_ref[part, r]
                if q_pad > columns_up:
                    x = jnp.concatenate([x, jnp.zeros((q_pad - columns_up, LANES), F32)], axis=0)
                for lane in range(0, q_pad, LANES):
                    turned = x[lane : lane + LANES].T
                    at = pl.ds(part * p_pad + step * table_rows + r, 128, stride=2 * p_pad)
                    table_by_kind[lane // LANES, at, :] = turned
            return carry

        lax.fori_loop(0, table_rows, one_row, 0)

    combine = combine_ref[...]

    def turn(main_ref, r, t):
        for part in range(2):
            x = jnp.concatenate(
                [
                    main_ref[part, 0, r],
                    side_ref[part, 0, t],
                    jnp.zeros((f_pad - columns - 8, LANES), F32),
                ],
                axis=0,
            )
            high, low = split(x)
            wide[part, pl.ds(t, 128, stride=t_pad), :] = dot_transposed(
                combine, jnp.concatenate([high, low], axis=1)
            )

    def main_row(r, carry):
        turn(child_ref, r, r)
        return carry

    def edge_row(r, carry):
        turn(next_ref, r, rows + r)
        turn(previous_ref, r, rows + 3 + r)
        return carry

    lax.fori_loop(0, rows, main_row, 0)
    lax.fori_loop(0, 3, edge_row, 0)

    polar = []
    for sign in (-1.0, 1.0):
        both = jnp.concatenate([polar_cos_ref[...], sign * polar_sin_ref[...]], axis=1)
        high, low = split(both)
        polar.append(jnp.concatenate([high, high, low], axis=1))
    azimuth = azimuth_up_ref[...]
    for part in range(2):
        for kind in range(2):
            for difference in range(2):
                first = (kind * 2 + difference) * parents

                def one_pair(pair, carry, part=part, first=first):
                    at = first + 2 * pair
                    stacked = []
                    for source, offset in ((part, 0), (1 - part, half)):
                        stacked.append(
                            jnp.concatenate(
                                [
                                    wide[source, pl.ds(pl.multiple_of((offset + at + i) * t_pad, 8), t_pad), :]
                                    for i in range(2)
                                ],
                                axis=1,
                            )
                        )
                    high, low = split(jnp.concatenate(stacked, axis=0))
                    result = dot(polar[part], jnp.concatenate([high, low, high], axis=0))
                    high, low = split(result)
                    for i in range(2):
                        lanes = slice(i * f_pad, (i + 1) * f_pad)
                        rows_done[pl.ds(pl.multiple_of((2 * pair + i) * p_pad, 16), p_pad), :] = jnp.concatenate(
                            [high[:, lanes], low[:, lanes], high[:, lanes]], axis=1
                        )
                    return carry

                lax.fori_loop(0, parents // 2, one_pair, 0)
                target = part if difference == 0 else 1 - part
                phase = phase_ref[2 * kind + difference]
                if difference == 1 and part == 1:
                    phase = -phase
                fresh = kind == 0 and difference == part

                starts = kind == 0 and part == 0

                def one_group(group, carry, target=target, phase=phase, starts=starts):
                    per = 4
                    x = rows_done[pl.ds(pl.multiple_of(group * per * p_pad, 16), per * p_pad), :]
                    y = dot(x, azimuth)
                    for i in range(per):
                        term = y[i * p_pad : (i + 1) * p_pad] * phase
                        if starts:
                            parent_out[target, step, group * per + i] = term
                        else:
                            parent_out[target, step, group * per + i] += term
                    return carry

                lax.fori_loop(0, parents // 4, one_group, 0)

    @pl.when(step == 3)
    def _():
        tiles = q_pad // LANES

        def one_tile(tile, carry):
            box = tile // (p_pad // 16)
            row = tile % (p_pad // 16) * 16
            sources = [source_ref[box, e] for e in range(entries)]
            kinds = [kind_ref[box, e] * (2 * p_pad) + row for e in range(entries)]
            for lane_tile in range(tiles):
                lanes = slice(lane_tile * LANES, (lane_tile + 1) * LANES)
                total = [None] * 8
                for e in range(entries):
                    real = table_by_kind[lane_tile, pl.ds(pl.multiple_of(kinds[e], 16), 16), :]
                    imag = table_by_kind[lane_tile, pl.ds(pl.multiple_of(kinds[e] + p_pad, 16), 16), :]
                    for c in range(4):
                        x = parent_out[0, c, sources[e], pl.ds(pl.multiple_of(row, 16), 16), lanes]
                        y = parent_out[1, c, sources[e], pl.ds(pl.multiple_of(row, 16), 16), lanes]
                        re = x * real - y * imag
                        im = x * imag + y * real
                        total[c] = re if e == 0 else total[c] + re
                        total[4 + c] = im if e == 0 else total[4 + c] + im
                for c in range(8):
                    high, low = split(total[c])
                    at = pl.ds(pl.multiple_of((c * parents + box) * p_pad + row, 16), 16)
                    in_high[at, lanes] = high
                    in_low[at, lanes] = low
            return carry

        lax.fori_loop(0, parents * (p_pad // 16), one_tile, 0)

        down = azimuth_down_ref[...]
        down_high = down[:, :f_pad]
        high, low = split(polar_down_ref[...])
        polar_back = jnp.concatenate([high, high, low], axis=1)
        per = 4

        def one_group(group, carry):
            at = pl.ds(pl.multiple_of(group * per * p_pad, 16), per * p_pad)
            high = in_high[at, :]
            low = in_low[at, :]
            both = dot(high, down)
            y = both[:, :f_pad] + both[:, f_pad:] + dot(low, down_high)
            for i in range(0, per, 2):
                x = jnp.concatenate([y[i * p_pad : (i + 1) * p_pad], y[(i + 1) * p_pad : (i + 2) * p_pad]], axis=1)
                high, low = split(x)
                z = dot(polar_back, jnp.concatenate([high, low, high], axis=0))
                for j in range(2):
                    lowered[pl.ds(pl.multiple_of((group * per + i + j) * t_pad, 8), t_pad), :] = z[
                        :, j * f_pad : (j + 1) * f_pad
                    ]
            return carry

        lax.fori_loop(0, 8 * parents // per, one_group, 0)

        def one_row(t, carry):
            turned = lowered[pl.ds(t, 8 * parents, stride=t_pad), :].T
            out_ref[t] = turned[: columns + 8]
            return carry

        lax.fori_loop(0, rows + 6, one_row, 0)


def parent_level(child_out, after, before, side, table, sources, kinds, combine, polar_cos, polar_sin, phase):
    _, rows, columns, boxes = child_out.shape
    _, rows_up, columns_up, translators = table.shape
    assert boxes == LANES and translators == LANES
    parents, entries = sources.shape
    t_pad, p_pad = polar_cos.shape[1], polar_cos.shape[0]
    f_pad, q_pad = round_up(columns + 8, LANES), round_up(columns_up, LANES)
    assert f_pad == LANES
    table_steps = next(s for s in (4, 2, 1) if rows_up % s == 0)
    table_rows = rows_up // table_steps
    n_theta, n_phi = lax.axis_size("theta"), lax.axis_size("phi")
    polar_up = local_up(rows_up * n_theta, rows * n_theta, True, rows_up, rows, 3, (p_pad, t_pad))
    azimuth_up = local_up(columns_up * n_phi, columns * n_phi, False, columns_up, columns, 2, (q_pad, f_pad))
    high, low = split_constant(np.ascontiguousarray(azimuth_up.T))
    azimuth_three = jnp.asarray(np.concatenate([high, high, low], axis=0))
    high, low = split_constant(azimuth_up)
    azimuth_down = jnp.asarray(np.concatenate([high, low], axis=1))
    polar_down = jnp.asarray(np.ascontiguousarray(polar_up.T))

    def whole(array):
        return pl.BlockSpec(array.shape, lambda g: (0,) * array.ndim)

    def channel(shape):
        return pl.BlockSpec((2, 1) + shape, lambda g: (0, g, 0, 0, 0))

    smem = pl.BlockSpec(memory_space=pltpu.SMEM)
    constants = [combine, polar_cos, polar_sin, azimuth_three, polar_down, azimuth_down, phase]
    return pl.pallas_call(
        functools.partial(
            parent_kernel, (rows, columns, rows_up, columns_up, parents, entries, table_steps, table_rows)
        ),
        grid=(4,),
        in_specs=[
            smem,
            smem,
            channel((rows, columns, boxes)),
            channel((3, columns, boxes)),
            channel((3, columns, boxes)),
            channel((rows + 6, 8, boxes)),
            pl.BlockSpec(
                (2, table_rows, columns_up, translators), lambda g: (0, jnp.minimum(g, table_steps - 1), 0, 0)
            ),
        ]
        + [whole(c) for c in constants],
        out_specs=pl.BlockSpec((rows + 6, columns + 8, 8 * parents), lambda g: (0, 0, 0)),
        out_shape=jax.ShapeDtypeStruct((rows + 6, columns + 8, 8 * parents), F32),
        scratch_shapes=[
            pltpu.VMEM((2, 128 * t_pad, f_pad), F32),
            pltpu.VMEM((parents * p_pad, 3 * f_pad), BF16),
            pltpu.VMEM((q_pad // LANES, translators * 2 * p_pad, LANES), F32),
            pltpu.VMEM((2, 4, parents, p_pad, q_pad), F32),
            pltpu.VMEM((8 * parents * p_pad, q_pad), BF16),
            pltpu.VMEM((8 * parents * p_pad, q_pad), BF16),
            pltpu.VMEM((8 * parents * t_pad, f_pad), F32),
        ],
        compiler_params=pltpu.CompilerParams(vmem_limit_bytes=60 * MIB),
        cost_estimate=pl.CostEstimate(
            flops=20_000_000_000, bytes_accessed=child_out.size * 8, transcendentals=0
        ),
        name="parent_level",
    )(
        sources,
        kinds,
        child_out.reshape((2, 4) + child_out.shape[1:]),
        after.reshape((2, 4) + after.shape[1:]),
        before.reshape((2, 4) + before.shape[1:]),
        side.reshape((2, 4) + side.shape[1:]),
        table,
        *constants,
    )


def final_kernel(local_ref, lowered_ref, phase_ref, parent_ref, octant_ref, out_ref):
    rows, columns = local_ref.shape[1], local_ref.shape[2]

    def one_row(row, carry):
        phase = phase_ref[row]
        turned = jnp.concatenate([phase, jnp.zeros((LANES - 16, phase.shape[1]), F32)], axis=0).T
        for tile in range(columns // 8):
            at = slice(tile * 8, tile * 8 + 8)
            cosine = jnp.take_along_axis(turned[at], octant_ref[0], axis=1, mode="promise_in_bounds")
            sine = jnp.take_along_axis(turned[at], octant_ref[1], axis=1, mode="promise_in_bounds")
            lowered = lowered_ref[row, at]
            for c in range(4):
                x = jnp.take_along_axis(lowered, parent_ref[c], axis=1, mode="promise_in_bounds")
                y = jnp.take_along_axis(lowered, parent_ref[4 + c], axis=1, mode="promise_in_bounds")
                out_ref[c, row, at] = local_ref[c, row, at] + (x * cosine + y * sine)
                out_ref[4 + c, row, at] = local_ref[4 + c, row, at] + (y * cosine - x * sine)
        return carry

    lax.fori_loop(0, rows, one_row, 0)


def final_sum(local, lowered, phase, parent_lanes, octant_lanes):
    _, rows, columns, boxes = local.shape
    block = next(b for b in (4, 3, 2, 1) if rows % b == 0)
    patterns = pl.BlockSpec((8, block, columns, boxes), lambda i: (0, i, 0, 0))
    return pl.pallas_call(
        final_kernel,
        grid=(rows // block,),
        in_specs=[
            patterns,
            pl.BlockSpec((block, columns, lowered.shape[2]), lambda i: (i, 0, 0)),
            pl.BlockSpec((block,) + phase.shape[1:], lambda i: (i, 0, 0)),
            pl.BlockSpec(parent_lanes.shape, lambda i: (0, 0, 0)),
            pl.BlockSpec(octant_lanes.shape, lambda i: (0, 0, 0)),
        ],
        out_specs=patterns,
        out_shape=jax.ShapeDtypeStruct(local.shape, F32),
        input_output_aliases={0: 0},
        compiler_params=pltpu.CompilerParams(vmem_limit_bytes=40 * MIB),
        cost_estimate=pl.CostEstimate(flops=local.size * 4, bytes_accessed=local.size * 9, transcendentals=0),
        name="final_sum",
    )(local, lowered, phase, parent_lanes, octant_lanes)


def chain(count, periodic):
    pairs = [(i, i + 1) for i in range(count - 1)]
    return pairs + [(count - 1, 0)] if periodic else pairs


def send(block, axis, up):
    pairs = chain(lax.axis_size(axis), axis == "phi")
    return lax.ppermute(block, axis, pairs if up else [(b, a) for a, b in pairs])


def angles(count, all_count, axis, centered):
    index = jnp.arange(count, dtype=jnp.int32) + lax.axis_index(axis) * count
    if centered:
        return (index.astype(F32) + 0.5) * (math.pi / all_count)
    return index.astype(F32) * (2.0 * math.pi / all_count)


def padded(array, shape):
    return jnp.pad(array, [(0, n - m) for m, n in zip(array.shape, shape)])


def per_device(
    child_out,
    child_slot,
    sources_child,
    kinds_child,
    table_child,
    sources_parent,
    kinds_parent,
    table_parent,
):
    _, rows, columns, boxes = child_out.shape
    _, rows_up, columns_up, _ = table_parent.shape
    parents = boxes // 8
    n_theta, n_phi = lax.axis_size("theta"), lax.axis_size("phi")
    t_pad, p_pad = round_up(rows + 6, 16), round_up(rows_up, 16)
    q_pad = round_up(columns_up, LANES)

    after = send(child_out[:, :3], "theta", False)
    before = send(child_out[:, rows - 3 :], "theta", True)
    right = send(child_out[:, :, :3], "phi", False)
    left = send(child_out[:, :, columns - 2 :], "phi", True)
    poles = jnp.concatenate([after, before], axis=1)
    right_poles = send(poles[:, :, :3], "phi", False)
    left_poles = send(poles[:, :, columns - 2 :], "phi", True)
    side = jnp.concatenate(
        [
            jnp.concatenate([right, right_poles], axis=1),
            jnp.concatenate([left, left_poles], axis=1),
            jnp.zeros((8, rows + 6, 3, boxes), F32),
        ],
        axis=2,
    )

    parent_of = child_slot % parents
    octant_of = child_slot // parents
    east = 2 * (octant_of % 2) - 1
    north = 2 * (octant_of // 2 % 2) - 1
    upper = 2 * (octant_of // 4) - 1
    upper_weight = jnp.stack([jnp.ones_like(upper), upper])[:, None, None, None, :]
    alike = (jnp.arange(2)[:, None] == (east != north).astype(jnp.int32)[None, :])[None, :, None, None, :]
    east_weight = jnp.stack([jnp.ones_like(east), east])[None, None, :, None, :]
    same_parent = (jnp.arange(parents)[:, None] == parent_of[None, :])[None, None, None, :, :]
    combine = jnp.where(alike & same_parent, upper_weight * east_weight, 0).reshape(8 * parents, boxes).astype(BF16)
    combine = jnp.concatenate([combine, combine], axis=1)

    def spread(index):
        return jnp.broadcast_to(index.T[:, None, :], (index.shape[1], 8, index.shape[0])).astype(jnp.int32)

    component = jnp.arange(8, dtype=jnp.int32)
    parent_lanes = spread(parent_of[:, None] + component[None, :] * parents)
    octant_lanes = spread(octant_of[:, None] + jnp.array([[0, 8]], jnp.int32))

    polar = angles(rows_up, rows_up * n_theta, "theta", True)
    azimuth = angles(columns_up, columns_up * n_phi, "phi", False)
    upright = WAVE * jnp.cos(polar)
    polar_up = jnp.asarray(local_up(rows_up * n_theta, rows * n_theta, True, rows_up, rows, 3, (p_pad, t_pad)))
    polar_cos = polar_up * padded(jnp.cos(upright), (p_pad,))[:, None]
    polar_sin = polar_up * padded(jnp.sin(upright), (p_pad,))[:, None]
    flat = WAVE * jnp.sin(polar)[None, :, None]
    turned = jnp.stack([jnp.cos(azimuth) + jnp.sin(azimuth), jnp.cos(azimuth) - jnp.sin(azimuth)])[:, None, :]
    phase = flat * turned
    phase = jnp.stack([jnp.cos(phase), jnp.sin(phase)], axis=1).reshape(4, rows_up, columns_up)
    phase = padded(phase, (4, p_pad, q_pad))

    polar = angles(rows, rows * n_theta, "theta", True)[:, None, None]
    azimuth = angles(columns, columns * n_phi, "phi", False)[None, None, :]
    octant = jnp.arange(8, dtype=jnp.int32)[None, :, None]
    signs = [(2 * (octant // n % 2) - 1).astype(F32) for n in (1, 2, 4)]
    angle = WAVE * (
        jnp.sin(polar) * jnp.cos(azimuth) * signs[0]
        + jnp.sin(polar) * jnp.sin(azimuth) * signs[1]
        + jnp.cos(polar) * signs[2]
    )
    phase_child = padded(
        jnp.concatenate([jnp.cos(angle), jnp.sin(angle)], axis=1), (rows, 16, round_up(columns, LANES))
    )

    first = rows // 2
    sources, kinds = spread(sources_child), spread(kinds_child)
    local = child_translate(child_out, table_child, sources, kinds, 0, first, None)

    lowered = parent_level(
        child_out,
        after,
        before,
        side,
        table_parent,
        sources_parent,
        kinds_parent,
        combine,
        polar_cos,
        polar_sin,
        phase,
    )
    local, lowered = lax.optimization_barrier((local, lowered))

    low = send(lowered[rows : rows + 3], "theta", True)
    high = send(lowered[rows + 3 : rows + 6], "theta", False)
    here = lowered[:rows]
    here = here + jnp.pad(low, ((0, rows - 3), (0, 0), (0, 0))) + jnp.pad(high, ((rows - 3, 0), (0, 0), (0, 0)))
    low = send(here[:, columns : columns + 3], "phi", True)
    high = send(here[:, columns + 3 : columns + 5], "phi", False)
    here = here[:, :columns]
    here = here + jnp.pad(low, ((0, 0), (0, columns - 3), (0, 0))) + jnp.pad(high, ((0, 0), (columns - 2, 0), (0, 0)))

    local = child_translate(child_out, table_child, sources, kinds, first, rows - first, local)
    return final_sum(local, here, phase_child, parent_lanes, octant_lanes)


def solution(mesh):
    placed = (
        P(None, "theta", "phi", None),
        P(),
        P(),
        P(),
        P(None, "theta", "phi", None),
        P(),
        P(),
        P(None, "theta", "phi", None),
    )
    return jax.shard_map(
        per_device,
        mesh=mesh,
        in_specs=placed,
        out_specs=P(None, "theta", "phi", None),
        check_vma=False,
    )
```

time: 1450 us -> 315 us (0.22)
  other arithmetic: 735 us -> 5.32 us
  local copies, waits for them, and re-layouts: 588 us -> 25.6 us
  Pallas kernels: 0 us -> 244 us
  matrix products: 68.3 us -> 0 us
    gather x50 -> x0, local copies, waits for them, and re-layouts: 335 us -> none  [the longest x24 199 us: accumulate(): gathered = jnp.take(pattern, source_column, axis=3)]
    add x25 -> x5, other arithmetic: 279 us -> 1.68 us  [the longest x1 1.4 us: per_device(): here + jnp.pad(low, ((0, rows - 3), (0, 0), (0, 0)))]
    select_n x76 -> x1, other arithmetic: 254 us -> 0.01 us  [per_device(): parent_of = child_slot % parents]
    pallas_call x0 -> x4, Pallas kernels: none -> 244 us  [the longest x1 148 us: parent_level(): pl.pallas_call(functools.partial(parent_kernel, (rows, columns, rows_up,...]
    sub x25 -> x1, other arithmetic: 147 us -> 0.06 us  [per_device(): jnp.cos(azimuth) - jnp.sin(azimuth)]
    slice x9 -> x8, local copies, waits for them, and re-layouts: 93.4 us -> 5.24 us  [the longest x1 1.79 us: per_device(): before = send(child_out[:, rows - 3:], 'theta', True)]
    dot_general x5 -> x0, matrix products: 68.3 us -> none  [the longest x1 32 us: per_device(): jnp.einsum('qf,cpfb->cpqb', azimuth_up, padded, precision=exact_mode)]
    transpose x1 -> x0, local copies, waits for them, and re-layouts: 47.3 us -> none  [per_device(): jnp.einsum('qf,cpfb->cpqb', azimuth_up, padded, precision=exact_mode)]
  transfers between devices with their start and end apart: 8 -> 10, of which waited for: 2 -> 4; matrix products, arithmetic and copies ran while one was open for 47% -> 6% of each run, Pallas kernels for 0% -> 26%
where the time goes in v1:
time: 315 us; the launch traced here: 311 us
  Pallas kernels  244 us (77%)
  local copies, waits for them, and re-layouts  25.6 us (8%)
  starting transfers between devices  21.1 us (7%)
  waiting for transfers between devices  15 us (5%)
  other arithmetic  5.32 us (2%)
    pallas_call x1, Pallas kernels, parent_level(): pl.pallas_call(functools.partial(parent_kernel, (rows, columns, rows_up,...  148 us
    pallas_call x2, Pallas kernels, child_translate(): pl.pallas_call(functools.partial(local_kernel, entries), grid=(count // b...  81.8 us
    ppermute x10, starting transfers between devices, send(): lax.ppermute(block, axis, pairs if up else [(b, a) for a, b in pairs])  21.1 us
    ppermute x10, waiting for transfers between devices, send(): lax.ppermute(block, axis, pairs if up else [(b, a) for a, b in pairs])  15 us
    pallas_call x1, Pallas kernels, final_sum(): pl.pallas_call(final_kernel, grid=(rows // block,), in_specs=[patterns, p...  14 us
    unnamed x23, local copies, waits for them, and re-layouts  11.3 us
  transfers between devices with their start and end apart: 10, of which 4 were waited for; matrix products, arithmetic and copies ran while one was open for 6% of the time, Pallas kernels for 26%

profile of v1, /device:TPU:28, one launch (start us, length us, event | category | flops | bytes accessed | tf_op | source)
XLA Modules:
  0.0 311.1 jit_solution(2126621883556556689)
XLA Ops:
  0.0 1.8 fusion.30
  1.8 0.7 copy.25
  2.5 2.8 collective-permute-start
  5.3 1.7 copy.26
  7.0 2.0 collective-permute-start.1
  9.0 1.2 slice.38
  10.2 0.0 copy-start.5
  10.2 0.7 copy.27
  11.0 0.4 collective-permute-start.2
  11.4 1.2 slice.40
  12.6 0.7 copy.28
  13.3 3.4 %collective-permute-start.4 = (f32[8,24,2,128]{3,1,2,0:T(8,128)}, f32[8,24,2,128]{3,1,2,0:T(8,128)}, u32[]{:S(2)}, u32[]{:S(2)}) collective-permute-start(f32[8,24,2,128]{3,1,2,0:T(8,128)} %copy.28), channel_id=1, source_target_pairs={{0,1},{1,2},{2,3},{3,0},{4,5},{5,6},{6,7},{7,4},{8,9},{9,10},{10,1... | collective-permute-start | bytes 589832 | tf_op jit(solution)/shard_map/ppermute | solution.py:466
  16.7 0.0 copy-done.8
  16.8 0.1 fusion.21
  16.8 0.1 sine_multiply_fusion
  17.0 0.6 pad_maximum_fusion.1.combine_ref
  17.8 0.1 broadcast_add_fusion
  17.8 0.4 multiply_cosine_fusion
  18.3 0.1 fusion.28
  18.4 0.1 broadcast_multiply_fusion.2
  18.5 0.1 broadcast_multiply_fusion.4
  18.6 0.7 broadcast_multiply_fusion
  19.3 1.1 fusion.2
  20.4 7.2 %collective-permute-done = f32[8,3,96,128]{3,0,2,1:T(8,128)S(1)} collective-permute-done((f32[8,3,96,128]{3,0,2,1:T(8,128)S(1)}, f32[8,3,96,128]{3,0,2,1:T(8,128)S(1)}, u32[]{:S(2)}, u32[]{:S(2)}) %collective-permute-start) | collective-permute-done | bytes 1179680 | tf_op jit(solution)/shard_map/ppermute | solution.py:466
  27.5 0.1 constant_dynamic-update-slice_fusion.1
  27.6 0.0 copy-start.6
  27.6 0.0 copy-start.7
  27.6 0.0 copy-start.2
  27.7 5.1 %collective-permute-done.1 = f32[8,3,96,128]{3,0,2,1:T(8,128)} collective-permute-done((f32[8,3,96,128]{3,0,2,1:T(8,128)}, f32[8,3,96,128]{3,0,2,1:T(8,128)}, u32[]{:S(2)}, u32[]{:S(2)}) %collective-permute-start.1) | collective-permute-done | bytes 1179680 | tf_op jit(solution)/shard_map/ppermute | solution.py:466
  32.8 1.3 constant_dynamic-update-slice_fusion
  34.1 0.5 collective-permute-start.3
  34.6 3.4 %collective-permute-start.5 = (f32[8,6,2,128]{3,0,2,1:T(8,128)S(1)}, f32[8,6,2,128]{3,0,2,1:T(8,128)S(1)}, u32[]{:S(2)}, u32[]{:S(2)}) collective-permute-start(f32[8,6,2,128]{3,0,2,1:T(8,128)S(1)} %slice.49), channel_id=1, source_target_pairs={{0,1},{1,2},{2,3},{3,0},{4,5},{5,6},{6,7},{7,4},{8,9},{9,10},{10,1... | collective-permute-start | bytes 147464 | tf_op jit(solution)/shard_map/ppermute | solution.py:466
  38.0 0.7 pad.35.phase_ref
  38.7 0.1 pad.53.clone
  38.8 0.0 copy-start
  38.9 3.7 %copy-done = f32[8,24,96,128]{3,2,1,0:T(8,128)S(1)} copy-done((f32[8,24,96,128]{3,2,1,0:T(8,128)S(1)}, f32[8,24,96,128]{3,2,1,0:T(8,128)}, u32[]{:S(2)}) %copy-start) | copy-done | bytes 9437208
  42.5 40.9 %child_translate.2.rest_0_ = f32[8,24,96,128]{3,2,1,0:T(8,128)} custom-call(f32[8,24,96,128]{3,2,1,0:T(8,128)S(1)} %copy-done, f32[2,24,96,128]{3,2,1,0:T(8,128)S(1)} %copy-done.2, s32[12,8,128]{2,1,0:T(8,128)S(1)} %broadcast_in_dim.30.source_ref, s32[12,8,128]{2,1,0:T(8,128)S(1)} %broadcast_in_dim.31.kind_ref), custom_call_target="tpu_custom_call" | custom-call | flops 56623104 | bytes 10616832 | tf_op jit(solution)/shard_map/child_translate/pallas_call | solution.py:122
  83.4 0.0 collective-permute-done.4
  83.4 1.0 copy.23
  84.4 0.0 collective-permute-done.2
  84.4 1.0 copy.21
  85.4 1.2 copy.17
  86.7 2.5 copy.19
  89.2 0.0 collective-permute-done.5
  89.2 0.0 collective-permute-done.3
  89.2 0.2 maximum_maximum_fusion
  89.4 1.1 copy.24
  90.5 148.0 %parent_level.1 = f32[30,104,128]{2,1,0:T(8,128)} custom-call(s32[16,12]{1,0:T(8,128)} %source_ref.1, s32[16,12]{1,0:T(8,128)} %kind_ref.1, f32[2,4,24,96,128]{4,3,2,1,0:T(8,128)} %bitcast.12, f32[2,4,3,96,128]{4,3,2,1,0:T(8,128)} %bitcast.13, f32[2,4,3,96,128]{4,3,2,1,0:T(8,128)} %bitcast.14, f32[2,4,30,8,128]{4,3,2,1,0:T(8,128)} %bitcast.15, ...), custom_call_target="tpu_custom_call" | custom-call | flops 20000000000 | bytes 18874368 | tf_op jit(solution)/shard_map/parent_level/pallas_call | solution.py:370
  238.5 1.0 fusion.31
  239.5 1.9 collective-permute-start.6
  241.5 4.5 %collective-permute-start.7 = (f32[3,104,128]{2,1,0:T(8,128)S(1)}, f32[3,104,128]{2,1,0:T(8,128)S(1)}, u32[]{:S(2)}, u32[]{:S(2)}) collective-permute-start(f32[3,104,128]{2,1,0:T(8,128)S(1)} %get-tuple-element.14), channel_id=1, source_target_pairs={{4,0},{8,4},{12,8},{16,12},{20,16},{24,20},{28,24},{5,1},{9,5},{13... | collective-permute-start | bytes 479240 | tf_op jit(solution)/shard_map/ppermute | solution.py:466
  246.0 0.1 broadcast_add_fusion.1
  246.1 1.3 collective-permute-done.6
  247.4 1.4 collective-permute-done.7
  248.8 1.4 pad_add_fusion
  250.2 0.1 collective-permute-start.8
  250.3 2.0 collective-permute-start.9
  252.4 0.0 copy-start.1
  252.4 3.7 %copy-done.1 = f32[8,24,96,128]{3,2,1,0:T(8,128)S(1)} copy-done((f32[8,24,96,128]{3,2,1,0:T(8,128)S(1)}, f32[8,24,96,128]{3,2,1,0:T(8,128)}, u32[]{:S(2)}) %copy-start.1) | copy-done | bytes 9437208
  256.0 40.9 %child_translate.3.local_ref = f32[8,24,96,128]{3,2,1,0:T(8,128)} custom-call(f32[8,24,96,128]{3,2,1,0:T(8,128)S(1)} %copy-done.1, f32[2,24,96,128]{3,2,1,0:T(8,128)S(1)} %copy-done.2, s32[12,8,128]{2,1,0:T(8,128)S(1)} %broadcast_in_dim.30.source_ref, s32[12,8,128]{2,1,0:T(8,128)S(1)} %broadcast_in_dim.31.kind_ref, ...), custom_call_target="tpu_custom_call", output_to_operand_aliasing={{}: (4, {})} | custom-call | flops 56623104 | bytes 10616832 | tf_op jit(solution)/shard_map/child_translate/pallas_call | solution.py:122
  296.9 0.0 collective-permute-done.9
  296.9 0.0 collective-permute-done.8
  296.9 0.1 fusion.lowered_ref
  297.1 14.0 %final_sum.1 = f32[8,24,96,128]{3,2,1,0:T(8,128)} custom-call(f32[8,24,96,128]{3,2,1,0:T(8,128)} %child_translate.3.local_ref, f32[24,96,128]{2,1,0:T(8,128)S(1)} %fusion.lowered_ref, f32[24,16,128]{2,1,0:T(8,128)S(1)} %select_maximum_fusion.phase_ref, s32[8,8,128]{2,1,0:T(8,128)S(1)} %broadcast_in_dim.36.parent_ref, ...), custom_call_target="tpu_custom_call", output_to_operand_aliasing={{}: (0, {})} | custom-call | flops 9437184 | bytes 21233664 | tf_op jit(solution)/shard_map/final_sum/pallas_call | solution.py:440
  (39 shorter events, 0.3 us)
Async XLA Ops:
  2.5 25.1 %collective-permute-start = (f32[8,3,96,128]{3,0,2,1:T(8,128)S(1)}, f32[8,3,96,128]{3,0,2,1:T(8,128)S(1)}, u32[]{:S(2)}, u32[]{:S(2)}) collective-permute-start(f32[8,3,96,128]{3,0,2,1:T(8,128)S(1)} %copy.25), channel_id=1, source_target_pairs={{4,0},{8,4},{12,8},{16,12},{20,16},{24,20},{28,24},{5,1},{9,5},{13... | collective-permute-start | bytes 3538952 | tf_op jit(solution)/shard_map/ppermute | solution.py:466
  7.0 9.7 %copy-start.8 = (s32[128]{0:T(128)S(1)}, s32[128]{0:T(128)}, u32[]{:S(2)}) copy-start(s32[128]{0:T(128)} %param.14) | copy-start | bytes 1540
  7.0 25.8 %collective-permute-start.1 = (f32[8,3,96,128]{3,0,2,1:T(8,128)}, f32[8,3,96,128]{3,0,2,1:T(8,128)}, u32[]{:S(2)}, u32[]{:S(2)}) collective-permute-start(f32[8,3,96,128]{3,0,2,1:T(8,128)} %copy.26), channel_id=1, source_target_pairs={{0,4},{4,8},{8,12},{12,16},{16,20},{20,24},{24,28},{1,5},{5,9},{9,... | collective-permute-start | bytes 3538952 | tf_op jit(solution)/shard_map/ppermute | solution.py:466
  10.2 8.3 %copy-start.5 = (f32[48,32]{1,0:T(8,128)S(1)}, f32[48,32]{1,0:T(8,128)}, u32[]{:S(2)}) copy-start(f32[48,32]{1,0:T(8,128)} %constant.166.clone) | copy-start | bytes 18436
  11.0 73.4 %collective-permute-start.2 = (f32[8,24,3,128]{3,1,2,0:T(8,128)}, f32[8,24,3,128]{3,1,2,0:T(8,128)}, u32[]{:S(2)}, u32[]{:S(2)}) collective-permute-start(f32[8,24,3,128]{3,1,2,0:T(8,128)} %copy.27), channel_id=1, source_target_pairs={{1,0},{2,1},{3,2},{0,3},{5,4},{6,5},{7,6},{4,7},{9,8},{10,9},{11,1... | collective-permute-start | bytes 884744 | tf_op jit(solution)/shard_map/ppermute | solution.py:466
  13.3 70.1 %collective-permute-start.4 = (f32[8,24,2,128]{3,1,2,0:T(8,128)}, f32[8,24,2,128]{3,1,2,0:T(8,128)}, u32[]{:S(2)}, u32[]{:S(2)}) collective-permute-start(f32[8,24,2,128]{3,1,2,0:T(8,128)} %copy.28), channel_id=1, source_target_pairs={{0,1},{1,2},{2,3},{3,0},{4,5},{5,6},{6,7},{7,4},{8,9},{9,10},{10,1... | collective-permute-start | bytes 589832 | tf_op jit(solution)/shard_map/ppermute | solution.py:466
  27.6 11.2 %copy-start.6 = (s32[128,12]{0,1:T(8,128)S(1)}, s32[128,12]{0,1:T(8,128)}, u32[]{:S(2)}) copy-start(s32[128,12]{0,1:T(8,128)} %param.15) | copy-start | bytes 18436
  27.6 11.2 %copy-start.7 = (s32[128,12]{0,1:T(8,128)S(1)}, s32[128,12]{0,1:T(8,128)}, u32[]{:S(2)}) copy-start(s32[128,12]{0,1:T(8,128)} %param.16) | copy-start | bytes 18436
  27.6 11.2 %copy-start.2 = (f32[2,24,96,128]{3,2,1,0:T(8,128)S(1)}, f32[2,24,96,128]{3,2,1,0:T(8,128)}, u32[]{:S(2)}) copy-start(f32[2,24,96,128]{3,2,1,0:T(8,128)} %table_ref.5) | copy-start | bytes 7077892
  34.1 55.1 %collective-permute-start.3 = (f32[8,6,3,128]{3,0,2,1:T(8,128)S(1)}, f32[8,6,3,128]{3,0,2,1:T(8,128)S(1)}, u32[]{:S(2)}, u32[]{:S(2)}) collective-permute-start(f32[8,6,3,128]{3,0,2,1:T(8,128)S(1)} %slice.48), channel_id=1, source_target_pairs={{1,0},{2,1},{3,2},{0,3},{5,4},{6,5},{7,6},{4,7},{9,8},{10,9},{11,1... | collective-permute-start | bytes 221192 | tf_op jit(solution)/shard_map/ppermute | solution.py:466
  34.6 54.6 %collective-permute-start.5 = (f32[8,6,2,128]{3,0,2,1:T(8,128)S(1)}, f32[8,6,2,128]{3,0,2,1:T(8,128)S(1)}, u32[]{:S(2)}, u32[]{:S(2)}) collective-permute-start(f32[8,6,2,128]{3,0,2,1:T(8,128)S(1)} %slice.49), channel_id=1, source_target_pairs={{0,1},{1,2},{2,3},{3,0},{4,5},{5,6},{6,7},{7,4},{8,9},{9,10},{10,1... | collective-permute-start | bytes 147464 | tf_op jit(solution)/shard_map/ppermute | solution.py:466
  38.8 3.7 %copy-start = (f32[8,24,96,128]{3,2,1,0:T(8,128)S(1)}, f32[8,24,96,128]{3,2,1,0:T(8,128)}, u32[]{:S(2)}) copy-start(f32[8,24,96,128]{3,2,1,0:T(8,128)} %child_ref.3) | copy-start | bytes 28311556
  239.5 7.9 %collective-permute-start.6 = (f32[3,104,128]{2,1,0:T(8,128)S(1)}, f32[3,104,128]{2,1,0:T(8,128)S(1)}, u32[]{:S(2)}, u32[]{:S(2)}) collective-permute-start(f32[3,104,128]{2,1,0:T(8,128)S(1)} %get-tuple-element.13), channel_id=1, source_target_pairs={{0,4},{4,8},{8,12},{12,16},{16,20},{20,24},{24,28},{1,5},{5,9},{9,... | collective-permute-start | bytes 479240 | tf_op jit(solution)/shard_map/ppermute | solution.py:466
  241.5 7.3 %collective-permute-start.7 = (f32[3,104,128]{2,1,0:T(8,128)S(1)}, f32[3,104,128]{2,1,0:T(8,128)S(1)}, u32[]{:S(2)}, u32[]{:S(2)}) collective-permute-start(f32[3,104,128]{2,1,0:T(8,128)S(1)} %get-tuple-element.14), channel_id=1, source_target_pairs={{4,0},{8,4},{12,8},{16,12},{20,16},{24,20},{28,24},{5,1},{9,5},{13... | collective-permute-start | bytes 479240 | tf_op jit(solution)/shard_map/ppermute | solution.py:466
  246.1 6.2 %copy-start.3 = (f32[24,8,96]{2,1,0:T(8,128)S(1)}, f32[24,8,96]{2,1,0:T(8,128)}, u32[]{:S(2)}) copy-start(f32[24,8,96]{2,1,0:T(8,128)} %get-tuple-element.15) | copy-start | bytes 221188
  246.1 6.2 %copy-start.4 = (f32[24,8,96]{2,1,0:T(8,128)S(1)}, f32[24,8,96]{2,1,0:T(8,128)}, u32[]{:S(2)}) copy-start(f32[24,8,96]{2,1,0:T(8,128)} %get-tuple-element.16) | copy-start | bytes 221188
  250.2 46.7 %collective-permute-start.8 = (f32[24,3,128]{2,1,0:T(4,128)S(1)}, f32[24,3,128]{2,1,0:T(4,128)S(1)}, u32[]{:S(2)}, u32[]{:S(2)}) collective-permute-start(f32[24,3,128]{2,1,0:T(4,128)S(1)} %slice.51), channel_id=1, source_target_pairs={{0,1},{1,2},{2,3},{3,0},{4,5},{5,6},{6,7},{7,4},{8,9},{9,10},{10,1... | collective-permute-start | bytes 110600 | tf_op jit(solution)/shard_map/ppermute | solution.py:466
  250.3 46.6 %collective-permute-start.9 = (f32[24,2,128]{2,1,0:T(2,128)S(1)}, f32[24,2,128]{2,1,0:T(2,128)S(1)}, u32[]{:S(2)}, u32[]{:S(2)}) collective-permute-start(f32[24,2,128]{2,1,0:T(2,128)S(1)} %slice.52), channel_id=1, source_target_pairs={{1,0},{2,1},{3,2},{0,3},{5,4},{6,5},{7,6},{4,7},{9,8},{10,9},{11,1... | collective-permute-start | bytes 73736 | tf_op jit(solution)/shard_map/ppermute | solution.py:466
  252.4 3.7 %copy-start.1 = (f32[8,24,96,128]{3,2,1,0:T(8,128)S(1)}, f32[8,24,96,128]{3,2,1,0:T(8,128)}, u32[]{:S(2)}) copy-start(f32[8,24,96,128]{3,2,1,0:T(8,128)} %child_ref.3) | copy-start | bytes 28311556

commit v2 on v1

--- a/solution.py
+++ b/solution.py
@@ -69,68 +69,160 @@
     return lax.dot_general(a, b, (((1,), (1,)), ((), ())), preferred_element_type=F32)
 
 
-def local_kernel(entries, child_ref, table_ref, source_ref, kind_ref, *rest):
-    out_ref = rest[-1]
-    rows, columns = child_ref.shape[1], child_ref.shape[2]
-
-    def one_tile(step, carry):
-        row = step // (columns // 8)
-        at = pl.ds(pl.multiple_of(step % (columns // 8) * 8, 8), 8)
-        pattern = [child_ref[c, row, at, :] for c in range(8)]
-        table = [table_ref[c, row, at, :] for c in range(2)]
-        total = [None] * 8
+def segments(samples):
+    full, rest = divmod(samples, 8 * LANES)
+    found = [(0, full, 1, 8)] if full else []
+    if rest:
+        rows = -(-rest // LANES)
+        packed = 4 if rows <= 2 else 2 if rows <= 4 else 1
+        found.append((full, 1, packed, rows))
+    return found
+
+
+def lie_across(from_rows, to_tiles, plane, offsets, row):
+    turned = from_rows.T
+    for offset in offsets:
+        to_tiles[plane, pl.ds(offset + row, LANES, stride=8), :] = turned
+
+
+def translate_kernel(entries, packed, rows, source_ref, kind_ref, child_ref, table_ref, out_ref, pattern, table):
+    groups, per = 4 // packed, 8 // packed
+
+    for row in range(rows):
+        at = slice(row * LANES, (row + 1) * LANES)
+        for part in range(2):
+            lie_across(table_ref[part, at], table, part, [c * per for c in range(packed)], row)
+
+    def one_channel(c, carry):
+        for part in range(2):
+            for row in range(rows):
+                lie_across(
+                    child_ref[part, c, row * LANES : (row + 1) * LANES],
+                    pattern,
+                    part * groups + c // packed,
+                    [c % packed * per],
+                    row,
+                )
+        return carry
+
+    lax.fori_loop(0, 4, one_channel, 0)
+
+    def one_box(box, carry):
+        total = [None] * (2 * groups)
         for entry in range(entries):
-            source, kind = source_ref[entry], kind_ref[entry]
-            real, imag = (jnp.take_along_axis(t, kind, axis=1, mode="promise_in_bounds") for t in table)
-            for c in range(4):
-                x = jnp.take_along_axis(pattern[c], source, axis=1, mode="promise_in_bounds")
-                y = jnp.take_along_axis(pattern[4 + c], source, axis=1, mode="promise_in_bounds")
+            source = pl.ds(pl.multiple_of(source_ref[box * entries + entry], 8), 8)
+            kind = pl.ds(pl.multiple_of(kind_ref[box * entries + entry], 8), 8)
+            real, imag = table[0, kind, :], table[1, kind, :]
+            for g in range(groups):
+                x, y = pattern[g, source, :], pattern[groups + g, source, :]
                 re = x * real - y * imag
                 im = x * imag + y * real
-                total[c] = re if entry == 0 else total[c] + re
-                total[4 + c] = im if entry == 0 else total[4 + c] + im
-        for c in range(8):
-            out_ref[c, row, at, :] = total[c]
+                total[g] = re if entry == 0 else total[g] + re
+                total[groups + g] = im if entry == 0 else total[groups + g] + im
+        for g in range(2 * groups):
+            out_ref[0, g, pl.ds(pl.multiple_of(box * 8, 8), 8), :] = total[g]
         return carry
 
-    lax.fori_loop(0, rows * (columns // 8), one_tile, 0)
-
-
-def child_translate(child_out, table, sources, kinds, first, count, onto):
-    _, rows, columns, boxes = child_out.shape
-    entries = sources.shape[0]
-    block = next(b for b in (4, 3, 2, 1) if count % b == 0 and first % b == 0)
-    at = first // block
-
-    def place(i):
-        return (0, at + i, 0, 0)
-
-    whole = pl.BlockSpec((entries, 8, boxes), lambda i: (0, 0, 0))
+    lax.fori_loop(0, LANES, one_box, 0, unroll=2)
+
+
+def child_translate(child, table, sources, kinds, segment):
+    first, count, packed, rows = segment
+    entries = sources.shape[0] // LANES
+    planes = 8 // packed
+    smem = pl.BlockSpec(memory_space=pltpu.SMEM)
+    work = count * rows * LANES * LANES
+    return pl.pallas_call(
+        functools.partial(translate_kernel, entries, packed, rows),
+        grid=(count,),
+        in_specs=[
+            smem,
+            smem,
+            pl.BlockSpec((2, 4, 8 * LANES, LANES), lambda i: (0, 0, first + i, 0)),
+            pl.BlockSpec((2, 8 * LANES, LANES), lambda i: (0, first + i, 0)),
+        ],
+        out_specs=pl.BlockSpec((1, planes, 8 * LANES, LANES), lambda i: (i, 0, 0, 0)),
+        out_shape=jax.ShapeDtypeStruct((count, planes, 8 * LANES, LANES), F32),
+        scratch_shapes=[
+            pltpu.VMEM((planes, 8 * LANES, LANES), F32),
+            pltpu.VMEM((2, 8 * LANES, LANES), F32),
+        ],
+        compiler_params=pltpu.CompilerParams(vmem_limit_bytes=60 * MIB),
+        cost_estimate=pl.CostEstimate(flops=work * entries * 32, bytes_accessed=work * 72, transcendentals=0),
+        name="child_translate",
+    )(sources, kinds, child, table)
+
+
+def sum_kernel(packed, rows, parents, parent_ref, octant_ref, local_ref, lowered_ref, phase_ref, *rest):
+    out_ref, lowered, total = rest[-3:]
+    groups, per = 4 // packed, 8 // packed
+
+    for row in range(rows):
+        lie_across(lowered_ref[row * LANES : (row + 1) * LANES], lowered, 0, [0], row)
+
+    def one_box(box, carry):
+        parent = parent_ref[box]
+        octant = octant_ref[box]
+        cosine, sine = phase_ref[octant], phase_ref[8 + octant]
+        here = pl.ds(pl.multiple_of(box * 8, 8), 8)
+        for c in range(4):
+            x = lowered[0, pl.ds(pl.multiple_of(parent + c * parents * 8, 8), 8), :][:per]
+            y = lowered[0, pl.ds(pl.multiple_of(parent + (4 + c) * parents * 8, 8), 8), :][:per]
+            re = x * cosine[:per] + y * sine[:per]
+            im = y * cosine[:per] - x * sine[:per]
+            if packed == 1:
+                total[c, here, :] = local_ref[0, c, here, :] + re
+                total[4 + c, here, :] = local_ref[0, 4 + c, here, :] + im
+            else:
+                here = pl.ds(pl.multiple_of(box * 8, 8) + c % packed * per, per)
+                total[c // packed, here, :] = local_ref[0, c // packed, here, :] + re
+                total[groups + c // packed, here, :] = local_ref[0, groups + c // packed, here, :] + im
+        return carry
+
+    lax.fori_loop(0, LANES, one_box, 0, unroll=4)
+
+    def one_channel(c, carry):
+        for part in range(2):
+            for row in range(rows):
+                turned = total[part * groups + c // packed, pl.ds(c % packed * per + row, LANES, stride=8), :].T
+                out_ref[part, c, row * LANES : (row + 1) * LANES] = turned
+        return carry
+
+    lax.fori_loop(0, 4, one_channel, 0)
+
+
+def final_sum(shape, local, lowered, phase, parent, octant, segment, onto):
+    first, count, packed, rows = segment
+    planes = 8 // packed
+    smem = pl.BlockSpec(memory_space=pltpu.SMEM)
     in_specs = [
-        pl.BlockSpec((8, block, columns, boxes), place),
-        pl.BlockSpec((2, block, columns, boxes), place),
-        whole,
-        whole,
+        smem,
+        smem,
+        pl.BlockSpec((1, planes, 8 * LANES, LANES), lambda i: (i, 0, 0, 0)),
+        pl.BlockSpec((8 * LANES, LANES), lambda i: (first + i, 0)),
+        pl.BlockSpec((16, 8, LANES), lambda i: (0, first + i, 0)),
     ]
-    operands = [child_out, table, sources, kinds]
+    operands = [parent, octant, local, lowered, phase]
     aliases = {}
     if onto is not None:
         in_specs.append(pl.BlockSpec(memory_space=pl.ANY))
         operands.append(onto)
-        aliases = {4: 0}
-    samples = count * columns * boxes
+        aliases = {5: 0}
+    work = count * rows * LANES * LANES
     return pl.pallas_call(
-        functools.partial(local_kernel, entries),
-        grid=(count // block,),
+        functools.partial(sum_kernel, packed, rows, LANES // 8),
+        grid=(count,),
         in_specs=in_specs,
-        out_specs=pl.BlockSpec((8, block, columns, boxes), place),
-        out_shape=jax.ShapeDtypeStruct(child_out.shape, F32),
+        out_specs=pl.BlockSpec((2, 4, 8 * LANES, LANES), lambda i: (0, 0, first + i, 0)),
+        out_shape=jax.ShapeDtypeStruct(shape, F32),
         input_output_aliases=aliases,
-        compiler_params=pltpu.CompilerParams(vmem_limit_bytes=40 * MIB),
-        cost_estimate=pl.CostEstimate(
-            flops=samples * entries * 32, bytes_accessed=samples * 72, transcendentals=0
-        ),
-        name="child_translate",
+        scratch_shapes=[
+            pltpu.VMEM((1, 8 * LANES, LANES), F32),
+            pltpu.VMEM((planes, 8 * LANES, LANES), F32),
+        ],
+        compiler_params=pltpu.CompilerParams(vmem_limit_bytes=60 * MIB),
+        cost_estimate=pl.CostEstimate(flops=work * 32, bytes_accessed=work * 72, transcendentals=0),
+        name="final_sum",
     )(*operands)
 
 
@@ -178,7 +270,7 @@
 
     @pl.when(step < table_steps)
     def _():
-        def one_row(r, carry):
+        for r in range(table_rows):
             for part in range(2):
                 x = table_ref[part, r]
                 if q_pad > columns_up:
@@ -187,38 +279,33 @@
                     turned = x[lane : lane + LANES].T
                     at = pl.ds(part * p_pad + step * table_rows + r, 128, stride=2 * p_pad)
                     table_by_kind[lane // LANES, at, :] = turned
-            return carry
-
-        lax.fori_loop(0, table_rows, one_row, 0)
 
     combine = combine_ref[...]
 
-    def turn(main_ref, r, t):
+    def samples(part, main_ref, r, t):
+        x = jnp.concatenate(
+            [main_ref[part, 0, r], side_ref[part, 0, t], jnp.zeros((f_pad - columns - 8, LANES), F32)], axis=0
+        )
+        high, low = split(x)
+        return jnp.concatenate([high, low], axis=1)
+
+    def turn(pieces):
         for part in range(2):
-            x = jnp.concatenate(
-                [
-                    main_ref[part, 0, r],
-                    side_ref[part, 0, t],
-                    jnp.zeros((f_pad - columns - 8, LANES), F32),
-                ],
-                axis=0,
-            )
-            high, low = split(x)
-            wide[part, pl.ds(t, 128, stride=t_pad), :] = dot_transposed(
-                combine, jnp.concatenate([high, low], axis=1)
-            )
-
-    def main_row(r, carry):
-        turn(child_ref, r, r)
+            for i in range(0, len(pieces), 2):
+                both = jnp.concatenate([samples(part, *piece) for piece in pieces[i : i + 2]], axis=0)
+                turned = dot_transposed(combine, both)
+                for j, piece in enumerate(pieces[i : i + 2]):
+                    at = pl.ds(piece[2], 128, stride=t_pad)
+                    wide[part, at, :] = turned[:, j * f_pad : (j + 1) * f_pad]
+
+    per_turn = next(n for n in (4, 3, 2, 1) if rows % n == 0)
+
+    def main_rows(i, carry):
+        turn([(child_ref, per_turn * i + r, per_turn * i + r) for r in range(per_turn)])
         return carry
 
-    def edge_row(r, carry):
-        turn(next_ref, r, rows + r)
-        turn(previous_ref, r, rows + 3 + r)
-        return carry
-
-    lax.fori_loop(0, rows, main_row, 0)
-    lax.fori_loop(0, 3, edge_row, 0)
+    lax.fori_loop(0, rows // per_turn, main_rows, 0)
+    turn([(next_ref, r, rows + r) for r in range(3)] + [(previous_ref, r, rows + 3 + r) for r in range(3)])
 
     polar = []
     for sign in (-1.0, 1.0):
@@ -226,21 +313,20 @@
         high, low = split(both)
         polar.append(jnp.concatenate([high, high, low], axis=1))
     azimuth = azimuth_up_ref[...]
-    for part in range(2):
-        for kind in range(2):
-            for difference in range(2):
+    per = 4
+    for target in range(2):
+        for difference in range(2):
+            part = target if difference == 0 else 1 - target
+
+            def one_kind(kind, carry, part=part, difference=difference):
                 first = (kind * 2 + difference) * parents
-
-                def one_pair(pair, carry, part=part, first=first):
-                    at = first + 2 * pair
+                for pair in range(parents // 2):
                     stacked = []
                     for source, offset in ((part, 0), (1 - part, half)):
+                        at = (offset + first + 2 * pair) * t_pad
                         stacked.append(
                             jnp.concatenate(
-                                [
-                                    wide[source, pl.ds(pl.multiple_of((offset + at + i) * t_pad, 8), t_pad), :]
-                                    for i in range(2)
-                                ],
+                                [wide[source, pl.ds(pl.multiple_of(at + i * t_pad, 8), t_pad), :] for i in range(2)],
                                 axis=1,
                             )
                         )
@@ -249,33 +335,26 @@
                     high, low = split(result)
                     for i in range(2):
                         lanes = slice(i * f_pad, (i + 1) * f_pad)
-                        rows_done[pl.ds(pl.multiple_of((2 * pair + i) * p_pad, 16), p_pad), :] = jnp.concatenate(
+                        rows_done[kind * 2 + difference, pl.ds((2 * pair + i) * p_pad, p_pad), :] = jnp.concatenate(
                             [high[:, lanes], low[:, lanes], high[:, lanes]], axis=1
                         )
-                    return carry
-
-                lax.fori_loop(0, parents // 2, one_pair, 0)
-                target = part if difference == 0 else 1 - part
-                phase = phase_ref[2 * kind + difference]
-                if difference == 1 and part == 1:
-                    phase = -phase
-                fresh = kind == 0 and difference == part
-
-                starts = kind == 0 and part == 0
-
-                def one_group(group, carry, target=target, phase=phase, starts=starts):
-                    per = 4
-                    x = rows_done[pl.ds(pl.multiple_of(group * per * p_pad, 16), per * p_pad), :]
-                    y = dot(x, azimuth)
-                    for i in range(per):
-                        term = y[i * p_pad : (i + 1) * p_pad] * phase
-                        if starts:
-                            parent_out[target, step, group * per + i] = term
-                        else:
-                            parent_out[target, step, group * per + i] += term
-                    return carry
-
-                lax.fori_loop(0, parents // 4, one_group, 0)
+                return carry
+
+            lax.fori_loop(0, 2, one_kind, 0)
+
+        def one_group(group, carry, target=target):
+            at = pl.ds(pl.multiple_of(group * per * p_pad, 16), per * p_pad)
+            y = dot(jnp.concatenate([rows_done[k, at, :] for k in range(4)], axis=0), azimuth)
+            for i in range(per):
+                terms = [y[(k * per + i) * p_pad : (k * per + i + 1) * p_pad] * phase_ref[k] for k in range(4)]
+                if target == 0:
+                    value = (terms[0] - terms[1]) + (terms[2] - terms[3])
+                else:
+                    value = (terms[0] + terms[1]) + (terms[2] + terms[3])
+                parent_out[target, step, group * per + i] = value
+            return carry
+
+        lax.fori_loop(0, parents // per, one_group, 0)
 
     @pl.when(step == 3)
     def _():
@@ -312,7 +391,7 @@
         down_high = down[:, :f_pad]
         high, low = split(polar_down_ref[...])
         polar_back = jnp.concatenate([high, high, low], axis=1)
-        per = 4
+        per = parents
 
         def one_group(group, carry):
             at = pl.ds(pl.multiple_of(group * per * p_pad, 16), per * p_pad)
@@ -332,12 +411,15 @@
 
         lax.fori_loop(0, 8 * parents // per, one_group, 0)
 
-        def one_row(t, carry):
-            turned = lowered[pl.ds(t, 8 * parents, stride=t_pad), :].T
-            out_ref[t] = turned[: columns + 8]
+        per_turn = next(n for n in (6, 5, 3, 2, 1) if (rows + 6) % n == 0)
+
+        def some_rows(i, carry):
+            for r in range(per_turn):
+                turned = lowered[pl.ds(i * per_turn + r, 8 * parents, stride=t_pad), :].T
+                out_ref[i * per_turn + r] = turned[: columns + 8]
             return carry
 
-        lax.fori_loop(0, rows + 6, one_row, 0)
+        lax.fori_loop(0, (rows + 6) // per_turn, some_rows, 0)
 
 
 def parent_level(child_out, after, before, side, table, sources, kinds, combine, polar_cos, polar_sin, phase):
@@ -388,7 +470,7 @@
         out_shape=jax.ShapeDtypeStruct((rows + 6, columns + 8, 8 * parents), F32),
         scratch_shapes=[
             pltpu.VMEM((2, 128 * t_pad, f_pad), F32),
-            pltpu.VMEM((parents * p_pad, 3 * f_pad), BF16),
+            pltpu.VMEM((4, parents * p_pad, 3 * f_pad), BF16),
             pltpu.VMEM((q_pad // LANES, translators * 2 * p_pad, LANES), F32),
             pltpu.VMEM((2, 4, parents, p_pad, q_pad), F32),
             pltpu.VMEM((8 * parents * p_pad, q_pad), BF16),
@@ -412,50 +494,6 @@
     )
 
 
-def final_kernel(local_ref, lowered_ref, phase_ref, parent_ref, octant_ref, out_ref):
-    rows, columns = local_ref.shape[1], local_ref.shape[2]
-
-    def one_row(row, carry):
-        phase = phase_ref[row]
-        turned = jnp.concatenate([phase, jnp.zeros((LANES - 16, phase.shape[1]), F32)], axis=0).T
-        for tile in range(columns // 8):
-            at = slice(tile * 8, tile * 8 + 8)
-            cosine = jnp.take_along_axis(turned[at], octant_ref[0], axis=1, mode="promise_in_bounds")
-            sine = jnp.take_along_axis(turned[at], octant_ref[1], axis=1, mode="promise_in_bounds")
-            lowered = lowered_ref[row, at]
-            for c in range(4):
-                x = jnp.take_along_axis(lowered, parent_ref[c], axis=1, mode="promise_in_bounds")
-                y = jnp.take_along_axis(lowered, parent_ref[4 + c], axis=1, mode="promise_in_bounds")
-                out_ref[c, row, at] = local_ref[c, row, at] + (x * cosine + y * sine)
-                out_ref[4 + c, row, at] = local_ref[4 + c, row, at] + (y * cosine - x * sine)
-        return carry
-
-    lax.fori_loop(0, rows, one_row, 0)
-
-
-def final_sum(local, lowered, phase, parent_lanes, octant_lanes):
-    _, rows, columns, boxes = local.shape
-    block = next(b for b in (4, 3, 2, 1) if rows % b == 0)
-    patterns = pl.BlockSpec((8, block, columns, boxes), lambda i: (0, i, 0, 0))
-    return pl.pallas_call(
-        final_kernel,
-        grid=(rows // block,),
-        in_specs=[
-            patterns,
-            pl.BlockSpec((block, columns, lowered.shape[2]), lambda i: (i, 0, 0)),
-            pl.BlockSpec((block,) + phase.shape[1:], lambda i: (i, 0, 0)),
-            pl.BlockSpec(parent_lanes.shape, lambda i: (0, 0, 0)),
-            pl.BlockSpec(octant_lanes.shape, lambda i: (0, 0, 0)),
-        ],
-        out_specs=patterns,
-        out_shape=jax.ShapeDtypeStruct(local.shape, F32),
-        input_output_aliases={0: 0},
-        compiler_params=pltpu.CompilerParams(vmem_limit_bytes=40 * MIB),
-        cost_estimate=pl.CostEstimate(flops=local.size * 4, bytes_accessed=local.size * 9, transcendentals=0),
-        name="final_sum",
-    )(local, lowered, phase, parent_lanes, octant_lanes)
-
-
 def chain(count, periodic):
     pairs = [(i, i + 1) for i in range(count - 1)]
     return pairs + [(count - 1, 0)] if periodic else pairs
@@ -464,6 +502,17 @@
 def send(block, axis, up):
     pairs = chain(lax.axis_size(axis), axis == "phi")
     return lax.ppermute(block, axis, pairs if up else [(b, a) for a, b in pairs])
+
+
+def send_diagonal(block, polar_step, azimuth_step):
+    n_theta, n_phi = lax.axis_size("theta"), lax.axis_size("phi")
+    pairs = [
+        ((i + polar_step) * n_phi + (j + azimuth_step) % n_phi, i * n_phi + j)
+        for i in range(n_theta)
+        for j in range(n_phi)
+        if 0 <= i + polar_step < n_theta
+    ]
+    return lax.ppermute(block, ("theta", "phi"), pairs)
 
 
 def angles(count, all_count, axis, centered):
@@ -498,13 +547,17 @@
     before = send(child_out[:, rows - 3 :], "theta", True)
     right = send(child_out[:, :, :3], "phi", False)
     left = send(child_out[:, :, columns - 2 :], "phi", True)
-    poles = jnp.concatenate([after, before], axis=1)
-    right_poles = send(poles[:, :, :3], "phi", False)
-    left_poles = send(poles[:, :, columns - 2 :], "phi", True)
+    corners = [
+        [
+            send_diagonal(child_out[:, at_rows, at_columns], polar_step, azimuth_step)
+            for at_columns, azimuth_step in ((slice(0, 3), 1), (slice(columns - 2, columns), -1))
+        ]
+        for at_rows, polar_step in ((slice(0, 3), 1), (slice(rows - 3, rows), -1))
+    ]
     side = jnp.concatenate(
         [
-            jnp.concatenate([right, right_poles], axis=1),
-            jnp.concatenate([left, left_poles], axis=1),
+            jnp.concatenate([right, corners[0][0], corners[1][0]], axis=1),
+            jnp.concatenate([left, corners[0][1], corners[1][1]], axis=1),
             jnp.zeros((8, rows + 6, 3, boxes), F32),
         ],
         axis=2,
@@ -522,13 +575,6 @@
     combine = jnp.where(alike & same_parent, upper_weight * east_weight, 0).reshape(8 * parents, boxes).astype(BF16)
     combine = jnp.concatenate([combine, combine], axis=1)
 
-    def spread(index):
-        return jnp.broadcast_to(index.T[:, None, :], (index.shape[1], 8, index.shape[0])).astype(jnp.int32)
-
-    component = jnp.arange(8, dtype=jnp.int32)
-    parent_lanes = spread(parent_of[:, None] + component[None, :] * parents)
-    octant_lanes = spread(octant_of[:, None] + jnp.array([[0, 8]], jnp.int32))
-
     polar = angles(rows_up, rows_up * n_theta, "theta", True)
     azimuth = angles(columns_up, columns_up * n_phi, "phi", False)
     upright = WAVE * jnp.cos(polar)
@@ -541,22 +587,27 @@
     phase = jnp.stack([jnp.cos(phase), jnp.sin(phase)], axis=1).reshape(4, rows_up, columns_up)
     phase = padded(phase, (4, p_pad, q_pad))
 
-    polar = angles(rows, rows * n_theta, "theta", True)[:, None, None]
-    azimuth = angles(columns, columns * n_phi, "phi", False)[None, None, :]
-    octant = jnp.arange(8, dtype=jnp.int32)[None, :, None]
+    samples = rows * columns
+    sample_rows = -(-samples // LANES)
+    sample = jnp.arange(sample_rows * LANES, dtype=jnp.int32).reshape(1, sample_rows, LANES)
+    polar = (sample // columns + lax.axis_index("theta") * rows).astype(F32) + 0.5
+    polar = polar * (math.pi / (rows * n_theta))
+    azimuth = (sample % columns + lax.axis_index("phi") * columns).astype(F32)
+    azimuth = azimuth * (2.0 * math.pi / (columns * n_phi))
+    octant = jnp.arange(8, dtype=jnp.int32)[:, None, None]
     signs = [(2 * (octant // n % 2) - 1).astype(F32) for n in (1, 2, 4)]
     angle = WAVE * (
         jnp.sin(polar) * jnp.cos(azimuth) * signs[0]
         + jnp.sin(polar) * jnp.sin(azimuth) * signs[1]
         + jnp.cos(polar) * signs[2]
     )
-    phase_child = padded(
-        jnp.concatenate([jnp.cos(angle), jnp.sin(angle)], axis=1), (rows, 16, round_up(columns, LANES))
-    )
-
-    first = rows // 2
-    sources, kinds = spread(sources_child), spread(kinds_child)
-    local = child_translate(child_out, table_child, sources, kinds, 0, first, None)
+    phase_child = jnp.concatenate([jnp.cos(angle), jnp.sin(angle)], axis=0)
+
+    flat_child = child_out.reshape(2, 4, samples, boxes)
+    flat_table = table_child.reshape(2, samples, table_child.shape[3])
+    sources, kinds = sources_child.reshape(-1) * 8, kinds_child.reshape(-1) * 8
+    pieces = segments(samples)
+    local = [child_translate(flat_child, flat_table, sources, kinds, pieces[0])]
 
     lowered = parent_level(
         child_out,
@@ -571,19 +622,26 @@
         polar_sin,
         phase,
     )
-    local, lowered = lax.optimization_barrier((local, lowered))
+    lowered, flat_table = lax.optimization_barrier((lowered, flat_table))
 
     low = send(lowered[rows : rows + 3], "theta", True)
     high = send(lowered[rows + 3 : rows + 6], "theta", False)
+    local += [child_translate(flat_child, flat_table, sources, kinds, piece) for piece in pieces[1:]]
+    local, lowered = lax.optimization_barrier((local, lowered))
     here = lowered[:rows]
     here = here + jnp.pad(low, ((0, rows - 3), (0, 0), (0, 0))) + jnp.pad(high, ((rows - 3, 0), (0, 0), (0, 0)))
     low = send(here[:, columns : columns + 3], "phi", True)
     high = send(here[:, columns + 3 : columns + 5], "phi", False)
     here = here[:, :columns]
     here = here + jnp.pad(low, ((0, 0), (0, columns - 3), (0, 0))) + jnp.pad(high, ((0, 0), (columns - 2, 0), (0, 0)))
-
-    local = child_translate(child_out, table_child, sources, kinds, first, rows - first, local)
-    return final_sum(local, here, phase_child, parent_lanes, octant_lanes)
+    here = here.reshape(samples, boxes)
+
+    result = None
+    for piece, part in zip(pieces, local):
+        result = final_sum(
+            flat_child.shape, part, here, phase_child, parent_of * 8, octant_of, piece, result
+        )
+    return result.reshape(child_out.shape)
 
 
 def solution(mesh):

time: 315 us -> 194 us (0.62)
  Pallas kernels: 244 us -> 129 us
  waiting for transfers between devices: 15 us -> 2.07 us
  starting transfers between devices: 21.1 us -> 31 us
  local copies, waits for them, and re-layouts: 25.6 us -> 16.7 us
  other arithmetic: 5.32 us -> 10.5 us
    pallas_call x1, Pallas kernels: 148 us -> 72.2 us  [parent_level(): pl.pallas_call(functools.partial(parent_kernel, (rows, columns, rows_up,...]
    pallas_call x3 -> x4, Pallas kernels: 95.8 us -> 56.8 us  [the longest x2 43.4 us: child_translate(): pl.pallas_call(functools.partial(translate_kernel, entries, packed, rows)...]
    ppermute x10 -> x8, waiting for transfers between devices: 15 us -> 2.06 us  [send(): lax.ppermute(block, axis, pairs if up else [(b, a) for a, b in pairs])]
    ppermute x0 -> x4, starting transfers between devices: none -> 12.1 us  [send_diagonal(): return lax.ppermute(block, ('theta', 'phi'), pairs)]
    unnamed x23 -> x24, local copies, waits for them, and re-layouts: 11.3 us -> 3.25 us
    ppermute x4 -> x2, local copies, waits for them, and re-layouts: 5.8 us -> 0.12 us  [send(): lax.ppermute(block, axis, pairs if up else [(b, a) for a, b in pairs])]
    ppermute x10 -> x8, starting transfers between devices: 21.1 us -> 18.9 us  [send(): lax.ppermute(block, axis, pairs if up else [(b, a) for a, b in pairs])]
  transfers between devices with their start and end apart: 10 -> 12, of which waited for: 4 -> 2; matrix products, arithmetic and copies ran while one was open for 6% -> 12% of each run, Pallas kernels for 26% -> 23%
where the time goes in v2:
time: 194 us; the launch traced here: 190 us
  Pallas kernels  129 us (66%)
  starting transfers between devices  31 us (16%)
  local copies, waits for them, and re-layouts  16.7 us (9%)
  other arithmetic  10.5 us (5%)
  waiting for transfers between devices  2.07 us (1%)
    pallas_call x1, Pallas kernels, parent_level(): pl.pallas_call(functools.partial(parent_kernel, (rows, columns, rows_up,...  72.2 us
    pallas_call x2, Pallas kernels, child_translate(): pl.pallas_call(functools.partial(translate_kernel, entries, packed, rows)...  43.4 us
    ppermute x8, starting transfers between devices, send(): lax.ppermute(block, axis, pairs if up else [(b, a) for a, b in pairs])  18.9 us
    pallas_call x2, Pallas kernels, final_sum(): pl.pallas_call(functools.partial(sum_kernel, packed, rows, LANES // 8), g...  13.4 us
    ppermute x4, starting transfers between devices, send_diagonal(): return lax.ppermute(block, ('theta', 'phi'), pairs)  12.1 us
  transfers between devices with their start and end apart: 12, of which 2 were waited for; matrix products, arithmetic and copies ran while one was open for 12% of the time, Pallas kernels for 23%

profile of v2, /device:TPU:28, one launch (start us, length us, event | category | flops | bytes accessed | tf_op | source)
XLA Modules:
  0.0 189.8 jit_solution(8864122573936305093)
XLA Ops:
  0.0 1.6 fusion.41
  1.6 0.6 copy.32
  2.2 1.9 %collective-permute-start.7 = (f32[8,3,2,128]{3,0,2,1:T(8,128)}, f32[8,3,2,128]{3,0,2,1:T(8,128)}, u32[]{:S(2)}, u32[]{:S(2)}) collective-permute-start(f32[8,3,2,128]{3,0,2,1:T(8,128)} %copy.32), channel_id=1, source_target_pairs={{3,4},{0,5},{1,6},{2,7},{7,8},{4,9},{5,10},{6,11},{11,12},{8,13},{... | collective-permute-start | bytes 73736 | tf_op jit(solution)/shard_map/ppermute | solution.py:515
  4.1 1.2 slice.47
  5.3 1.3 collective-permute-start.5
  6.6 1.2 slice.44
  7.8 0.0 copy-start.8
  7.9 0.0 copy-start.3
  7.9 0.0 copy-start.4
  7.9 0.9 collective-permute-start.2
  8.7 1.8 fusion.42
  10.5 2.7 %collective-permute-start.1 = (f32[8,3,96,128]{3,2,1,0:T(8,128)S(1)}, f32[8,3,96,128]{3,2,1,0:T(8,128)}, u32[]{:S(2)}, u32[]{:S(2)}) collective-permute-start(f32[8,3,96,128]{3,2,1,0:T(8,128)S(1)} %get-tuple-element.23), channel_id=1, source_target_pairs={{0,4},{4,8},{8,12},{12,16},{16,20},{20,24},{24,28},{1,5},{5,9},{9,... | collective-permute-start | bytes 3538952 | tf_op jit(solution)/shard_map/ppermute | solution.py:504
  13.2 3.8 %collective-permute-start = (f32[8,3,96,128]{3,2,1,0:T(8,128)S(1)}, f32[8,3,96,128]{3,2,1,0:T(8,128)}, u32[]{:S(2)}, u32[]{:S(2)}) collective-permute-start(f32[8,3,96,128]{3,2,1,0:T(8,128)S(1)} %get-tuple-element.24), channel_id=1, source_target_pairs={{4,0},{8,4},{12,8},{16,12},{20,16},{24,20},{28,24},{5,1},{9,5},{13... | collective-permute-start | bytes 3538952 | tf_op jit(solution)/shard_map/ppermute | solution.py:504
  17.1 0.6 broadcast_multiply_fusion.5
  17.6 0.7 sine_multiply_fusion.1
  18.4 0.1 fusion.35
  18.4 0.6 broadcast_multiply_fusion.3
  19.0 0.6 broadcast_multiply_fusion.2
  19.7 0.7 pad_maximum_fusion.2.combine_ref
  20.3 0.4 multiply_cosine_fusion
  20.8 0.1 fusion.38
  20.9 0.7 pad.30
  21.6 1.4 broadcast_multiply_fusion
  23.0 1.0 fusion.40
  24.0 0.7 sine_multiply_fusion
  24.7 0.7 fusion.15
  25.4 0.5 fusion.25
  25.9 1.3 copy.31
  27.3 0.6 copy.28
  27.9 0.6 copy.29
  28.5 0.0 collective-permute-done.7
  28.5 4.4 %collective-permute-start.6 = (f32[8,3,2,128]{3,0,2,1:T(8,128)}, f32[8,3,2,128]{3,0,2,1:T(8,128)}, u32[]{:S(2)}, u32[]{:S(2)}) collective-permute-start(f32[8,3,2,128]{3,0,2,1:T(8,128)} %copy.31), channel_id=1, source_target_pairs={{7,0},{4,1},{5,2},{6,3},{11,4},{8,5},{9,6},{10,7},{15,8},{12,9},{1... | collective-permute-start | bytes 73736 | tf_op jit(solution)/shard_map/ppermute | solution.py:515
  32.9 1.9 %collective-permute-start.4 = (f32[8,3,3,128]{3,0,2,1:T(8,128)}, f32[8,3,3,128]{3,0,2,1:T(8,128)S(1)}, u32[]{:S(2)}, u32[]{:S(2)}) collective-permute-start(f32[8,3,3,128]{3,0,2,1:T(8,128)} %copy.29), channel_id=1, source_target_pairs={{1,4},{2,5},{3,6},{0,7},{5,8},{6,9},{7,10},{4,11},{9,12},{10,13},{... | collective-permute-start | bytes 110600 | tf_op jit(solution)/shard_map/ppermute | solution.py:515
  34.8 3.9 %collective-permute-start.3 = (f32[8,3,3,128]{3,0,2,1:T(8,128)}, f32[8,3,3,128]{3,0,2,1:T(8,128)S(1)}, u32[]{:S(2)}, u32[]{:S(2)}) collective-permute-start(f32[8,3,3,128]{3,0,2,1:T(8,128)} %copy.28), channel_id=1, source_target_pairs={{5,0},{6,1},{7,2},{4,3},{9,4},{10,5},{11,6},{8,7},{13,8},{14,9},{1... | collective-permute-start | bytes 110600 | tf_op jit(solution)/shard_map/ppermute | solution.py:515
  38.7 0.8 copy.17
  39.5 0.7 mul.249.kind_ref
  40.2 0.8 copy.16
  41.0 0.7 mul.247.source_ref
  41.7 0.7 pad.31.phase_ref
  42.4 0.1 pad.50.clone
  42.5 36.5 %child_translate.2.local_ref = f32[2,8,1024,128]{3,2,1,0:T(8,128)} custom-call(s32[1536]{0:T(1024)} %mul.247.source_ref, s32[1536]{0:T(1024)} %mul.249.kind_ref, f32[2,4,2304,128]{3,2,1,0:T(8,128)} %bitcast.14, f32[2,2304,128]{2,1,0:T(8,128)} %bitcast.19), custom_call_target="tpu_custom_call" | custom-call | flops 100663296 | bytes 18874368 | tf_op jit(solution)/shard_map/child_translate/pallas_call | solution.py:135
  79.0 0.1 copy.25
  79.1 0.1 copy.21
  79.2 0.0 collective-permute-done.6
  79.2 0.9 maximum_maximum_fusion
  80.2 1.1 copy.26
  81.3 0.0 collective-permute-done.1
  81.3 0.0 collective-permute-done
  81.3 72.2 %parent_level.1 = f32[30,104,128]{2,1,0:T(8,128)} custom-call(s32[16,12]{1,0:T(8,128)} %source_ref.1, s32[16,12]{1,0:T(8,128)} %kind_ref.1, f32[2,4,24,96,128]{4,3,2,1,0:T(8,128)} %bitcast.15, f32[2,4,3,96,128]{4,3,2,1,0:T(8,128)} %bitcast.3.next_ref, f32[2,4,3,96,128]{4,3,2,1,0:T(8,128)} %bitcast.4.previous_ref, f32[2,4,30,8,128]{4,3,2,1,0:T(8,128)} %bitcast.21, ...), custom_call_target="tpu_custom_call" | custom-call | flops 20000000000 | bytes 18874368 | tf_op jit(solution)/shard_map/parent_level/pallas_call | solution.py:452
  153.6 1.0 fusion.43
  154.6 1.9 %collective-permute-start.8 = (f32[3,104,128]{2,1,0:T(8,128)S(1)}, f32[3,104,128]{2,1,0:T(8,128)S(1)}, u32[]{:S(2)}, u32[]{:S(2)}) collective-permute-start(f32[3,104,128]{2,1,0:T(8,128)S(1)} %get-tuple-element.25), channel_id=1, source_target_pairs={{0,4},{4,8},{8,12},{12,16},{16,20},{20,24},{24,28},{1,5},{5,9},{9,... | collective-permute-start | bytes 479240 | tf_op jit(solution)/shard_map/ppermute | solution.py:504
  156.5 4.5 %collective-permute-start.9 = (f32[3,104,128]{2,1,0:T(8,128)S(1)}, f32[3,104,128]{2,1,0:T(8,128)S(1)}, u32[]{:S(2)}, u32[]{:S(2)}) collective-permute-start(f32[3,104,128]{2,1,0:T(8,128)S(1)} %get-tuple-element.26), channel_id=1, source_target_pairs={{4,0},{8,4},{12,8},{16,12},{20,16},{24,20},{28,24},{5,1},{9,5},{13... | collective-permute-start | bytes 479240 | tf_op jit(solution)/shard_map/ppermute | solution.py:504
  161.1 0.4 fusion.2
  161.6 0.0 copy-start
  161.6 6.9 %child_translate.3.local_ref = f32[1,2,1024,128]{3,2,1,0:T(8,128)} custom-call(s32[1536]{0:T(1024)} %mul.247.source_ref, s32[1536]{0:T(1024)} %mul.249.kind_ref, f32[2,4,2304,128]{3,2,1,0:T(8,128)} %bitcast.16, f32[2,2304,128]{2,1,0:T(8,128)} %bitcast.20), custom_call_target="tpu_custom_call" | custom-call | flops 12582912 | bytes 2359296 | tf_op jit(solution)/shard_map/child_translate/pallas_call | solution.py:135
  168.5 0.1 pad_add_fusion
  168.6 1.3 collective-permute-start.11
  169.9 2.6 %collective-permute-start.10 = (f32[24,3,128]{2,1,0:T(4,128)S(1)}, f32[24,3,128]{2,1,0:T(4,128)S(1)}, u32[]{:S(2)}, u32[]{:S(2)}) collective-permute-start(f32[24,3,128]{2,1,0:T(4,128)S(1)} %slice.57), channel_id=1, source_target_pairs={{0,1},{1,2},{2,3},{3,0},{4,5},{5,6},{6,7},{7,4},{8,9},{9,10},{10,1... | collective-permute-start | bytes 110600 | tf_op jit(solution)/shard_map/ppermute | solution.py:504
  172.5 0.7 pad_maximum_fusion.1.phase_ref
  173.2 1.1 collective-permute-done.11
  174.3 0.9 collective-permute-done.10
  175.2 1.2 fusion
  176.4 9.6 %final_sum.2.rest_0_ = f32[2,4,2304,128]{3,2,1,0:T(8,128)} custom-call(s32[128]{0:T(128)} %get-tuple-element.17.parent_ref, s32[128]{0:T(128)} %copy-done.5, f32[2,8,1024,128]{3,2,1,0:T(8,128)} %child_translate.2.local_ref, f32[2304,128]{1,0:T(8,128)} %bitcast.17, f32[16,18,128]{2,1,0:T(8,128)} %pad_maximum_fusion.1.phase_ref), custom_call_target="tpu_custom_call" | custom-call | flops 8388608 | bytes 18874368 | tf_op jit(solution)/shard_map/final_sum/pallas_call | solution.py:212
  186.0 3.8 %final_sum.3 = f32[2,4,2304,128]{3,2,1,0:T(8,128)} custom-call(s32[128]{0:T(128)} %get-tuple-element.17.parent_ref, s32[128]{0:T(128)} %copy-done.5, f32[1,2,1024,128]{3,2,1,0:T(8,128)} %child_translate.3.local_ref, f32[2304,128]{1,0:T(8,128)} %bitcast.18, f32[16,18,128]{2,1,0:T(8,128)} %pad_maximum_fusion.1.phase_ref, ...), custom_call_target="tpu_custom_call", output_to_operand_aliasing={{}: (5, {})} | custom-call | flops 1048576 | bytes 2359296 | tf_op jit(solution)/shard_map/final_sum/pallas_call | solution.py:212
  (38 shorter events, 0.2 us)
Async XLA Ops:
  2.2 26.3 %collective-permute-start.7 = (f32[8,3,2,128]{3,0,2,1:T(8,128)}, f32[8,3,2,128]{3,0,2,1:T(8,128)}, u32[]{:S(2)}, u32[]{:S(2)}) collective-permute-start(f32[8,3,2,128]{3,0,2,1:T(8,128)} %copy.32), channel_id=1, source_target_pairs={{3,4},{0,5},{1,6},{2,7},{7,8},{4,9},{5,10},{6,11},{11,12},{8,13},{... | collective-permute-start | bytes 73736 | tf_op jit(solution)/shard_map/ppermute | solution.py:515
  5.3 27.5 %collective-permute-start.5 = (f32[8,24,2,128]{3,1,2,0:T(8,128)S(1)}, f32[8,24,2,128]{3,1,2,0:T(8,128)S(1)}, u32[]{:S(2)}, u32[]{:S(2)}) collective-permute-start(f32[8,24,2,128]{3,1,2,0:T(8,128)S(1)} %copy.30), channel_id=1, source_target_pairs={{0,1},{1,2},{2,3},{3,0},{4,5},{5,6},{6,7},{7,4},{8,9},{9,10},{10,1... | collective-permute-start | bytes 589832 | tf_op jit(solution)/shard_map/ppermute | solution.py:504
  7.8 9.2 %copy-start.8 = (s32[128]{0:T(128)S(1)}, s32[128]{0:T(128)}, u32[]{:S(2)}) copy-start(s32[128]{0:T(128)} %param.13) | copy-start | bytes 1540
  7.9 10.6 %copy-start.3 = (s32[128,12]{0,1:T(8,128)S(1)}, s32[128,12]{0,1:T(8,128)}, u32[]{:S(2)}) copy-start(s32[128,12]{0,1:T(8,128)} %param.14) | copy-start | bytes 18436
  7.9 11.2 %copy-start.4 = (s32[128,12]{0,1:T(8,128)S(1)}, s32[128,12]{0,1:T(8,128)}, u32[]{:S(2)}) copy-start(s32[128,12]{0,1:T(8,128)} %param.15) | copy-start | bytes 18436
  7.9 26.9 %collective-permute-start.2 = (f32[8,24,3,128]{3,1,2,0:T(8,128)S(1)}, f32[8,24,3,128]{3,1,2,0:T(8,128)S(1)}, u32[]{:S(2)}, u32[]{:S(2)}) collective-permute-start(f32[8,24,3,128]{3,1,2,0:T(8,128)S(1)} %copy.27), channel_id=1, source_target_pairs={{1,0},{2,1},{3,2},{0,3},{5,4},{6,5},{7,6},{4,7},{9,8},{10,9},{11,1... | collective-permute-start | bytes 884744 | tf_op jit(solution)/shard_map/ppermute | solution.py:504
  10.5 70.8 %collective-permute-start.1 = (f32[8,3,96,128]{3,2,1,0:T(8,128)S(1)}, f32[8,3,96,128]{3,2,1,0:T(8,128)}, u32[]{:S(2)}, u32[]{:S(2)}) collective-permute-start(f32[8,3,96,128]{3,2,1,0:T(8,128)S(1)} %get-tuple-element.23), channel_id=1, source_target_pairs={{0,4},{4,8},{8,12},{12,16},{16,20},{20,24},{24,28},{1,5},{5,9},{9,... | collective-permute-start | bytes 3538952 | tf_op jit(solution)/shard_map/ppermute | solution.py:504
  13.2 68.1 %collective-permute-start = (f32[8,3,96,128]{3,2,1,0:T(8,128)S(1)}, f32[8,3,96,128]{3,2,1,0:T(8,128)}, u32[]{:S(2)}, u32[]{:S(2)}) collective-permute-start(f32[8,3,96,128]{3,2,1,0:T(8,128)S(1)} %get-tuple-element.24), channel_id=1, source_target_pairs={{4,0},{8,4},{12,8},{16,12},{20,16},{24,20},{28,24},{5,1},{9,5},{13... | collective-permute-start | bytes 3538952 | tf_op jit(solution)/shard_map/ppermute | solution.py:504
  17.0 62.0 %copy-start.5 = (s32[128]{0:T(128)}, s32[128]{0:T(128)S(1)}, u32[]{:S(2)}) copy-start(s32[128]{0:T(128)S(1)} %get-tuple-element.16.octant_ref) | copy-start | bytes 1540
  28.5 50.7 %collective-permute-start.6 = (f32[8,3,2,128]{3,0,2,1:T(8,128)}, f32[8,3,2,128]{3,0,2,1:T(8,128)}, u32[]{:S(2)}, u32[]{:S(2)}) collective-permute-start(f32[8,3,2,128]{3,0,2,1:T(8,128)} %copy.31), channel_id=1, source_target_pairs={{7,0},{4,1},{5,2},{6,3},{11,4},{8,5},{9,6},{10,7},{15,8},{12,9},{1... | collective-permute-start | bytes 73736 | tf_op jit(solution)/shard_map/ppermute | solution.py:515
  32.9 46.3 %collective-permute-start.4 = (f32[8,3,3,128]{3,0,2,1:T(8,128)}, f32[8,3,3,128]{3,0,2,1:T(8,128)S(1)}, u32[]{:S(2)}, u32[]{:S(2)}) collective-permute-start(f32[8,3,3,128]{3,0,2,1:T(8,128)} %copy.29), channel_id=1, source_target_pairs={{1,4},{2,5},{3,6},{0,7},{5,8},{6,9},{7,10},{4,11},{9,12},{10,13},{... | collective-permute-start | bytes 110600 | tf_op jit(solution)/shard_map/ppermute | solution.py:515
  34.8 44.4 %collective-permute-start.3 = (f32[8,3,3,128]{3,0,2,1:T(8,128)}, f32[8,3,3,128]{3,0,2,1:T(8,128)S(1)}, u32[]{:S(2)}, u32[]{:S(2)}) collective-permute-start(f32[8,3,3,128]{3,0,2,1:T(8,128)} %copy.28), channel_id=1, source_target_pairs={{5,0},{6,1},{7,2},{4,3},{9,4},{10,5},{11,6},{8,7},{13,8},{14,9},{1... | collective-permute-start | bytes 110600 | tf_op jit(solution)/shard_map/ppermute | solution.py:515
  81.3 79.8 %copy-start.1 = (f32[18,128]{1,0:T(8,128)S(1)}, f32[18,128]{1,0:T(8,128)}, u32[]{:S(2)}) copy-start(f32[18,128]{1,0:T(8,128)} %get-tuple-element.40) | copy-start | bytes 27652
  81.3 79.8 %copy-start.2 = (f32[18,128]{1,0:T(8,128)S(1)}, f32[18,128]{1,0:T(8,128)}, u32[]{:S(2)}) copy-start(f32[18,128]{1,0:T(8,128)} %fusion.15) | copy-start | bytes 27652
  81.3 79.8 %copy-start.6 = (f32[8]{0:T(128)S(1)}, f32[8]{0:T(128)}, u32[]{:S(2)}) copy-start(f32[8]{0:T(128)} %get-tuple-element.41) | copy-start | bytes 100
  81.3 79.8 %copy-start.7 = (f32[8]{0:T(128)S(1)}, f32[8]{0:T(128)}, u32[]{:S(2)}) copy-start(f32[8]{0:T(128)} %get-tuple-element.42) | copy-start | bytes 100
  154.6 13.9 %collective-permute-start.8 = (f32[3,104,128]{2,1,0:T(8,128)S(1)}, f32[3,104,128]{2,1,0:T(8,128)S(1)}, u32[]{:S(2)}, u32[]{:S(2)}) collective-permute-start(f32[3,104,128]{2,1,0:T(8,128)S(1)} %get-tuple-element.25), channel_id=1, source_target_pairs={{0,4},{4,8},{8,12},{12,16},{16,20},{20,24},{24,28},{1,5},{5,9},{9,... | collective-permute-start | bytes 479240 | tf_op jit(solution)/shard_map/ppermute | solution.py:504
  156.5 11.9 %collective-permute-start.9 = (f32[3,104,128]{2,1,0:T(8,128)S(1)}, f32[3,104,128]{2,1,0:T(8,128)S(1)}, u32[]{:S(2)}, u32[]{:S(2)}) collective-permute-start(f32[3,104,128]{2,1,0:T(8,128)S(1)} %get-tuple-element.26), channel_id=1, source_target_pairs={{4,0},{8,4},{12,8},{16,12},{20,16},{24,20},{28,24},{5,1},{9,5},{13... | collective-permute-start | bytes 479240 | tf_op jit(solution)/shard_map/ppermute | solution.py:504
  161.6 6.9 %copy-start = (f32[30,104,128]{2,1,0:T(8,128)S(1)}, f32[30,104,128]{2,1,0:T(8,128)}, u32[]{:S(2)}) copy-start(f32[30,104,128]{2,1,0:T(8,128)} %parent_level.1) | copy-start | bytes 4792324
  168.6 5.7 %collective-permute-start.11 = (f32[24,2,128]{2,1,0:T(2,128)S(1)}, f32[24,2,128]{2,1,0:T(2,128)S(1)}, u32[]{:S(2)}, u32[]{:S(2)}) collective-permute-start(f32[24,2,128]{2,1,0:T(2,128)S(1)} %slice.58), channel_id=1, source_target_pairs={{1,0},{2,1},{3,2},{0,3},{5,4},{6,5},{7,6},{4,7},{9,8},{10,9},{11,1... | collective-permute-start | bytes 73736 | tf_op jit(solution)/shard_map/ppermute | solution.py:504
  169.9 5.3 %collective-permute-start.10 = (f32[24,3,128]{2,1,0:T(4,128)S(1)}, f32[24,3,128]{2,1,0:T(4,128)S(1)}, u32[]{:S(2)}, u32[]{:S(2)}) collective-permute-start(f32[24,3,128]{2,1,0:T(4,128)S(1)} %slice.57), channel_id=1, source_target_pairs={{0,1},{1,2},{2,3},{3,0},{4,5},{5,6},{6,7},{7,4},{8,9},{9,10},{10,1... | collective-permute-start | bytes 110600 | tf_op jit(solution)/shard_map/ppermute | solution.py:504

commit v3 on v2

--- a/solution.py
+++ b/solution.py
@@ -71,7 +71,7 @@
 
 def segments(samples):
     full, rest = divmod(samples, 8 * LANES)
-    found = [(0, full, 1, 8)] if full else []
+    found = [(i, 1, 1, 8) for i in range(full)]
     if rest:
         rows = -(-rest // LANES)
         packed = 4 if rows <= 2 else 2 if rows <= 4 else 1
@@ -85,8 +85,9 @@
         to_tiles[plane, pl.ds(offset + row, LANES, stride=8), :] = turned
 
 
-def translate_kernel(entries, packed, rows, source_ref, kind_ref, child_ref, table_ref, out_ref, pattern, table):
+def translate_kernel(packed, rows, source_ref, kind_ref, child_ref, table_ref, out_ref, pattern, table):
     groups, per = 4 // packed, 8 // packed
+    entries = source_ref.shape[0]
 
     for row in range(rows):
         at = slice(row * LANES, (row + 1) * LANES)
@@ -110,8 +111,8 @@
     def one_box(box, carry):
         total = [None] * (2 * groups)
         for entry in range(entries):
-            source = pl.ds(pl.multiple_of(source_ref[box * entries + entry], 8), 8)
-            kind = pl.ds(pl.multiple_of(kind_ref[box * entries + entry], 8), 8)
+            source = pl.ds(pl.multiple_of(source_ref[entry, box] * 8, 8), 8)
+            kind = pl.ds(pl.multiple_of(kind_ref[entry, box] * 8, 8), 8)
             real, imag = table[0, kind, :], table[1, kind, :]
             for g in range(groups):
                 x, y = pattern[g, source, :], pattern[groups + g, source, :]
@@ -123,17 +124,17 @@
             out_ref[0, g, pl.ds(pl.multiple_of(box * 8, 8), 8), :] = total[g]
         return carry
 
-    lax.fori_loop(0, LANES, one_box, 0, unroll=2)
+    lax.fori_loop(0, LANES, one_box, 0, unroll=8)
 
 
 def child_translate(child, table, sources, kinds, segment):
     first, count, packed, rows = segment
-    entries = sources.shape[0] // LANES
+    entries = sources.shape[0]
     planes = 8 // packed
     smem = pl.BlockSpec(memory_space=pltpu.SMEM)
     work = count * rows * LANES * LANES
     return pl.pallas_call(
-        functools.partial(translate_kernel, entries, packed, rows),
+        functools.partial(translate_kernel, packed, rows),
         grid=(count,),
         in_specs=[
             smem,
@@ -153,7 +154,7 @@
     )(sources, kinds, child, table)
 
 
-def sum_kernel(packed, rows, parents, parent_ref, octant_ref, local_ref, lowered_ref, phase_ref, *rest):
+def sum_kernel(packed, rows, parents, slot_ref, local_ref, lowered_ref, phase_ref, *rest):
     out_ref, lowered, total = rest[-3:]
     groups, per = 4 // packed, 8 // packed
 
@@ -161,8 +162,9 @@
         lie_across(lowered_ref[row * LANES : (row + 1) * LANES], lowered, 0, [0], row)
 
     def one_box(box, carry):
-        parent = parent_ref[box]
-        octant = octant_ref[box]
+        slot = slot_ref[box]
+        parent = slot % parents * 8
+        octant = slot // parents
         cosine, sine = phase_ref[octant], phase_ref[8 + octant]
         here = pl.ds(pl.multiple_of(box * 8, 8), 8)
         for c in range(4):
@@ -191,23 +193,22 @@
     lax.fori_loop(0, 4, one_channel, 0)
 
 
-def final_sum(shape, local, lowered, phase, parent, octant, segment, onto):
+def final_sum(shape, local, lowered, phase, slots, segment, onto):
     first, count, packed, rows = segment
     planes = 8 // packed
     smem = pl.BlockSpec(memory_space=pltpu.SMEM)
     in_specs = [
         smem,
-        smem,
         pl.BlockSpec((1, planes, 8 * LANES, LANES), lambda i: (i, 0, 0, 0)),
         pl.BlockSpec((8 * LANES, LANES), lambda i: (first + i, 0)),
         pl.BlockSpec((16, 8, LANES), lambda i: (0, first + i, 0)),
     ]
-    operands = [parent, octant, local, lowered, phase]
+    operands = [slots, local, lowered, phase]
     aliases = {}
     if onto is not None:
         in_specs.append(pl.BlockSpec(memory_space=pl.ANY))
         operands.append(onto)
-        aliases = {5: 0}
+        aliases = {4: 0}
     work = count * rows * LANES * LANES
     return pl.pallas_call(
         functools.partial(sum_kernel, packed, rows, LANES // 8),
@@ -224,6 +225,101 @@
         cost_estimate=pl.CostEstimate(flops=work * 32, bytes_accessed=work * 72, transcendentals=0),
         name="final_sum",
     )(*operands)
+
+
+def cos_sin(x):
+    turns = jnp.floor(x * (2.0 / math.pi) + 0.5)
+    rest = ((x - turns * 1.5703125) - turns * 4.837512969970703e-4) - turns * 7.54978995489188e-8
+    square = rest * rest
+    sine = rest + rest * square * (
+        -1.6666654611e-1 + square * (8.3321608736e-3 + square * -1.9515295891e-4)
+    )
+    cosine = (1.0 - 0.5 * square) + square * square * (
+        4.166664568298827e-2 + square * (-1.388731625493765e-3 + square * 2.443315711809948e-5)
+    )
+    quarter = turns.astype(jnp.int32)
+    odd = (quarter & 1) == 1
+    first, second = jnp.where(odd, sine, cosine), jnp.where(odd, cosine, sine)
+    first = jnp.where(((quarter + 1) & 2) == 2, -first, first)
+    second = jnp.where((quarter & 2) == 2, -second, second)
+    return first, second
+
+
+def tables_kernel(sizes, slot_ref, polar_up_ref, combine_ref, cos_ref, sin_ref, phase_ref, child_ref):
+    rows, columns, rows_up, columns_up, parents, n_theta, n_phi = sizes
+    polar_index, azimuth_index = lax.axis_index("theta"), lax.axis_index("phi")
+
+    def iota(shape, axis):
+        return lax.broadcasted_iota(jnp.int32, shape, axis)
+
+    boxes = slot_ref.shape[1]
+    slot = jnp.broadcast_to(slot_ref[...], (parents, boxes))
+    same = (slot & (parents - 1)) == iota((parents, boxes), 0)
+    octant = slot >> (parents.bit_length() - 1)
+    east, north, upper = (2 * ((octant >> n) & 1) - 1 for n in range(3))
+    blocks = []
+    for z in range(2):
+        for kind in range(2):
+            for difference in range(2):
+                chosen = same & ((east == north) if kind == 0 else (east != north))
+                weight = (upper if z else 1) * (east if difference else 1)
+                weight = jnp.where(chosen, weight, 0).astype(F32)
+                blocks.append(weight)
+    combine = jnp.concatenate(blocks, axis=0).astype(BF16)
+    combine_ref[...] = jnp.concatenate([combine, combine], axis=1)
+
+    p_pad, t_pad = cos_ref.shape
+    q_pad = phase_ref.shape[2]
+    polar = (iota((p_pad, LANES), 0) + polar_index * rows_up).astype(F32) + 0.5
+    cosine, sine = cos_sin(polar * (math.pi / (rows_up * n_theta)))
+    up_cos, up_sin = cos_sin(WAVE * cosine)
+    cos_ref[...] = polar_up_ref[...] * up_cos[:, :t_pad]
+    sin_ref[...] = polar_up_ref[...] * up_sin[:, :t_pad]
+    azimuth = (iota((8, q_pad), 1) + azimuth_index * columns_up).astype(F32)
+    east, north = cos_sin(azimuth * (2.0 * math.pi / (columns_up * n_phi)))
+    flat = WAVE * sine
+    valid = iota((p_pad, LANES), 0) < rows_up
+    for lane in range(0, q_pad, LANES):
+        lanes = slice(lane, lane + LANES)
+        inside = valid & (iota((p_pad, LANES), 1) + lane < columns_up)
+        for kind in range(2):
+            turned = (east - north if kind else east + north)[:1, lanes]
+            found = cos_sin(flat * turned)
+            for i in range(2):
+                phase_ref[2 * kind + i, :, lanes] = jnp.where(inside, found[i], 0.0)
+
+    count = child_ref.shape[1]
+    sample = iota((count, LANES), 0) * LANES + iota((count, LANES), 1)
+    row = jnp.floor((sample.astype(F32) + 0.5) * (1.0 / columns))
+    polar = row + (polar_index * rows).astype(F32) + 0.5
+    azimuth = sample.astype(F32) - row * columns + (azimuth_index * columns).astype(F32)
+    up, flat = cos_sin(polar * (math.pi / (rows * n_theta)))
+    east, north = cos_sin(azimuth * (2.0 * math.pi / (columns * n_phi)))
+    for octant in range(4):
+        signs = [2 * ((octant >> n) & 1) - 1 for n in range(3)]
+        found = cos_sin(WAVE * (flat * east * signs[0] + flat * north * signs[1] + up * signs[2]))
+        child_ref[octant] = found[0]
+        child_ref[7 - octant] = found[0]
+        child_ref[8 + octant] = found[1]
+        child_ref[15 - octant] = -found[1]
+
+
+def tables(slots, sizes, p_pad, t_pad, q_pad, polar_up):
+    rows, columns, rows_up, columns_up, parents, n_theta, n_phi = sizes
+    boxes = slots.shape[0]
+    assert parents & (parents - 1) == 0
+    return pl.pallas_call(
+        functools.partial(tables_kernel, sizes),
+        out_shape=[
+            jax.ShapeDtypeStruct((8 * parents, 2 * boxes), BF16),
+            jax.ShapeDtypeStruct((p_pad, t_pad), F32),
+            jax.ShapeDtypeStruct((p_pad, t_pad), F32),
+            jax.ShapeDtypeStruct((4, p_pad, q_pad), F32),
+            jax.ShapeDtypeStruct((16, -(-rows * columns // LANES), LANES), F32),
+        ],
+        compiler_params=pltpu.CompilerParams(vmem_limit_bytes=60 * MIB),
+        name="tables",
+    )(slots.reshape(1, boxes), polar_up)
 
 
 def parent_kernel(
@@ -255,6 +351,7 @@
     t_pad, p_pad, f_pad, q_pad = wide.shape[1] // 128, parent_out.shape[3], wide.shape[2], parent_out.shape[4]
     step = pl.program_id(0)
     half = 4 * parents
+    table_first = jnp.minimum(step, table_steps - 1) * table_rows
 
     @pl.when(step == 0)
     def _():
@@ -268,18 +365,6 @@
                         (128, LANES), F32
                     )
 
-    @pl.when(step < table_steps)
-    def _():
-        for r in range(table_rows):
-            for part in range(2):
-                x = table_ref[part, r]
-                if q_pad > columns_up:
-                    x = jnp.concatenate([x, jnp.zeros((q_pad - columns_up, LANES), F32)], axis=0)
-                for lane in range(0, q_pad, LANES):
-                    turned = x[lane : lane + LANES].T
-                    at = pl.ds(part * p_pad + step * table_rows + r, 128, stride=2 * p_pad)
-                    table_by_kind[lane // LANES, at, :] = turned
-
     combine = combine_ref[...]
 
     def samples(part, main_ref, r, t):
@@ -300,11 +385,24 @@
 
     per_turn = next(n for n in (4, 3, 2, 1) if rows % n == 0)
 
+    turns = rows // per_turn
+    table_per_turn = -(-table_rows // turns)
+
     def main_rows(i, carry):
         turn([(child_ref, per_turn * i + r, per_turn * i + r) for r in range(per_turn)])
+        for j in range(table_per_turn):
+            r = jnp.minimum(i * table_per_turn + j, table_rows - 1)
+            for part in range(2):
+                x = table_ref[part, r]
+                if q_pad > columns_up:
+                    x = jnp.concatenate([x, jnp.zeros((q_pad - columns_up, LANES), F32)], axis=0)
+                for lane in range(0, q_pad, LANES):
+                    turned = x[lane : lane + LANES].T
+                    at = pl.ds(part * p_pad + table_first + r, 128, stride=2 * p_pad)
+                    table_by_kind[lane // LANES, at, :] = turned
         return carry
 
-    lax.fori_loop(0, rows // per_turn, main_rows, 0)
+    lax.fori_loop(0, turns, main_rows, 0)
     turn([(next_ref, r, rows + r) for r in range(3)] + [(previous_ref, r, rows + 3 + r) for r in range(3)])
 
     polar = []
@@ -504,28 +602,6 @@
     return lax.ppermute(block, axis, pairs if up else [(b, a) for a, b in pairs])
 
 
-def send_diagonal(block, polar_step, azimuth_step):
-    n_theta, n_phi = lax.axis_size("theta"), lax.axis_size("phi")
-    pairs = [
-        ((i + polar_step) * n_phi + (j + azimuth_step) % n_phi, i * n_phi + j)
-        for i in range(n_theta)
-        for j in range(n_phi)
-        if 0 <= i + polar_step < n_theta
-    ]
-    return lax.ppermute(block, ("theta", "phi"), pairs)
-
-
-def angles(count, all_count, axis, centered):
-    index = jnp.arange(count, dtype=jnp.int32) + lax.axis_index(axis) * count
-    if centered:
-        return (index.astype(F32) + 0.5) * (math.pi / all_count)
-    return index.astype(F32) * (2.0 * math.pi / all_count)
-
-
-def padded(array, shape):
-    return jnp.pad(array, [(0, n - m) for m, n in zip(array.shape, shape)])
-
-
 def per_device(
     child_out,
     child_slot,
@@ -542,72 +618,40 @@
     n_theta, n_phi = lax.axis_size("theta"), lax.axis_size("phi")
     t_pad, p_pad = round_up(rows + 6, 16), round_up(rows_up, 16)
     q_pad = round_up(columns_up, LANES)
+    barrier = lax.optimization_barrier
+
+    polar_up = local_up(rows_up * n_theta, rows * n_theta, True, rows_up, rows, 3, (p_pad, t_pad))
+    sizes = (rows, columns, rows_up, columns_up, parents, n_theta, n_phi)
+    combine, polar_cos, polar_sin, phase, phase_child = tables(
+        child_slot, sizes, p_pad, t_pad, q_pad, jnp.asarray(polar_up)
+    )
+
+    samples = rows * columns
+    flat_child = child_out.reshape(2, 4, samples, boxes)
+    flat_table = table_child.reshape(2, samples, table_child.shape[3])
+    pieces = segments(samples)
+    local = []
+
+    def translate_next(child):
+        if len(local) < len(pieces):
+            local.append(child_translate(child, flat_table, sources_child.T, kinds_child.T, pieces[len(local)]))
 
     after = send(child_out[:, :3], "theta", False)
     before = send(child_out[:, rows - 3 :], "theta", True)
-    right = send(child_out[:, :, :3], "phi", False)
-    left = send(child_out[:, :, columns - 2 :], "phi", True)
-    corners = [
-        [
-            send_diagonal(child_out[:, at_rows, at_columns], polar_step, azimuth_step)
-            for at_columns, azimuth_step in ((slice(0, 3), 1), (slice(columns - 2, columns), -1))
-        ]
-        for at_rows, polar_step in ((slice(0, 3), 1), (slice(rows - 3, rows), -1))
-    ]
-    side = jnp.concatenate(
-        [
-            jnp.concatenate([right, corners[0][0], corners[1][0]], axis=1),
-            jnp.concatenate([left, corners[0][1], corners[1][1]], axis=1),
-            jnp.zeros((8, rows + 6, 3, boxes), F32),
-        ],
-        axis=2,
+    translate_next(flat_child)
+    after, before, local = barrier((after, before, local))
+
+    low, high = (
+        jnp.concatenate([edge[:, :, at] for edge in (child_out, after, before)], axis=1)
+        for at in (slice(0, 3), slice(columns - 2, columns))
     )
-
-    parent_of = child_slot % parents
-    octant_of = child_slot // parents
-    east = 2 * (octant_of % 2) - 1
-    north = 2 * (octant_of // 2 % 2) - 1
-    upper = 2 * (octant_of // 4) - 1
-    upper_weight = jnp.stack([jnp.ones_like(upper), upper])[:, None, None, None, :]
-    alike = (jnp.arange(2)[:, None] == (east != north).astype(jnp.int32)[None, :])[None, :, None, None, :]
-    east_weight = jnp.stack([jnp.ones_like(east), east])[None, None, :, None, :]
-    same_parent = (jnp.arange(parents)[:, None] == parent_of[None, :])[None, None, None, :, :]
-    combine = jnp.where(alike & same_parent, upper_weight * east_weight, 0).reshape(8 * parents, boxes).astype(BF16)
-    combine = jnp.concatenate([combine, combine], axis=1)
-
-    polar = angles(rows_up, rows_up * n_theta, "theta", True)
-    azimuth = angles(columns_up, columns_up * n_phi, "phi", False)
-    upright = WAVE * jnp.cos(polar)
-    polar_up = jnp.asarray(local_up(rows_up * n_theta, rows * n_theta, True, rows_up, rows, 3, (p_pad, t_pad)))
-    polar_cos = polar_up * padded(jnp.cos(upright), (p_pad,))[:, None]
-    polar_sin = polar_up * padded(jnp.sin(upright), (p_pad,))[:, None]
-    flat = WAVE * jnp.sin(polar)[None, :, None]
-    turned = jnp.stack([jnp.cos(azimuth) + jnp.sin(azimuth), jnp.cos(azimuth) - jnp.sin(azimuth)])[:, None, :]
-    phase = flat * turned
-    phase = jnp.stack([jnp.cos(phase), jnp.sin(phase)], axis=1).reshape(4, rows_up, columns_up)
-    phase = padded(phase, (4, p_pad, q_pad))
-
-    samples = rows * columns
-    sample_rows = -(-samples // LANES)
-    sample = jnp.arange(sample_rows * LANES, dtype=jnp.int32).reshape(1, sample_rows, LANES)
-    polar = (sample // columns + lax.axis_index("theta") * rows).astype(F32) + 0.5
-    polar = polar * (math.pi / (rows * n_theta))
-    azimuth = (sample % columns + lax.axis_index("phi") * columns).astype(F32)
-    azimuth = azimuth * (2.0 * math.pi / (columns * n_phi))
-    octant = jnp.arange(8, dtype=jnp.int32)[:, None, None]
-    signs = [(2 * (octant // n % 2) - 1).astype(F32) for n in (1, 2, 4)]
-    angle = WAVE * (
-        jnp.sin(polar) * jnp.cos(azimuth) * signs[0]
-        + jnp.sin(polar) * jnp.sin(azimuth) * signs[1]
-        + jnp.cos(polar) * signs[2]
-    )
-    phase_child = jnp.concatenate([jnp.cos(angle), jnp.sin(angle)], axis=0)
-
-    flat_child = child_out.reshape(2, 4, samples, boxes)
-    flat_table = table_child.reshape(2, samples, table_child.shape[3])
-    sources, kinds = sources_child.reshape(-1) * 8, kinds_child.reshape(-1) * 8
-    pieces = segments(samples)
-    local = [child_translate(flat_child, flat_table, sources, kinds, pieces[0])]
+    low, high, later_child = barrier((low, high, flat_child))
+    right = send(low, "phi", False)
+    left = send(high, "phi", True)
+    if len(pieces) > 2:
+        translate_next(later_child)
+    right, left, local = barrier((right, left, local))
+    side = jnp.concatenate([right, left, jnp.zeros((8, rows + 6, 3, boxes), F32)], axis=2)
 
     lowered = parent_level(
         child_out,
@@ -622,12 +666,13 @@
         polar_sin,
         phase,
     )
-    lowered, flat_table = lax.optimization_barrier((lowered, flat_table))
+    lowered, later_child = barrier((lowered, flat_child))
 
     low = send(lowered[rows : rows + 3], "theta", True)
     high = send(lowered[rows + 3 : rows + 6], "theta", False)
-    local += [child_translate(flat_child, flat_table, sources, kinds, piece) for piece in pieces[1:]]
-    local, lowered = lax.optimization_barrier((local, lowered))
+    while len(local) < len(pieces):
+        translate_next(later_child)
+    local, lowered = barrier((local, lowered))
     here = lowered[:rows]
     here = here + jnp.pad(low, ((0, rows - 3), (0, 0), (0, 0))) + jnp.pad(high, ((rows - 3, 0), (0, 0), (0, 0)))
     low = send(here[:, columns : columns + 3], "phi", True)
@@ -638,9 +683,7 @@
 
     result = None
     for piece, part in zip(pieces, local):
-        result = final_sum(
-            flat_child.shape, part, here, phase_child, parent_of * 8, octant_of, piece, result
-        )
+        result = final_sum(flat_child.shape, part, here, phase_child, child_slot, piece, result)
     return result.reshape(child_out.shape)
 
 

time: 194 us -> 173 us (0.89); the launches traced: 190 us -> 172 us
  starting transfers between devices: 31 us -> 17.3 us
  Pallas kernels: 129 us -> 138 us
  other arithmetic: 10.5 us -> 1.58 us
  local copies, waits for them, and re-layouts: 16.7 us -> 11.7 us
    ppermute x4 -> x0, starting transfers between devices: 12.1 us -> none  [send_diagonal(): return lax.ppermute(block, ('theta', 'phi'), pairs)]
    pallas_call x2 -> x4, Pallas kernels: 43.4 us -> 50.2 us  [the longest x3 48.4 us: child_translate(): pl.pallas_call(functools.partial(translate_kernel, packed, rows), grid=(c...]
    pallas_call x2 -> x3, Pallas kernels: 13.4 us -> 18.4 us  [final_sum(): pl.pallas_call(functools.partial(sum_kernel, packed, rows, LANES // 8), g...]
    mul x7 -> x0, other arithmetic: 4.62 us -> none  [the longest x1 1.44 us: per_device(): polar_sin = polar_up * padded(jnp.sin(upright), (p_pad,))[:, None]]
    mul x4 -> x0, local copies, waits for them, and re-layouts: 3 us -> none  [the longest x2 1.5 us: per_device(): sources_child.reshape(-1) * 8]
    pallas_call x1, Pallas kernels: 72.2 us -> 69.4 us  [parent_level(): pl.pallas_call(functools.partial(parent_kernel, (rows, columns, rows_up,...]
    optimization_barrier x0 -> x2, local copies, waits for them, and re-layouts: none -> 2.56 us  [per_device(): after, before, local = barrier((after, before, local))]
    slice x4 -> x6, local copies, waits for them, and re-layouts: 4.94 us -> 2.42 us  [per_device(): edge[:, :, at]]
  transfers between devices with their start and end apart: 12 -> 8, of which waited for: 2 -> 2; matrix products, arithmetic and copies ran while one was open for 12% -> 4% of each run, Pallas kernels for 23% -> 29%
where the time goes in v3:
time: 173 us; the launch traced here: 172 us
  Pallas kernels  138 us (80%)
  starting transfers between devices  17.3 us (10%)
  local copies, waits for them, and re-layouts  11.7 us (7%)
  waiting for transfers between devices  3.76 us (2%)
    pallas_call x1, Pallas kernels, parent_level(): pl.pallas_call(functools.partial(parent_kernel, (rows, columns, rows_up,...  69.4 us
    pallas_call x3, Pallas kernels, child_translate(): pl.pallas_call(functools.partial(translate_kernel, packed, rows), grid=(c...  48.4 us
    pallas_call x3, Pallas kernels, final_sum(): pl.pallas_call(functools.partial(sum_kernel, packed, rows, LANES // 8), g...  18.4 us
    ppermute x8, starting transfers between devices, send(): lax.ppermute(block, axis, pairs if up else [(b, a) for a, b in pairs])  17.3 us
    ppermute x8, waiting for transfers between devices, send(): lax.ppermute(block, axis, pairs if up else [(b, a) for a, b in pairs])  3.76 us
  transfers between devices with their start and end apart: 8, of which 2 were waited for; matrix products, arithmetic and copies ran while one was open for 4% of the time, Pallas kernels for 29%

profile of v3, /device:TPU:28, one launch (start us, length us, event | category | flops | bytes accessed | tf_op | source)
XLA Modules:
  0.0 172.5 jit_solution(11322937872457225821)
XLA Ops:
  0.0 1.8 %fusion.1 = (f32[8,3,96,128]{3,2,1,0:T(8,128)S(1)}, f32[8,3,96,128]{3,2,1,0:T(8,128)S(1)}) fusion(f32[8,24,96,128]{3,2,1,0:T(8,128)} %param.12), kind=kLoop, calls=%fused_computation.6 | loop fusion | bytes 4718592 | tf_op jit(solution)/shard_map/slice | solution.py:640
  1.8 0.7 copy.23
  2.5 2.8 %collective-permute-start = (f32[8,3,96,128]{3,0,2,1:T(8,128)S(1)}, f32[8,3,96,128]{3,0,2,1:T(8,128)S(1)}, u32[]{:S(2)}, u32[]{:S(2)}) collective-permute-start(f32[8,3,96,128]{3,0,2,1:T(8,128)S(1)} %copy.23), channel_id=1, source_target_pairs={{4,0},{8,4},{12,8},{16,12},{20,16},{24,20},{28,24},{5,1},{9,5},{13... | collective-permute-start | bytes 3538952 | tf_op jit(solution)/shard_map/ppermute | solution.py:602
  5.3 1.7 copy.24
  7.0 1.9 %collective-permute-start.1 = (f32[8,3,96,128]{3,0,2,1:T(8,128)}, f32[8,3,96,128]{3,0,2,1:T(8,128)S(1)}, u32[]{:S(2)}, u32[]{:S(2)}) collective-permute-start(f32[8,3,96,128]{3,0,2,1:T(8,128)} %copy.24), channel_id=1, source_target_pairs={{0,4},{4,8},{8,12},{12,16},{16,20},{20,24},{24,28},{1,5},{5,9},{9,... | collective-permute-start | bytes 3538952 | tf_op jit(solution)/shard_map/ppermute | solution.py:602
  8.9 1.2 slice.47
  10.1 1.2 slice.42
  11.3 0.1 copy.25
  11.4 0.2 copy.22
  11.6 20.9 %child_translate.3.local_ref = f32[1,8,1024,128]{3,2,1,0:T(8,128)} custom-call(s32[12,128]{1,0:T(8,128)} %bitcast.24, s32[12,128]{1,0:T(8,128)} %bitcast.27, f32[2,4,2304,128]{3,2,1,0:T(8,128)} %bitcast.11, f32[2,2304,128]{2,1,0:T(8,128)} %bitcast.15), custom_call_target="tpu_custom_call" | custom-call | flops 50331648 | bytes 9437184 | tf_op jit(solution)/shard_map/child_translate/pallas_call | solution.py:136
  32.5 0.0 collective-permute-done
  32.5 0.1 collective-permute-done.1
  32.7 0.5 collective-permute-start.2
  33.2 3.4 %collective-permute-start.3 = (f32[8,30,2,128]{3,0,2,1:T(8,128)S(1)}, f32[8,30,2,128]{3,0,2,1:T(8,128)S(1)}, u32[]{:S(2)}, u32[]{:S(2)}) collective-permute-start(f32[8,30,2,128]{3,0,2,1:T(8,128)S(1)} %pad_maximum_fusion.1), channel_id=1, source_target_pairs={{0,1},{1,2},{2,3},{3,0},{4,5},{5,6},{6,7},{7,4},{8,9},{9,10},{10,1... | collective-permute-start | bytes 737288 | tf_op jit(solution)/shard_map/ppermute | solution.py:602
  36.6 0.1 pad.22.clone
  36.7 1.8 %tables.1 = (bf16[128,256]{1,0:T(8,128)(2,1)}, f32[48,32]{1,0:T(8,128)}, f32[48,32]{1,0:T(8,128)}, f32[4,48,256]{2,1,0:T(8,128)}, f32[16,18,128]{2,1,0:T(8,128)}) custom-call(s32[1,128]{1,0:T(1,128)} %bitcast.30, f32[48,32]{1,0:T(8,128)} %constant.12.clone.polar_up_ref), custom_call_target="tpu_custom_call" | custom-call | tf_op jit(solution)/shard_map/tables/pallas_call | solution.py:311
  38.5 1.3 copy.19
  39.8 1.2 copy.20
  41.0 20.9 %child_translate.4.local_ref = f32[1,8,1024,128]{3,2,1,0:T(8,128)} custom-call(s32[12,128]{1,0:T(8,128)} %bitcast.25, s32[12,128]{1,0:T(8,128)} %bitcast.28, f32[2,4,2304,128]{3,2,1,0:T(8,128)} %bitcast.12, f32[2,2304,128]{2,1,0:T(8,128)} %bitcast.16), custom_call_target="tpu_custom_call" | custom-call | flops 50331648 | bytes 9437184 | tf_op jit(solution)/shard_map/child_translate/pallas_call | solution.py:136
  62.0 0.0 collective-permute-done.3
  62.0 0.0 collective-permute-done.2
  62.0 0.2 maximum_maximum_fusion
  62.2 1.1 copy.21
  63.3 69.4 %parent_level.1 = f32[30,104,128]{2,1,0:T(8,128)} custom-call(s32[16,12]{1,0:T(8,128)} %source_ref.1, s32[16,12]{1,0:T(8,128)} %kind_ref.1, f32[2,4,24,96,128]{4,3,2,1,0:T(8,128)} %bitcast.13, f32[2,4,3,96,128]{4,3,2,1,0:T(8,128)} %bitcast.21, f32[2,4,3,96,128]{4,3,2,1,0:T(8,128)} %bitcast.22, f32[2,4,30,8,128]{4,3,2,1,0:T(8,128)} %bitcast.23, ...), custom_call_target="tpu_custom_call" | custom-call | flops 20000000000 | bytes 18874368 | tf_op jit(solution)/shard_map/parent_level/pallas_call | solution.py:550
  132.7 1.0 fusion.2
  133.8 2.0 %collective-permute-start.4 = (f32[3,104,128]{2,1,0:T(8,128)S(1)}, f32[3,104,128]{2,1,0:T(8,128)S(1)}, u32[]{:S(2)}, u32[]{:S(2)}) collective-permute-start(f32[3,104,128]{2,1,0:T(8,128)S(1)} %get-tuple-element.49), channel_id=1, source_target_pairs={{0,4},{4,8},{8,12},{12,16},{16,20},{20,24},{24,28},{1,5},{5,9},{9,... | collective-permute-start | bytes 479240 | tf_op jit(solution)/shard_map/ppermute | solution.py:602
  135.7 0.0 copy-start
  135.8 4.6 %collective-permute-start.5 = (f32[3,104,128]{2,1,0:T(8,128)S(1)}, f32[3,104,128]{2,1,0:T(8,128)S(1)}, u32[]{:S(2)}, u32[]{:S(2)}) collective-permute-start(f32[3,104,128]{2,1,0:T(8,128)S(1)} %get-tuple-element.50), channel_id=1, source_target_pairs={{4,0},{8,4},{12,8},{16,12},{20,16},{24,20},{28,24},{5,1},{9,5},{13... | collective-permute-start | bytes 479240 | tf_op jit(solution)/shard_map/ppermute | solution.py:602
  140.4 6.5 %child_translate.5.local_ref = f32[1,2,1024,128]{3,2,1,0:T(8,128)} custom-call(s32[12,128]{1,0:T(8,128)} %bitcast.26, s32[12,128]{1,0:T(8,128)} %bitcast.29, f32[2,4,2304,128]{3,2,1,0:T(8,128)} %bitcast.14, f32[2,2304,128]{2,1,0:T(8,128)} %bitcast.17), custom_call_target="tpu_custom_call" | custom-call | flops 12582912 | bytes 2359296 | tf_op jit(solution)/shard_map/child_translate/pallas_call | solution.py:136
  146.9 0.0 collective-permute-done.4
  146.9 0.0 collective-permute-done.5
  146.9 0.0 copy-done
  146.9 0.1 pad_add_fusion
  147.0 0.1 collective-permute-start.6
  147.1 2.1 %collective-permute-start.7 = (f32[24,2,128]{2,1,0:T(2,128)S(1)}, f32[24,2,128]{2,1,0:T(2,128)S(1)}, u32[]{:S(2)}, u32[]{:S(2)}) collective-permute-start(f32[24,2,128]{2,1,0:T(2,128)S(1)} %slice.58), channel_id=1, source_target_pairs={{1,0},{2,1},{3,2},{0,3},{5,4},{6,5},{7,6},{4,7},{9,8},{10,9},{11,1... | collective-permute-start | bytes 73736 | tf_op jit(solution)/shard_map/ppermute | solution.py:602
  149.2 3.6 %collective-permute-done.7 = f32[24,2,128]{2,1,0:T(2,128)S(1)} collective-permute-done((f32[24,2,128]{2,1,0:T(2,128)S(1)}, f32[24,2,128]{2,1,0:T(2,128)S(1)}, u32[]{:S(2)}, u32[]{:S(2)}) %collective-permute-start.7) | collective-permute-done | bytes 24608 | tf_op jit(solution)/shard_map/ppermute | solution.py:602
  152.8 0.0 collective-permute-done.6
  152.8 1.2 fusion
  154.1 7.1 %final_sum.3.rest_0_ = f32[2,4,2304,128]{3,2,1,0:T(8,128)} custom-call(s32[128]{0:T(128)} %slot_ref.5, f32[1,8,1024,128]{3,2,1,0:T(8,128)} %child_translate.3.local_ref, f32[2304,128]{1,0:T(8,128)} %bitcast.18, f32[16,18,128]{2,1,0:T(8,128)} %get-tuple-element.44.phase_ref), custom_call_target="tpu_custom_call" | custom-call | flops 4194304 | bytes 9437184 | tf_op jit(solution)/shard_map/final_sum/pallas_call | solution.py:213
  161.2 7.1 %final_sum.4.rest_0_ = f32[2,4,2304,128]{3,2,1,0:T(8,128)} custom-call(s32[128]{0:T(128)} %slot_ref.5, f32[1,8,1024,128]{3,2,1,0:T(8,128)} %child_translate.4.local_ref, f32[2304,128]{1,0:T(8,128)} %bitcast.19, f32[16,18,128]{2,1,0:T(8,128)} %get-tuple-element.44.phase_ref, f32[2,4,2304,128]{3,2,1,0:T(8,128)} %final_sum.3.rest_0_), custom_call_target="tpu_custom_call", output_to_operand_aliasing={{}: (4, {})} | custom-call | flops 4194304 | bytes 9437184 | tf_op jit(solution)/shard_map/final_sum/pallas_call | solution.py:213
  168.3 4.1 %final_sum.5 = f32[2,4,2304,128]{3,2,1,0:T(8,128)} custom-call(s32[128]{0:T(128)} %slot_ref.5, f32[1,2,1024,128]{3,2,1,0:T(8,128)} %child_translate.5.local_ref, f32[2304,128]{1,0:T(8,128)} %bitcast.20, f32[16,18,128]{2,1,0:T(8,128)} %get-tuple-element.44.phase_ref, f32[2,4,2304,128]{3,2,1,0:T(8,128)} %final_sum.4.rest_0_), custom_call_target="tpu_custom_call", output_to_operand_aliasing={{}: (4, {})} | custom-call | flops 1048576 | bytes 2359296 | tf_op jit(solution)/shard_map/final_sum/pallas_call | solution.py:213
  (9 shorter events, 0.1 us)
Async XLA Ops:
  2.5 30.0 %collective-permute-start = (f32[8,3,96,128]{3,0,2,1:T(8,128)S(1)}, f32[8,3,96,128]{3,0,2,1:T(8,128)S(1)}, u32[]{:S(2)}, u32[]{:S(2)}) collective-permute-start(f32[8,3,96,128]{3,0,2,1:T(8,128)S(1)} %copy.23), channel_id=1, source_target_pairs={{4,0},{8,4},{12,8},{16,12},{20,16},{24,20},{28,24},{5,1},{9,5},{13... | collective-permute-start | bytes 3538952 | tf_op jit(solution)/shard_map/ppermute | solution.py:602
  7.0 25.7 %collective-permute-start.1 = (f32[8,3,96,128]{3,0,2,1:T(8,128)}, f32[8,3,96,128]{3,0,2,1:T(8,128)S(1)}, u32[]{:S(2)}, u32[]{:S(2)}) collective-permute-start(f32[8,3,96,128]{3,0,2,1:T(8,128)} %copy.24), channel_id=1, source_target_pairs={{0,4},{4,8},{8,12},{12,16},{16,20},{20,24},{24,28},{1,5},{5,9},{9,... | collective-permute-start | bytes 3538952 | tf_op jit(solution)/shard_map/ppermute | solution.py:602
  32.7 29.3 %collective-permute-start.2 = (f32[8,30,3,128]{3,0,2,1:T(8,128)S(1)}, f32[8,30,3,128]{3,0,2,1:T(8,128)S(1)}, u32[]{:S(2)}, u32[]{:S(2)}) collective-permute-start(f32[8,30,3,128]{3,0,2,1:T(8,128)S(1)} %pad_maximum_fusion), channel_id=1, source_target_pairs={{1,0},{2,1},{3,2},{0,3},{5,4},{6,5},{7,6},{4,7},{9,8},{10,9},{11,1... | collective-permute-start | bytes 1105928 | tf_op jit(solution)/shard_map/ppermute | solution.py:602
  33.2 28.8 %collective-permute-start.3 = (f32[8,30,2,128]{3,0,2,1:T(8,128)S(1)}, f32[8,30,2,128]{3,0,2,1:T(8,128)S(1)}, u32[]{:S(2)}, u32[]{:S(2)}) collective-permute-start(f32[8,30,2,128]{3,0,2,1:T(8,128)S(1)} %pad_maximum_fusion.1), channel_id=1, source_target_pairs={{0,1},{1,2},{2,3},{3,0},{4,5},{5,6},{6,7},{7,4},{8,9},{9,10},{10,1... | collective-permute-start | bytes 737288 | tf_op jit(solution)/shard_map/ppermute | solution.py:602
  133.8 13.1 %collective-permute-start.4 = (f32[3,104,128]{2,1,0:T(8,128)S(1)}, f32[3,104,128]{2,1,0:T(8,128)S(1)}, u32[]{:S(2)}, u32[]{:S(2)}) collective-permute-start(f32[3,104,128]{2,1,0:T(8,128)S(1)} %get-tuple-element.49), channel_id=1, source_target_pairs={{0,4},{4,8},{8,12},{12,16},{16,20},{20,24},{24,28},{1,5},{5,9},{9,... | collective-permute-start | bytes 479240 | tf_op jit(solution)/shard_map/ppermute | solution.py:602
  135.7 11.2 %copy-start = (f32[30,104,128]{2,1,0:T(8,128)S(1)}, f32[30,104,128]{2,1,0:T(8,128)}, u32[]{:S(2)}) copy-start(f32[30,104,128]{2,1,0:T(8,128)} %parent_level.1) | copy-start | bytes 4792324
  135.8 11.1 %collective-permute-start.5 = (f32[3,104,128]{2,1,0:T(8,128)S(1)}, f32[3,104,128]{2,1,0:T(8,128)S(1)}, u32[]{:S(2)}, u32[]{:S(2)}) collective-permute-start(f32[3,104,128]{2,1,0:T(8,128)S(1)} %get-tuple-element.50), channel_id=1, source_target_pairs={{4,0},{8,4},{12,8},{16,12},{20,16},{24,20},{28,24},{5,1},{9,5},{13... | collective-permute-start | bytes 479240 | tf_op jit(solution)/shard_map/ppermute | solution.py:602
  147.0 5.8 %collective-permute-start.6 = (f32[24,3,128]{2,1,0:T(4,128)S(1)}, f32[24,3,128]{2,1,0:T(4,128)S(1)}, u32[]{:S(2)}, u32[]{:S(2)}) collective-permute-start(f32[24,3,128]{2,1,0:T(4,128)S(1)} %slice.57), channel_id=1, source_target_pairs={{0,1},{1,2},{2,3},{3,0},{4,5},{5,6},{6,7},{7,4},{8,9},{9,10},{10,1... | collective-permute-start | bytes 110600 | tf_op jit(solution)/shard_map/ppermute | solution.py:602
  147.1 5.7 %collective-permute-start.7 = (f32[24,2,128]{2,1,0:T(2,128)S(1)}, f32[24,2,128]{2,1,0:T(2,128)S(1)}, u32[]{:S(2)}, u32[]{:S(2)}) collective-permute-start(f32[24,2,128]{2,1,0:T(2,128)S(1)} %slice.58), channel_id=1, source_target_pairs={{1,0},{2,1},{3,2},{0,3},{5,4},{6,5},{7,6},{4,7},{9,8},{10,9},{11,1... | collective-permute-start | bytes 73736 | tf_op jit(solution)/shard_map/ppermute | solution.py:602

commit v4 on v3

--- a/solution.py
+++ b/solution.py
@@ -71,7 +71,7 @@
 
 def segments(samples):
     full, rest = divmod(samples, 8 * LANES)
-    found = [(i, 1, 1, 8) for i in range(full)]
+    found = [(0, full, 1, 8)] if full else []
     if rest:
         rows = -(-rest // LANES)
         packed = 4 if rows <= 2 else 2 if rows <= 4 else 1
@@ -79,129 +79,139 @@
     return found
 
 
-def lie_across(from_rows, to_tiles, plane, offsets, row):
-    turned = from_rows.T
-    for offset in offsets:
-        to_tiles[plane, pl.ds(offset + row, LANES, stride=8), :] = turned
-
-
-def translate_kernel(packed, rows, source_ref, kind_ref, child_ref, table_ref, out_ref, pattern, table):
+def translate_kernel(packed, rows, source_ref, kind_ref, child_ref, table_ref, *rest):
+    out_ref, pattern, table = rest[-3:]
     groups, per = 4 // packed, 8 // packed
+    tile = 16 * groups
     entries = source_ref.shape[0]
-
-    for row in range(rows):
-        at = slice(row * LANES, (row + 1) * LANES)
-        for part in range(2):
-            lie_across(table_ref[part, at], table, part, [c * per for c in range(packed)], row)
-
-    def one_channel(c, carry):
-        for part in range(2):
-            for row in range(rows):
-                lie_across(
-                    child_ref[part, c, row * LANES : (row + 1) * LANES],
-                    pattern,
-                    part * groups + c // packed,
-                    [c % packed * per],
-                    row,
-                )
-        return carry
-
-    lax.fori_loop(0, 4, one_channel, 0)
-
-    def one_box(box, carry):
-        total = [None] * (2 * groups)
-        for entry in range(entries):
-            source = pl.ds(pl.multiple_of(source_ref[entry, box] * 8, 8), 8)
-            kind = pl.ds(pl.multiple_of(kind_ref[entry, box] * 8, 8), 8)
-            real, imag = table[0, kind, :], table[1, kind, :]
-            for g in range(groups):
-                x, y = pattern[g, source, :], pattern[groups + g, source, :]
-                re = x * real - y * imag
-                im = x * imag + y * real
-                total[g] = re if entry == 0 else total[g] + re
-                total[groups + g] = im if entry == 0 else total[groups + g] + im
-        for g in range(2 * groups):
-            out_ref[0, g, pl.ds(pl.multiple_of(box * 8, 8), 8), :] = total[g]
-        return carry
-
-    lax.fori_loop(0, LANES, one_box, 0, unroll=8)
-
-
-def child_translate(child, table, sources, kinds, segment):
+    step = pl.program_id(0)
+
+    @pl.when(step == 0)
+    def _():
+        for row in range(rows):
+            for part in range(2):
+                turned = table_ref[part, row * LANES : (row + 1) * LANES].T
+                for c in range(packed):
+                    table[pl.ds(part * 8 + c * per + row, LANES, stride=16), :] = turned
+
+    @pl.when(step < 2)
+    def _():
+        for i in range(2):
+            c = 2 * step + i
+            plane, sub = (c, 0) if packed == 1 else (c // packed, c % packed * per)
+            for part in range(2):
+                for row in range(rows):
+                    at = pl.ds((part * groups + plane) * 8 + sub + row, LANES, stride=tile)
+                    pattern[at, :] = child_ref[part, i, row * LANES : (row + 1) * LANES].T
+
+    @pl.when(step >= 2)
+    def _():
+        half = LANES // 2
+
+        def one_box(i, carry):
+            box = (step - 2) * half + i
+            total = [None] * (2 * groups)
+            for entry in range(entries):
+                x = pattern[pl.ds(pl.multiple_of(source_ref[entry, box] * tile, tile), tile), :]
+                factor = table[pl.ds(pl.multiple_of(kind_ref[entry, box] * 16, 16), 16), :]
+                real, imag = factor[:8], factor[8:]
+                for g in range(groups):
+                    xr, xi = x[g * 8 : g * 8 + 8], x[(groups + g) * 8 : (groups + g) * 8 + 8]
+                    re = xr * real - xi * imag
+                    im = xr * imag + xi * real
+                    total[g] = re if entry == 0 else total[g] + re
+                    total[groups + g] = im if entry == 0 else total[groups + g] + im
+            for g in range(2 * groups):
+                out_ref[0, pl.ds(pl.multiple_of(i * tile, tile) + g * 8, 8), :] = total[g]
+            return carry
+
+        lax.fori_loop(0, half, one_box, 0, unroll=2)
+
+
+def child_translate(child, table, sources, kinds, segment, chunk, onto):
     first, count, packed, rows = segment
-    entries = sources.shape[0]
-    planes = 8 // packed
+    tile = 64 // packed
     smem = pl.BlockSpec(memory_space=pltpu.SMEM)
-    work = count * rows * LANES * LANES
+    in_specs = [
+        smem,
+        smem,
+        pl.BlockSpec((2, 2, 8 * LANES, LANES), lambda s: (0, jnp.minimum(s, 1), first + chunk, 0)),
+        pl.BlockSpec((2, 8 * LANES, LANES), lambda s: (0, first + chunk, 0)),
+    ]
+    operands = [sources, kinds, child, table]
+    aliases = {}
+    if onto is not None:
+        in_specs.append(pl.BlockSpec(memory_space=pl.ANY))
+        operands.append(onto)
+        aliases = {4: 0}
+    work = rows * LANES * LANES
     return pl.pallas_call(
         functools.partial(translate_kernel, packed, rows),
-        grid=(count,),
-        in_specs=[
-            smem,
-            smem,
-            pl.BlockSpec((2, 4, 8 * LANES, LANES), lambda i: (0, 0, first + i, 0)),
-            pl.BlockSpec((2, 8 * LANES, LANES), lambda i: (0, first + i, 0)),
-        ],
-        out_specs=pl.BlockSpec((1, planes, 8 * LANES, LANES), lambda i: (i, 0, 0, 0)),
-        out_shape=jax.ShapeDtypeStruct((count, planes, 8 * LANES, LANES), F32),
-        scratch_shapes=[
-            pltpu.VMEM((planes, 8 * LANES, LANES), F32),
-            pltpu.VMEM((2, 8 * LANES, LANES), F32),
-        ],
+        grid=(4,),
+        in_specs=in_specs,
+        out_specs=pl.BlockSpec((1, LANES // 2 * tile, LANES), lambda s: (chunk, jnp.maximum(s - 2, 0), 0)),
+        out_shape=jax.ShapeDtypeStruct((count, LANES * tile, LANES), F32),
+        input_output_aliases=aliases,
+        scratch_shapes=[pltpu.VMEM((LANES * tile, LANES), F32), pltpu.VMEM((LANES * 16, LANES), F32)],
         compiler_params=pltpu.CompilerParams(vmem_limit_bytes=60 * MIB),
-        cost_estimate=pl.CostEstimate(flops=work * entries * 32, bytes_accessed=work * 72, transcendentals=0),
+        cost_estimate=pl.CostEstimate(
+            flops=work * sources.shape[0] * 32, bytes_accessed=work * 72, transcendentals=0
+        ),
         name="child_translate",
-    )(sources, kinds, child, table)
+    )(*operands)
 
 
 def sum_kernel(packed, rows, parents, slot_ref, local_ref, lowered_ref, phase_ref, *rest):
     out_ref, lowered, total = rest[-3:]
     groups, per = 4 // packed, 8 // packed
-
-    for row in range(rows):
-        lie_across(lowered_ref[row * LANES : (row + 1) * LANES], lowered, 0, [0], row)
-
-    def one_box(box, carry):
-        slot = slot_ref[box]
-        parent = slot % parents * 8
-        octant = slot // parents
-        cosine, sine = phase_ref[octant], phase_ref[8 + octant]
-        here = pl.ds(pl.multiple_of(box * 8, 8), 8)
-        for c in range(4):
-            x = lowered[0, pl.ds(pl.multiple_of(parent + c * parents * 8, 8), 8), :][:per]
-            y = lowered[0, pl.ds(pl.multiple_of(parent + (4 + c) * parents * 8, 8), 8), :][:per]
-            re = x * cosine[:per] + y * sine[:per]
-            im = y * cosine[:per] - x * sine[:per]
-            if packed == 1:
-                total[c, here, :] = local_ref[0, c, here, :] + re
-                total[4 + c, here, :] = local_ref[0, 4 + c, here, :] + im
-            else:
-                here = pl.ds(pl.multiple_of(box * 8, 8) + c % packed * per, per)
-                total[c // packed, here, :] = local_ref[0, c // packed, here, :] + re
-                total[groups + c // packed, here, :] = local_ref[0, groups + c // packed, here, :] + im
-        return carry
-
-    lax.fori_loop(0, LANES, one_box, 0, unroll=4)
-
-    def one_channel(c, carry):
-        for part in range(2):
-            for row in range(rows):
-                turned = total[part * groups + c // packed, pl.ds(c % packed * per + row, LANES, stride=8), :].T
-                out_ref[part, c, row * LANES : (row + 1) * LANES] = turned
-        return carry
-
-    lax.fori_loop(0, 4, one_channel, 0)
+    tile = 16 * groups
+    step = pl.program_id(1)
+
+    @pl.when(step == 0)
+    def _():
+        for row in range(rows):
+            lowered[pl.ds(row, LANES, stride=8), :] = lowered_ref[row * LANES : (row + 1) * LANES].T
+
+    @pl.when(step < 2)
+    def _():
+        half = LANES // 2
+
+        def one_box(i, carry):
+            slot = slot_ref[step * half + i]
+            octant = slot // parents
+            cosine, sine = phase_ref[octant][:per], phase_ref[8 + octant][:per]
+            x = lowered[pl.ds(pl.multiple_of(slot % parents * 64, 64), 64), :]
+            local = local_ref[0, pl.ds(pl.multiple_of(i * tile, tile), tile), :]
+            for c in range(4):
+                real, imag = x[c * 8 : c * 8 + per], x[(4 + c) * 8 : (4 + c) * 8 + per]
+                at = c // packed * 8 + c % packed * per
+                here = pl.multiple_of((step * half + i) * tile, tile)
+                total[pl.ds(here + at, per), :] = local[at : at + per] + (real * cosine + imag * sine)
+                at += groups * 8
+                total[pl.ds(here + at, per), :] = local[at : at + per] + (imag * cosine - real * sine)
+            return carry
+
+        lax.fori_loop(0, half, one_box, 0, unroll=4)
+
+    @pl.when(step >= 2)
+    def _():
+        for i in range(2):
+            c = 2 * (step - 2) + i
+            plane, sub = (c, 0) if packed == 1 else (c // packed, c % packed * per)
+            for part in range(2):
+                for row in range(rows):
+                    at = pl.ds((part * groups + plane) * 8 + sub + row, LANES, stride=tile)
+                    out_ref[part, i, row * LANES : (row + 1) * LANES] = total[at, :].T
 
 
 def final_sum(shape, local, lowered, phase, slots, segment, onto):
     first, count, packed, rows = segment
-    planes = 8 // packed
-    smem = pl.BlockSpec(memory_space=pltpu.SMEM)
+    tile = 64 // packed
     in_specs = [
-        smem,
-        pl.BlockSpec((1, planes, 8 * LANES, LANES), lambda i: (i, 0, 0, 0)),
-        pl.BlockSpec((8 * LANES, LANES), lambda i: (first + i, 0)),
-        pl.BlockSpec((16, 8, LANES), lambda i: (0, first + i, 0)),
+        pl.BlockSpec(memory_space=pltpu.SMEM),
+        pl.BlockSpec((1, LANES // 2 * tile, LANES), lambda i, s: (i, jnp.minimum(s, 1), 0)),
+        pl.BlockSpec((8 * LANES, LANES), lambda i, s: (first + i, 0)),
+        pl.BlockSpec((16, 8, LANES), lambda i, s: (0, first + i, 0)),
     ]
     operands = [slots, local, lowered, phase]
     aliases = {}
@@ -212,15 +222,12 @@
     work = count * rows * LANES * LANES
     return pl.pallas_call(
         functools.partial(sum_kernel, packed, rows, LANES // 8),
-        grid=(count,),
+        grid=(count, 4),
         in_specs=in_specs,
-        out_specs=pl.BlockSpec((2, 4, 8 * LANES, LANES), lambda i: (0, 0, first + i, 0)),
+        out_specs=pl.BlockSpec((2, 2, 8 * LANES, LANES), lambda i, s: (0, jnp.maximum(s - 2, 0), first + i, 0)),
         out_shape=jax.ShapeDtypeStruct(shape, F32),
         input_output_aliases=aliases,
-        scratch_shapes=[
-            pltpu.VMEM((1, 8 * LANES, LANES), F32),
-            pltpu.VMEM((planes, 8 * LANES, LANES), F32),
-        ],
+        scratch_shapes=[pltpu.VMEM((8 * LANES, LANES), F32), pltpu.VMEM((LANES * tile, LANES), F32)],
         compiler_params=pltpu.CompilerParams(vmem_limit_bytes=60 * MIB),
         cost_estimate=pl.CostEstimate(flops=work * 32, bytes_accessed=work * 72, transcendentals=0),
         name="final_sum",
@@ -348,7 +355,9 @@
     lowered,
 ):
     (rows, columns, rows_up, columns_up, parents, entries, table_steps, table_rows) = sizes
-    t_pad, p_pad, f_pad, q_pad = wide.shape[1] // 128, parent_out.shape[3], wide.shape[2], parent_out.shape[4]
+    t_pad, f_pad = wide.shape[1] // 128, wide.shape[2]
+    p_pad, q_pad = phase_ref.shape[1], phase_ref.shape[2]
+    row_tiles, lane_tiles = p_pad // 8, q_pad // LANES
     step = pl.program_id(0)
     half = 4 * parents
     table_first = jnp.minimum(step, table_steps - 1) * table_rows
@@ -360,10 +369,9 @@
                 wide[part, pl.ds(t, 128, stride=t_pad), :] = jnp.zeros((128, f_pad), F32)
         for part in range(2):
             for p in range(rows_up, p_pad):
-                for lane in range(0, q_pad, LANES):
-                    table_by_kind[lane // LANES, pl.ds(part * p_pad + p, 128, stride=2 * p_pad), :] = jnp.zeros(
-                        (128, LANES), F32
-                    )
+                for lane_tile in range(lane_tiles):
+                    at = pl.ds(part * 8 + p % 8, 128, stride=16)
+                    table_by_kind[lane_tile * row_tiles + p // 8, at, :] = jnp.zeros((128, LANES), F32)
 
     combine = combine_ref[...]
 
@@ -398,8 +406,9 @@
                     x = jnp.concatenate([x, jnp.zeros((q_pad - columns_up, LANES), F32)], axis=0)
                 for lane in range(0, q_pad, LANES):
                     turned = x[lane : lane + LANES].T
-                    at = pl.ds(part * p_pad + table_first + r, 128, stride=2 * p_pad)
-                    table_by_kind[lane // LANES, at, :] = turned
+                    p = table_first + r
+                    at = pl.ds(part * 8 + p % 8, 128, stride=16)
+                    table_by_kind[lane // LANES * row_tiles + p // 8, at, :] = turned
         return carry
 
     lax.fori_loop(0, turns, main_rows, 0)
@@ -449,36 +458,43 @@
                     value = (terms[0] - terms[1]) + (terms[2] - terms[3])
                 else:
                     value = (terms[0] + terms[1]) + (terms[2] + terms[3])
-                parent_out[target, step, group * per + i] = value
+                at = pl.ds(pl.multiple_of((group * per + i) * 64 + target * 32 + step * 8, 8), 8)
+                for lane_tile in range(lane_tiles):
+                    lanes = slice(lane_tile * LANES, (lane_tile + 1) * LANES)
+                    for row_tile in range(row_tiles):
+                        tile = value[row_tile * 8 : row_tile * 8 + 8, lanes]
+                        parent_out[lane_tile * row_tiles + row_tile, at, :] = tile
             return carry
 
         lax.fori_loop(0, parents // per, one_group, 0)
 
     @pl.when(step == 3)
     def _():
-        tiles = q_pad // LANES
-
         def one_tile(tile, carry):
             box = tile // (p_pad // 16)
-            row = tile % (p_pad // 16) * 16
-            sources = [source_ref[box, e] for e in range(entries)]
-            kinds = [kind_ref[box, e] * (2 * p_pad) + row for e in range(entries)]
-            for lane_tile in range(tiles):
-                lanes = slice(lane_tile * LANES, (lane_tile + 1) * LANES)
-                total = [None] * 8
-                for e in range(entries):
-                    real = table_by_kind[lane_tile, pl.ds(pl.multiple_of(kinds[e], 16), 16), :]
-                    imag = table_by_kind[lane_tile, pl.ds(pl.multiple_of(kinds[e] + p_pad, 16), 16), :]
-                    for c in range(4):
-                        x = parent_out[0, c, sources[e], pl.ds(pl.multiple_of(row, 16), 16), lanes]
-                        y = parent_out[1, c, sources[e], pl.ds(pl.multiple_of(row, 16), 16), lanes]
-                        re = x * real - y * imag
-                        im = x * imag + y * real
-                        total[c] = re if e == 0 else total[c] + re
-                        total[4 + c] = im if e == 0 else total[4 + c] + im
+            row_pair = tile % (p_pad // 16)
+            sources = [pl.ds(pl.multiple_of(source_ref[box, e] * 64, 64), 64) for e in range(entries)]
+            kinds = [pl.ds(pl.multiple_of(kind_ref[box, e] * 16, 16), 16) for e in range(entries)]
+            for lane_tile in range(lane_tiles):
+                halves = []
+                for i in range(2):
+                    where = lane_tile * row_tiles + 2 * row_pair + i
+                    total = [None] * 8
+                    for e in range(entries):
+                        x = parent_out[where, sources[e], :]
+                        factor = table_by_kind[where, kinds[e], :]
+                        real, imag = factor[:8], factor[8:]
+                        for c in range(4):
+                            xr, xi = x[c * 8 : c * 8 + 8], x[(4 + c) * 8 : (4 + c) * 8 + 8]
+                            re = xr * real - xi * imag
+                            im = xr * imag + xi * real
+                            total[c] = re if e == 0 else total[c] + re
+                            total[4 + c] = im if e == 0 else total[4 + c] + im
+                    halves.append(total)
                 for c in range(8):
-                    high, low = split(total[c])
-                    at = pl.ds(pl.multiple_of((c * parents + box) * p_pad + row, 16), 16)
+                    high, low = split(jnp.concatenate([halves[0][c], halves[1][c]], axis=0))
+                    at = pl.ds(pl.multiple_of((c * parents + box) * p_pad + row_pair * 16, 16), 16)
+                    lanes = slice(lane_tile * LANES, (lane_tile + 1) * LANES)
                     in_high[at, lanes] = high
                     in_low[at, lanes] = low
             return carry
@@ -502,7 +518,7 @@
                 high, low = split(x)
                 z = dot(polar_back, jnp.concatenate([high, low, high], axis=0))
                 for j in range(2):
-                    lowered[pl.ds(pl.multiple_of((group * per + i + j) * t_pad, 8), t_pad), :] = z[
+                    lowered[pl.ds(pl.multiple_of(((i + j) * 8 + group) * t_pad, 8), t_pad), :] = z[
                         :, j * f_pad : (j + 1) * f_pad
                     ]
             return carry
@@ -569,8 +585,8 @@
         scratch_shapes=[
             pltpu.VMEM((2, 128 * t_pad, f_pad), F32),
             pltpu.VMEM((4, parents * p_pad, 3 * f_pad), BF16),
-            pltpu.VMEM((q_pad // LANES, translators * 2 * p_pad, LANES), F32),
-            pltpu.VMEM((2, 4, parents, p_pad, q_pad), F32),
+            pltpu.VMEM((q_pad // LANES * (p_pad // 8), translators * 16, LANES), F32),
+            pltpu.VMEM((q_pad // LANES * (p_pad // 8), parents * 64, LANES), F32),
             pltpu.VMEM((8 * parents * p_pad, q_pad), BF16),
             pltpu.VMEM((8 * parents * p_pad, q_pad), BF16),
             pltpu.VMEM((8 * parents * t_pad, f_pad), F32),
@@ -630,11 +646,15 @@
     flat_child = child_out.reshape(2, 4, samples, boxes)
     flat_table = table_child.reshape(2, samples, table_child.shape[3])
     pieces = segments(samples)
-    local = []
+    local = [None] * len(pieces)
+    chunks = [(n, i) for n, piece in enumerate(pieces) for i in range(piece[1])]
 
     def translate_next(child):
-        if len(local) < len(pieces):
-            local.append(child_translate(child, flat_table, sources_child.T, kinds_child.T, pieces[len(local)]))
+        if chunks:
+            n, i = chunks.pop(0)
+            local[n] = child_translate(
+                child, flat_table, sources_child.T, kinds_child.T, pieces[n], i, local[n]
+            )
 
     after = send(child_out[:, :3], "theta", False)
     before = send(child_out[:, rows - 3 :], "theta", True)
@@ -648,7 +668,7 @@
     low, high, later_child = barrier((low, high, flat_child))
     right = send(low, "phi", False)
     left = send(high, "phi", True)
-    if len(pieces) > 2:
+    if len(chunks) > 1:
         translate_next(later_child)
     right, left, local = barrier((right, left, local))
     side = jnp.concatenate([right, left, jnp.zeros((8, rows + 6, 3, boxes), F32)], axis=2)
@@ -670,7 +690,7 @@
 
     low = send(lowered[rows : rows + 3], "theta", True)
     high = send(lowered[rows + 3 : rows + 6], "theta", False)
-    while len(local) < len(pieces):
+    while chunks:
         translate_next(later_child)
     local, lowered = barrier((local, lowered))
     here = lowered[:rows]

time: 173 us -> 159 us (0.919)
  Pallas kernels: 138 us -> 118 us
  waiting for transfers between devices: 3.76 us -> 9.46 us
    pallas_call x3, Pallas kernels: 48.4 us -> 37.3 us  [child_translate(): pl.pallas_call(functools.partial(translate_kernel, packed, rows), grid=(4...]
    pallas_call x1, Pallas kernels: 69.4 us -> 62 us  [parent_level(): pl.pallas_call(functools.partial(parent_kernel, (rows, columns, rows_up,...]
    ppermute x8, waiting for transfers between devices: 3.76 us -> 9.46 us  [send(): lax.ppermute(block, axis, pairs if up else [(b, a) for a, b in pairs])]
    pallas_call x3 -> x2, Pallas kernels: 18.4 us -> 17.2 us  [final_sum(): pl.pallas_call(functools.partial(sum_kernel, packed, rows, LANES // 8), g...]
  transfers between devices with their start and end apart: 8 -> 8, of which waited for: 2 -> 3; matrix products, arithmetic and copies ran while one was open for 4% -> 4% of each run, Pallas kernels for 29% -> 25%
where the time goes in v4:
time: 159 us
  Pallas kernels  118 us (74%)
  starting transfers between devices  17.5 us (11%)
  local copies, waits for them, and re-layouts  11.7 us (7%)
  waiting for transfers between devices  9.46 us (6%)
    pallas_call x1, Pallas kernels, parent_level(): pl.pallas_call(functools.partial(parent_kernel, (rows, columns, rows_up,...  62 us
    pallas_call x3, Pallas kernels, child_translate(): pl.pallas_call(functools.partial(translate_kernel, packed, rows), grid=(4...  37.3 us
    ppermute x8, starting transfers between devices, send(): lax.ppermute(block, axis, pairs if up else [(b, a) for a, b in pairs])  17.5 us
    pallas_call x2, Pallas kernels, final_sum(): pl.pallas_call(functools.partial(sum_kernel, packed, rows, LANES // 8), g...  17.2 us
    ppermute x8, waiting for transfers between devices, send(): lax.ppermute(block, axis, pairs if up else [(b, a) for a, b in pairs])  9.46 us
  transfers between devices with their start and end apart: 8, of which 3 were waited for; matrix products, arithmetic and copies ran while one was open for 4% of the time, Pallas kernels for 25%

profile of v4, /device:TPU:28, one launch (start us, length us, event | category | flops | bytes accessed | tf_op | source)
XLA Modules:
  0.0 158.7 jit_solution(14475588309418725111)
XLA Ops:
  0.0 1.8 %fusion.1 = (f32[8,3,96,128]{3,2,1,0:T(8,128)S(1)}, f32[8,3,96,128]{3,2,1,0:T(8,128)S(1)}) fusion(f32[8,24,96,128]{3,2,1,0:T(8,128)} %param.12), kind=kLoop, calls=%fused_computation.6 | loop fusion | bytes 4718592 | tf_op jit(solution)/shard_map/slice | solution.py:660
  1.8 0.7 copy.23
  2.5 2.8 %collective-permute-start = (f32[8,3,96,128]{3,0,2,1:T(8,128)S(1)}, f32[8,3,96,128]{3,0,2,1:T(8,128)S(1)}, u32[]{:S(2)}, u32[]{:S(2)}) collective-permute-start(f32[8,3,96,128]{3,0,2,1:T(8,128)S(1)} %copy.23), channel_id=1, source_target_pairs={{4,0},{8,4},{12,8},{16,12},{20,16},{24,20},{28,24},{5,1},{9,5},{13... | collective-permute-start | bytes 3538952 | tf_op jit(solution)/shard_map/ppermute | solution.py:618
  5.3 1.7 %copy.24 = f32[8,3,96,128]{3,0,2,1:T(8,128)} copy(f32[8,3,96,128]{3,2,1,0:T(8,128)S(1)} %get-tuple-element.43) | data formatting | bytes 2359296
  7.0 1.9 %collective-permute-start.1 = (f32[8,3,96,128]{3,0,2,1:T(8,128)}, f32[8,3,96,128]{3,0,2,1:T(8,128)S(1)}, u32[]{:S(2)}, u32[]{:S(2)}) collective-permute-start(f32[8,3,96,128]{3,0,2,1:T(8,128)} %copy.24), channel_id=1, source_target_pairs={{0,4},{4,8},{8,12},{12,16},{16,20},{20,24},{24,28},{1,5},{5,9},{9,... | collective-permute-start | bytes 3538952 | tf_op jit(solution)/shard_map/ppermute | solution.py:618
  8.9 1.2 slice.47
  10.1 1.2 slice.42
  11.3 0.1 copy.25
  11.4 0.2 copy.22
  11.6 15.2 %child_translate.3.rest_0_ = f32[2,8192,128]{2,1,0:T(8,128)} custom-call(s32[12,128]{1,0:T(8,128)} %bitcast.23, s32[12,128]{1,0:T(8,128)} %bitcast.26, f32[2,4,2304,128]{3,2,1,0:T(8,128)} %bitcast.11, f32[2,2304,128]{2,1,0:T(8,128)} %bitcast.15), custom_call_target="tpu_custom_call" | custom-call | flops 50331648 | bytes 9437184 | tf_op jit(solution)/shard_map/child_translate/pallas_call | solution.py:148
  26.8 0.9 collective-permute-done
  27.7 5.0 %collective-permute-done.1 = f32[8,3,96,128]{3,0,2,1:T(8,128)S(1)} collective-permute-done((f32[8,3,96,128]{3,0,2,1:T(8,128)}, f32[8,3,96,128]{3,0,2,1:T(8,128)S(1)}, u32[]{:S(2)}, u32[]{:S(2)}) %collective-permute-start.1) | collective-permute-done | bytes 1179680 | tf_op jit(solution)/shard_map/ppermute | solution.py:618
  32.7 0.5 collective-permute-start.2
  33.2 3.4 %collective-permute-start.3 = (f32[8,30,2,128]{3,0,2,1:T(8,128)S(1)}, f32[8,30,2,128]{3,0,2,1:T(8,128)S(1)}, u32[]{:S(2)}, u32[]{:S(2)}) collective-permute-start(f32[8,30,2,128]{3,0,2,1:T(8,128)S(1)} %pad_maximum_fusion.1), channel_id=1, source_target_pairs={{0,1},{1,2},{2,3},{3,0},{4,5},{5,6},{6,7},{7,4},{8,9},{9,10},{10,1... | collective-permute-start | bytes 737288 | tf_op jit(solution)/shard_map/ppermute | solution.py:618
  36.6 0.1 pad.22.clone
  36.7 1.8 %tables.1 = (bf16[128,256]{1,0:T(8,128)(2,1)}, f32[48,32]{1,0:T(8,128)}, f32[48,32]{1,0:T(8,128)}, f32[4,48,256]{2,1,0:T(8,128)}, f32[16,18,128]{2,1,0:T(8,128)}) custom-call(s32[1,128]{1,0:T(1,128)} %bitcast.29, f32[48,32]{1,0:T(8,128)} %constant.12.clone.polar_up_ref), custom_call_target="tpu_custom_call" | custom-call | tf_op jit(solution)/shard_map/tables/pallas_call | solution.py:318
  38.5 1.3 copy.19
  39.8 1.2 copy.20
  41.0 15.2 %child_translate.4.local_ref = f32[2,8192,128]{2,1,0:T(8,128)} custom-call(s32[12,128]{1,0:T(8,128)} %bitcast.24, s32[12,128]{1,0:T(8,128)} %bitcast.27, f32[2,4,2304,128]{3,2,1,0:T(8,128)} %bitcast.12, f32[2,2304,128]{2,1,0:T(8,128)} %bitcast.16, f32[2,8192,128]{2,1,0:T(8,128)} %child_translate.3.rest_0_), custom_call_target="tpu_custom_call", output_to_operand_aliasing={{}: (4, {})} | custom-call | flops 50331648 | bytes 9437184 | tf_op jit(solution)/shard_map/child_translate/pallas_call | solution.py:148
  56.3 0.0 collective-permute-done.3
  56.3 0.0 collective-permute-done.2
  56.3 0.2 maximum_maximum_fusion
  56.5 1.1 copy.21
  57.6 62.0 %parent_level.1 = f32[30,104,128]{2,1,0:T(8,128)} custom-call(s32[16,12]{1,0:T(8,128)} %source_ref.1, s32[16,12]{1,0:T(8,128)} %kind_ref.1, f32[2,4,24,96,128]{4,3,2,1,0:T(8,128)} %bitcast.13, f32[2,4,3,96,128]{4,3,2,1,0:T(8,128)} %bitcast.20, f32[2,4,3,96,128]{4,3,2,1,0:T(8,128)} %bitcast.21, f32[2,4,30,8,128]{4,3,2,1,0:T(8,128)} %bitcast.22, ...), custom_call_target="tpu_custom_call" | custom-call | flops 20000000000 | bytes 18874368 | tf_op jit(solution)/shard_map/parent_level/pallas_call | solution.py:566
  119.6 1.0 fusion.2
  120.7 1.9 %collective-permute-start.4 = (f32[3,104,128]{2,1,0:T(8,128)S(1)}, f32[3,104,128]{2,1,0:T(8,128)S(1)}, u32[]{:S(2)}, u32[]{:S(2)}) collective-permute-start(f32[3,104,128]{2,1,0:T(8,128)S(1)} %get-tuple-element.45), channel_id=1, source_target_pairs={{0,4},{4,8},{8,12},{12,16},{16,20},{20,24},{24,28},{1,5},{5,9},{9,... | collective-permute-start | bytes 479240 | tf_op jit(solution)/shard_map/ppermute | solution.py:618
  122.6 0.0 copy-start
  122.6 4.9 %collective-permute-start.5 = (f32[3,104,128]{2,1,0:T(8,128)S(1)}, f32[3,104,128]{2,1,0:T(8,128)S(1)}, u32[]{:S(2)}, u32[]{:S(2)}) collective-permute-start(f32[3,104,128]{2,1,0:T(8,128)S(1)} %get-tuple-element.46), channel_id=1, source_target_pairs={{4,0},{8,4},{12,8},{16,12},{20,16},{24,20},{28,24},{5,1},{9,5},{13... | collective-permute-start | bytes 479240 | tf_op jit(solution)/shard_map/ppermute | solution.py:618
  127.5 6.9 %child_translate.5.local_ref = f32[1,2048,128]{2,1,0:T(8,128)} custom-call(s32[12,128]{1,0:T(8,128)} %bitcast.25, s32[12,128]{1,0:T(8,128)} %bitcast.28, f32[2,4,2304,128]{3,2,1,0:T(8,128)} %bitcast.14, f32[2,2304,128]{2,1,0:T(8,128)} %bitcast.17), custom_call_target="tpu_custom_call" | custom-call | flops 12582912 | bytes 2359296 | tf_op jit(solution)/shard_map/child_translate/pallas_call | solution.py:148
  134.3 0.0 collective-permute-done.4
  134.3 0.0 collective-permute-done.5
  134.3 0.0 copy-done
  134.3 0.1 pad_add_fusion
  134.5 0.1 collective-permute-start.6
  134.6 2.1 %collective-permute-start.7 = (f32[24,2,128]{2,1,0:T(2,128)S(1)}, f32[24,2,128]{2,1,0:T(2,128)S(1)}, u32[]{:S(2)}, u32[]{:S(2)}) collective-permute-start(f32[24,2,128]{2,1,0:T(2,128)S(1)} %slice.58), channel_id=1, source_target_pairs={{1,0},{2,1},{3,2},{0,3},{5,4},{6,5},{7,6},{4,7},{9,8},{10,9},{11,1... | collective-permute-start | bytes 73736 | tf_op jit(solution)/shard_map/ppermute | solution.py:618
  136.6 3.6 %collective-permute-done.7 = f32[24,2,128]{2,1,0:T(2,128)S(1)} collective-permute-done((f32[24,2,128]{2,1,0:T(2,128)S(1)}, f32[24,2,128]{2,1,0:T(2,128)S(1)}, u32[]{:S(2)}, u32[]{:S(2)}) %collective-permute-start.7) | collective-permute-done | bytes 24608 | tf_op jit(solution)/shard_map/ppermute | solution.py:618
  140.2 0.0 collective-permute-done.6
  140.2 1.2 fusion
  141.5 13.3 %final_sum.2.rest_0_ = f32[2,4,2304,128]{3,2,1,0:T(8,128)} custom-call(s32[128]{0:T(128)} %slot_ref.3, f32[2,8192,128]{2,1,0:T(8,128)} %child_translate.4.local_ref, f32[2304,128]{1,0:T(8,128)} %bitcast.18, f32[16,18,128]{2,1,0:T(8,128)} %get-tuple-element.41.phase_ref), custom_call_target="tpu_custom_call" | custom-call | flops 8388608 | bytes 18874368 | tf_op jit(solution)/shard_map/final_sum/pallas_call | solution.py:223
  154.8 3.9 %final_sum.3 = f32[2,4,2304,128]{3,2,1,0:T(8,128)} custom-call(s32[128]{0:T(128)} %slot_ref.3, f32[1,2048,128]{2,1,0:T(8,128)} %child_translate.5.local_ref, f32[2304,128]{1,0:T(8,128)} %bitcast.19, f32[16,18,128]{2,1,0:T(8,128)} %get-tuple-element.41.phase_ref, f32[2,4,2304,128]{3,2,1,0:T(8,128)} %final_sum.2.rest_0_), custom_call_target="tpu_custom_call", output_to_operand_aliasing={{}: (4, {})} | custom-call | flops 1048576 | bytes 2359296 | tf_op jit(solution)/shard_map/final_sum/pallas_call | solution.py:223
  (9 shorter events, 0.1 us)
Async XLA Ops:
  2.5 25.2 %collective-permute-start = (f32[8,3,96,128]{3,0,2,1:T(8,128)S(1)}, f32[8,3,96,128]{3,0,2,1:T(8,128)S(1)}, u32[]{:S(2)}, u32[]{:S(2)}) collective-permute-start(f32[8,3,96,128]{3,0,2,1:T(8,128)S(1)} %copy.23), channel_id=1, source_target_pairs={{4,0},{8,4},{12,8},{16,12},{20,16},{24,20},{28,24},{5,1},{9,5},{13... | collective-permute-start | bytes 3538952 | tf_op jit(solution)/shard_map/ppermute | solution.py:618
  7.0 25.7 %collective-permute-start.1 = (f32[8,3,96,128]{3,0,2,1:T(8,128)}, f32[8,3,96,128]{3,0,2,1:T(8,128)S(1)}, u32[]{:S(2)}, u32[]{:S(2)}) collective-permute-start(f32[8,3,96,128]{3,0,2,1:T(8,128)} %copy.24), channel_id=1, source_target_pairs={{0,4},{4,8},{8,12},{12,16},{16,20},{20,24},{24,28},{1,5},{5,9},{9,... | collective-permute-start | bytes 3538952 | tf_op jit(solution)/shard_map/ppermute | solution.py:618
  32.7 23.5 %collective-permute-start.2 = (f32[8,30,3,128]{3,0,2,1:T(8,128)S(1)}, f32[8,30,3,128]{3,0,2,1:T(8,128)S(1)}, u32[]{:S(2)}, u32[]{:S(2)}) collective-permute-start(f32[8,30,3,128]{3,0,2,1:T(8,128)S(1)} %pad_maximum_fusion), channel_id=1, source_target_pairs={{1,0},{2,1},{3,2},{0,3},{5,4},{6,5},{7,6},{4,7},{9,8},{10,9},{11,1... | collective-permute-start | bytes 1105928 | tf_op jit(solution)/shard_map/ppermute | solution.py:618
  33.2 23.0 %collective-permute-start.3 = (f32[8,30,2,128]{3,0,2,1:T(8,128)S(1)}, f32[8,30,2,128]{3,0,2,1:T(8,128)S(1)}, u32[]{:S(2)}, u32[]{:S(2)}) collective-permute-start(f32[8,30,2,128]{3,0,2,1:T(8,128)S(1)} %pad_maximum_fusion.1), channel_id=1, source_target_pairs={{0,1},{1,2},{2,3},{3,0},{4,5},{5,6},{6,7},{7,4},{8,9},{9,10},{10,1... | collective-permute-start | bytes 737288 | tf_op jit(solution)/shard_map/ppermute | solution.py:618
  120.7 13.7 %collective-permute-start.4 = (f32[3,104,128]{2,1,0:T(8,128)S(1)}, f32[3,104,128]{2,1,0:T(8,128)S(1)}, u32[]{:S(2)}, u32[]{:S(2)}) collective-permute-start(f32[3,104,128]{2,1,0:T(8,128)S(1)} %get-tuple-element.45), channel_id=1, source_target_pairs={{0,4},{4,8},{8,12},{12,16},{16,20},{20,24},{24,28},{1,5},{5,9},{9,... | collective-permute-start | bytes 479240 | tf_op jit(solution)/shard_map/ppermute | solution.py:618
  122.6 11.7 %copy-start = (f32[30,104,128]{2,1,0:T(8,128)S(1)}, f32[30,104,128]{2,1,0:T(8,128)}, u32[]{:S(2)}) copy-start(f32[30,104,128]{2,1,0:T(8,128)} %parent_level.1) | copy-start | bytes 4792324
  122.6 11.7 %collective-permute-start.5 = (f32[3,104,128]{2,1,0:T(8,128)S(1)}, f32[3,104,128]{2,1,0:T(8,128)S(1)}, u32[]{:S(2)}, u32[]{:S(2)}) collective-permute-start(f32[3,104,128]{2,1,0:T(8,128)S(1)} %get-tuple-element.46), channel_id=1, source_target_pairs={{4,0},{8,4},{12,8},{16,12},{20,16},{24,20},{28,24},{5,1},{9,5},{13... | collective-permute-start | bytes 479240 | tf_op jit(solution)/shard_map/ppermute | solution.py:618
  134.5 5.8 %collective-permute-start.6 = (f32[24,3,128]{2,1,0:T(4,128)S(1)}, f32[24,3,128]{2,1,0:T(4,128)S(1)}, u32[]{:S(2)}, u32[]{:S(2)}) collective-permute-start(f32[24,3,128]{2,1,0:T(4,128)S(1)} %slice.57), channel_id=1, source_target_pairs={{0,1},{1,2},{2,3},{3,0},{4,5},{5,6},{6,7},{7,4},{8,9},{9,10},{10,1... | collective-permute-start | bytes 110600 | tf_op jit(solution)/shard_map/ppermute | solution.py:618
  134.6 5.7 %collective-permute-start.7 = (f32[24,2,128]{2,1,0:T(2,128)S(1)}, f32[24,2,128]{2,1,0:T(2,128)S(1)}, u32[]{:S(2)}, u32[]{:S(2)}) collective-permute-start(f32[24,2,128]{2,1,0:T(2,128)S(1)} %slice.58), channel_id=1, source_target_pairs={{1,0},{2,1},{3,2},{0,3},{5,4},{6,5},{7,6},{4,7},{9,8},{10,9},{11,1... | collective-permute-start | bytes 73736 | tf_op jit(solution)/shard_map/ppermute | solution.py:618

commit v5 on v4

--- a/solution.py
+++ b/solution.py
@@ -6,6 +6,7 @@
 import numpy as np
 from jax import lax
 from jax.experimental import pallas as pl
+from jax.experimental.layout import Layout, with_layout_constraint
 from jax.experimental.pallas import tpu as pltpu
 from jax.sharding import PartitionSpec as P
 
@@ -83,6 +84,7 @@
     out_ref, pattern, table = rest[-3:]
     groups, per = 4 // packed, 8 // packed
     tile = 16 * groups
+    pitch = tile + 8
     entries = source_ref.shape[0]
     step = pl.program_id(0)
 
@@ -92,7 +94,7 @@
             for part in range(2):
                 turned = table_ref[part, row * LANES : (row + 1) * LANES].T
                 for c in range(packed):
-                    table[pl.ds(part * 8 + c * per + row, LANES, stride=16), :] = turned
+                    table[part, pl.ds(c * per + row, LANES, stride=8), :] = turned
 
     @pl.when(step < 2)
     def _():
@@ -101,7 +103,7 @@
             plane, sub = (c, 0) if packed == 1 else (c // packed, c % packed * per)
             for part in range(2):
                 for row in range(rows):
-                    at = pl.ds((part * groups + plane) * 8 + sub + row, LANES, stride=tile)
+                    at = pl.ds((part * groups + plane) * 8 + sub + row, LANES, stride=pitch)
                     pattern[at, :] = child_ref[part, i, row * LANES : (row + 1) * LANES].T
 
     @pl.when(step >= 2)
@@ -112,9 +114,9 @@
             box = (step - 2) * half + i
             total = [None] * (2 * groups)
             for entry in range(entries):
-                x = pattern[pl.ds(pl.multiple_of(source_ref[entry, box] * tile, tile), tile), :]
-                factor = table[pl.ds(pl.multiple_of(kind_ref[entry, box] * 16, 16), 16), :]
-                real, imag = factor[:8], factor[8:]
+                x = pattern[pl.ds(pl.multiple_of(source_ref[entry, box] * pitch, 8), tile), :]
+                kind = pl.ds(pl.multiple_of(kind_ref[entry, box] * 8, 8), 8)
+                real, imag = table[0, kind, :], table[1, kind, :]
                 for g in range(groups):
                     xr, xi = x[g * 8 : g * 8 + 8], x[(groups + g) * 8 : (groups + g) * 8 + 8]
                     re = xr * real - xi * imag
@@ -152,7 +154,7 @@
         out_specs=pl.BlockSpec((1, LANES // 2 * tile, LANES), lambda s: (chunk, jnp.maximum(s - 2, 0), 0)),
         out_shape=jax.ShapeDtypeStruct((count, LANES * tile, LANES), F32),
         input_output_aliases=aliases,
-        scratch_shapes=[pltpu.VMEM((LANES * tile, LANES), F32), pltpu.VMEM((LANES * 16, LANES), F32)],
+        scratch_shapes=[pltpu.VMEM((LANES * (tile + 8), LANES), F32), pltpu.VMEM((2, LANES * 8, LANES), F32)],
         compiler_params=pltpu.CompilerParams(vmem_limit_bytes=60 * MIB),
         cost_estimate=pl.CostEstimate(
             flops=work * sources.shape[0] * 32, bytes_accessed=work * 72, transcendentals=0
@@ -165,6 +167,7 @@
     out_ref, lowered, total = rest[-3:]
     groups, per = 4 // packed, 8 // packed
     tile = 16 * groups
+    pitch = tile + 8
     step = pl.program_id(1)
 
     @pl.when(step == 0)
@@ -185,7 +188,7 @@
             for c in range(4):
                 real, imag = x[c * 8 : c * 8 + per], x[(4 + c) * 8 : (4 + c) * 8 + per]
                 at = c // packed * 8 + c % packed * per
-                here = pl.multiple_of((step * half + i) * tile, tile)
+                here = pl.multiple_of((step * half + i) * pitch, 8)
                 total[pl.ds(here + at, per), :] = local[at : at + per] + (real * cosine + imag * sine)
                 at += groups * 8
                 total[pl.ds(here + at, per), :] = local[at : at + per] + (imag * cosine - real * sine)
@@ -200,7 +203,7 @@
             plane, sub = (c, 0) if packed == 1 else (c // packed, c % packed * per)
             for part in range(2):
                 for row in range(rows):
-                    at = pl.ds((part * groups + plane) * 8 + sub + row, LANES, stride=tile)
+                    at = pl.ds((part * groups + plane) * 8 + sub + row, LANES, stride=pitch)
                     out_ref[part, i, row * LANES : (row + 1) * LANES] = total[at, :].T
 
 
@@ -227,7 +230,7 @@
         out_specs=pl.BlockSpec((2, 2, 8 * LANES, LANES), lambda i, s: (0, jnp.maximum(s - 2, 0), first + i, 0)),
         out_shape=jax.ShapeDtypeStruct(shape, F32),
         input_output_aliases=aliases,
-        scratch_shapes=[pltpu.VMEM((8 * LANES, LANES), F32), pltpu.VMEM((LANES * tile, LANES), F32)],
+        scratch_shapes=[pltpu.VMEM((8 * LANES, LANES), F32), pltpu.VMEM((LANES * (tile + 8), LANES), F32)],
         compiler_params=pltpu.CompilerParams(vmem_limit_bytes=60 * MIB),
         cost_estimate=pl.CostEstimate(flops=work * 32, bytes_accessed=work * 72, transcendentals=0),
         name="final_sum",
@@ -355,7 +358,8 @@
     lowered,
 ):
     (rows, columns, rows_up, columns_up, parents, entries, table_steps, table_rows) = sizes
-    t_pad, f_pad = wide.shape[1] // 128, wide.shape[2]
+    pitch, f_pad = wide.shape[1] // 128, wide.shape[2]
+    t_pad = pitch - 8
     p_pad, q_pad = phase_ref.shape[1], phase_ref.shape[2]
     row_tiles, lane_tiles = p_pad // 8, q_pad // LANES
     step = pl.program_id(0)
@@ -366,12 +370,12 @@
     def _():
         for part in range(2):
             for t in range(rows + 6, t_pad):
-                wide[part, pl.ds(t, 128, stride=t_pad), :] = jnp.zeros((128, f_pad), F32)
+                wide[part, pl.ds(t, 128, stride=pitch), :] = jnp.zeros((128, f_pad), F32)
         for part in range(2):
             for p in range(rows_up, p_pad):
                 for lane_tile in range(lane_tiles):
-                    at = pl.ds(part * 8 + p % 8, 128, stride=16)
-                    table_by_kind[lane_tile * row_tiles + p // 8, at, :] = jnp.zeros((128, LANES), F32)
+                    at = pl.ds(p % 8, 128, stride=8)
+                    table_by_kind[lane_tile * row_tiles + p // 8, part, at, :] = jnp.zeros((128, LANES), F32)
 
     combine = combine_ref[...]
 
@@ -388,7 +392,7 @@
                 both = jnp.concatenate([samples(part, *piece) for piece in pieces[i : i + 2]], axis=0)
                 turned = dot_transposed(combine, both)
                 for j, piece in enumerate(pieces[i : i + 2]):
-                    at = pl.ds(piece[2], 128, stride=t_pad)
+                    at = pl.ds(piece[2], 128, stride=pitch)
                     wide[part, at, :] = turned[:, j * f_pad : (j + 1) * f_pad]
 
     per_turn = next(n for n in (4, 3, 2, 1) if rows % n == 0)
@@ -407,8 +411,8 @@
                 for lane in range(0, q_pad, LANES):
                     turned = x[lane : lane + LANES].T
                     p = table_first + r
-                    at = pl.ds(part * 8 + p % 8, 128, stride=16)
-                    table_by_kind[lane // LANES * row_tiles + p // 8, at, :] = turned
+                    at = pl.ds(p % 8, 128, stride=8)
+                    table_by_kind[lane // LANES * row_tiles + p // 8, part, at, :] = turned
         return carry
 
     lax.fori_loop(0, turns, main_rows, 0)
@@ -430,10 +434,10 @@
                 for pair in range(parents // 2):
                     stacked = []
                     for source, offset in ((part, 0), (1 - part, half)):
-                        at = (offset + first + 2 * pair) * t_pad
+                        at = (offset + first + 2 * pair) * pitch
                         stacked.append(
                             jnp.concatenate(
-                                [wide[source, pl.ds(pl.multiple_of(at + i * t_pad, 8), t_pad), :] for i in range(2)],
+                                [wide[source, pl.ds(pl.multiple_of(at + i * pitch, 8), t_pad), :] for i in range(2)],
                                 axis=1,
                             )
                         )
@@ -474,7 +478,7 @@
             box = tile // (p_pad // 16)
             row_pair = tile % (p_pad // 16)
             sources = [pl.ds(pl.multiple_of(source_ref[box, e] * 64, 64), 64) for e in range(entries)]
-            kinds = [pl.ds(pl.multiple_of(kind_ref[box, e] * 16, 16), 16) for e in range(entries)]
+            kinds = [pl.ds(pl.multiple_of(kind_ref[box, e] * 8, 8), 8) for e in range(entries)]
             for lane_tile in range(lane_tiles):
                 halves = []
                 for i in range(2):
@@ -482,8 +486,7 @@
                     total = [None] * 8
                     for e in range(entries):
                         x = parent_out[where, sources[e], :]
-                        factor = table_by_kind[where, kinds[e], :]
-                        real, imag = factor[:8], factor[8:]
+                        real, imag = (table_by_kind[where, part, kinds[e], :] for part in range(2))
                         for c in range(4):
                             xr, xi = x[c * 8 : c * 8 + 8], x[(4 + c) * 8 : (4 + c) * 8 + 8]
                             re = xr * real - xi * imag
@@ -518,7 +521,7 @@
                 high, low = split(x)
                 z = dot(polar_back, jnp.concatenate([high, low, high], axis=0))
                 for j in range(2):
-                    lowered[pl.ds(pl.multiple_of(((i + j) * 8 + group) * t_pad, 8), t_pad), :] = z[
+                    lowered[pl.ds(pl.multiple_of(((i + j) * 8 + group) * pitch, 8), t_pad), :] = z[
                         :, j * f_pad : (j + 1) * f_pad
                     ]
             return carry
@@ -529,7 +532,7 @@
 
         def some_rows(i, carry):
             for r in range(per_turn):
-                turned = lowered[pl.ds(i * per_turn + r, 8 * parents, stride=t_pad), :].T
+                turned = lowered[pl.ds(i * per_turn + r, 8 * parents, stride=pitch), :].T
                 out_ref[i * per_turn + r] = turned[: columns + 8]
             return carry
 
@@ -583,13 +586,13 @@
         out_specs=pl.BlockSpec((rows + 6, columns + 8, 8 * parents), lambda g: (0, 0, 0)),
         out_shape=jax.ShapeDtypeStruct((rows + 6, columns + 8, 8 * parents), F32),
         scratch_shapes=[
-            pltpu.VMEM((2, 128 * t_pad, f_pad), F32),
+            pltpu.VMEM((2, 128 * (t_pad + 8), f_pad), F32),
             pltpu.VMEM((4, parents * p_pad, 3 * f_pad), BF16),
-            pltpu.VMEM((q_pad // LANES * (p_pad // 8), translators * 16, LANES), F32),
+            pltpu.VMEM((q_pad // LANES * (p_pad // 8), 2, translators * 8, LANES), F32),
             pltpu.VMEM((q_pad // LANES * (p_pad // 8), parents * 64, LANES), F32),
             pltpu.VMEM((8 * parents * p_pad, q_pad), BF16),
             pltpu.VMEM((8 * parents * p_pad, q_pad), BF16),
-            pltpu.VMEM((8 * parents * t_pad, f_pad), F32),
+            pltpu.VMEM((8 * parents * (t_pad + 8), f_pad), F32),
         ],
         compiler_params=pltpu.CompilerParams(vmem_limit_bytes=60 * MIB),
         cost_estimate=pl.CostEstimate(
@@ -616,6 +619,10 @@
 def send(block, axis, up):
     pairs = chain(lax.axis_size(axis), axis == "phi")
     return lax.ppermute(block, axis, pairs if up else [(b, a) for a, b in pairs])
+
+
+def plain(array):
+    return with_layout_constraint(array, Layout(major_to_minor=tuple(range(array.ndim))))
 
 
 def per_device(
@@ -656,8 +663,8 @@
                 child, flat_table, sources_child.T, kinds_child.T, pieces[n], i, local[n]
             )
 
-    after = send(child_out[:, :3], "theta", False)
-    before = send(child_out[:, rows - 3 :], "theta", True)
+    after = plain(send(plain(child_out[:, :3]), "theta", False))
+    before = plain(send(plain(child_out[:, rows - 3 :]), "theta", True))
     translate_next(flat_child)
     after, before, local = barrier((after, before, local))
 

time: 159 us -> 146 us (0.918)
  Pallas kernels: 118 us -> 107 us
  local copies, waits for them, and re-layouts: 11.7 us -> 8.56 us
  starting transfers between devices: 17.5 us -> 19.1 us
    pallas_call x1, Pallas kernels: 62 us -> 52.8 us  [parent_level(): pl.pallas_call(functools.partial(parent_kernel, (rows, columns, rows_up,...]
    optimization_barrier x2 -> x0, local copies, waits for them, and re-layouts: 2.56 us -> none  [per_device(): after, before, local = barrier((after, before, local))]
    unnamed x6, local copies, waits for them, and re-layouts: 2.64 us -> 0.25 us
    slice x6 -> x10, local copies, waits for them, and re-layouts: 2.42 us -> 4.26 us  [per_device(): edge[:, :, at]]
    pallas_call x2, Pallas kernels: 17.2 us -> 15.4 us  [final_sum(): pl.pallas_call(functools.partial(sum_kernel, packed, rows, LANES // 8), g...]
    ppermute x8, starting transfers between devices: 17.5 us -> 19.1 us  [send(): lax.ppermute(block, axis, pairs if up else [(b, a) for a, b in pairs])]
  transfers between devices with their start and end apart: 8 -> 8, of which waited for: 3 -> 3; matrix products, arithmetic and copies ran while one was open for 4% -> 2% of each run, Pallas kernels for 25% -> 27%
where the time goes in v5:
time: 146 us; the launch traced here: 145 us
  Pallas kernels  107 us (73%)
  starting transfers between devices  19.1 us (13%)
  waiting for transfers between devices  8.68 us (6%)
  local copies, waits for them, and re-layouts  8.56 us (6%)
  other arithmetic  1.59 us (1%)
    pallas_call x1, Pallas kernels, parent_level(): pl.pallas_call(functools.partial(parent_kernel, (rows, columns, rows_up,...  52.8 us
    pallas_call x3, Pallas kernels, child_translate(): pl.pallas_call(functools.partial(translate_kernel, packed, rows), grid=(4...  36.6 us
    ppermute x8, starting transfers between devices, send(): lax.ppermute(block, axis, pairs if up else [(b, a) for a, b in pairs])  19.1 us
    pallas_call x2, Pallas kernels, final_sum(): pl.pallas_call(functools.partial(sum_kernel, packed, rows, LANES // 8), g...  15.4 us
    ppermute x8, waiting for transfers between devices, send(): lax.ppermute(block, axis, pairs if up else [(b, a) for a, b in pairs])  8.68 us
    slice x10, local copies, waits for them, and re-layouts, per_device(): edge[:, :, at]  4.26 us
  transfers between devices with their start and end apart: 8, of which 3 were waited for; matrix products, arithmetic and copies ran while one was open for 2% of the time, Pallas kernels for 27%

profile of v5, /device:TPU:28, one launch (start us, length us, event | category | flops | bytes accessed | tf_op | source)
XLA Modules:
  0.0 144.7 jit_solution(14054356892599221605)
XLA Ops:
  0.0 1.8 %fusion.1 = (f32[8,3,96,128]{3,2,1,0:T(8,128)S(1)}, f32[8,3,96,128]{3,2,1,0:T(8,128)S(1)}) fusion(f32[8,24,96,128]{3,2,1,0:T(8,128)} %param.12), kind=kLoop, calls=%fused_computation.6 | loop fusion | bytes 4718592 | tf_op jit(solution)/shard_map/slice | solution.py:667
  1.8 1.9 %collective-permute-start.1 = (f32[8,3,96,128]{3,2,1,0:T(8,128)S(1)}, f32[8,3,96,128]{3,2,1,0:T(8,128)S(1)}, u32[]{:S(2)}, u32[]{:S(2)}) collective-permute-start(f32[8,3,96,128]{3,2,1,0:T(8,128)S(1)} %get-tuple-element.43), channel_id=1, source_target_pairs={{0,4},{4,8},{8,12},{12,16},{16,20},{20,24},{24,28},{1,5},{5,9},{9,... | collective-permute-start | bytes 3538952 | tf_op jit(solution)/shard_map/ppermute | solution.py:621
  3.7 4.5 %collective-permute-start = (f32[8,3,96,128]{3,2,1,0:T(8,128)S(1)}, f32[8,3,96,128]{3,2,1,0:T(8,128)}, u32[]{:S(2)}, u32[]{:S(2)}) collective-permute-start(f32[8,3,96,128]{3,2,1,0:T(8,128)S(1)} %get-tuple-element.44), channel_id=1, source_target_pairs={{4,0},{8,4},{12,8},{16,12},{20,16},{24,20},{28,24},{5,1},{9,5},{13... | collective-permute-start | bytes 3538952 | tf_op jit(solution)/shard_map/ppermute | solution.py:621
  8.3 1.2 slice.47
  9.5 1.2 slice.42
  10.7 0.1 copy.23
  10.8 0.2 copy.22
  11.0 15.0 %child_translate.3.rest_0_ = f32[2,8192,128]{2,1,0:T(8,128)} custom-call(s32[12,128]{1,0:T(8,128)} %bitcast.21, s32[12,128]{1,0:T(8,128)} %bitcast.24, f32[2,4,2304,128]{3,2,1,0:T(8,128)} %bitcast.11, f32[2,2304,128]{2,1,0:T(8,128)} %bitcast.15), custom_call_target="tpu_custom_call" | custom-call | flops 50331648 | bytes 9437184 | tf_op jit(solution)/shard_map/child_translate/pallas_call | solution.py:150
  25.9 4.1 %collective-permute-done.1 = f32[8,3,96,128]{3,2,1,0:T(8,128)S(1)} collective-permute-done((f32[8,3,96,128]{3,2,1,0:T(8,128)S(1)}, f32[8,3,96,128]{3,2,1,0:T(8,128)S(1)}, u32[]{:S(2)}, u32[]{:S(2)}) %collective-permute-start.1) | collective-permute-done | bytes 1179680 | tf_op jit(solution)/shard_map/ppermute | solution.py:621
  30.1 0.0 copy-start.1
  30.1 0.9 collective-permute-done
  31.0 0.9 slice.48
  31.9 0.9 slice.45
  32.9 0.5 collective-permute-start.2
  33.4 3.4 %collective-permute-start.3 = (f32[8,30,2,128]{3,0,2,1:T(8,128)S(1)}, f32[8,30,2,128]{3,0,2,1:T(8,128)S(1)}, u32[]{:S(2)}, u32[]{:S(2)}) collective-permute-start(f32[8,30,2,128]{3,0,2,1:T(8,128)S(1)} %pad_maximum_fusion.1), channel_id=1, source_target_pairs={{0,1},{1,2},{2,3},{3,0},{4,5},{5,6},{6,7},{7,4},{8,9},{9,10},{10,1... | collective-permute-start | bytes 737288 | tf_op jit(solution)/shard_map/ppermute | solution.py:621
  36.8 0.1 pad.22.clone
  36.9 1.8 %tables.1 = (bf16[128,256]{1,0:T(8,128)(2,1)}, f32[48,32]{1,0:T(8,128)}, f32[48,32]{1,0:T(8,128)}, f32[4,48,256]{2,1,0:T(8,128)}, f32[16,18,128]{2,1,0:T(8,128)}) custom-call(s32[1,128]{1,0:T(1,128)} %bitcast.27, f32[48,32]{1,0:T(8,128)} %constant.12.clone.polar_up_ref), custom_call_target="tpu_custom_call" | custom-call | tf_op jit(solution)/shard_map/tables/pallas_call | solution.py:321
  38.7 15.0 %child_translate.4.local_ref = f32[2,8192,128]{2,1,0:T(8,128)} custom-call(s32[12,128]{1,0:T(8,128)} %bitcast.22, s32[12,128]{1,0:T(8,128)} %bitcast.25, f32[2,4,2304,128]{3,2,1,0:T(8,128)} %bitcast.12, f32[2,2304,128]{2,1,0:T(8,128)} %bitcast.16, f32[2,8192,128]{2,1,0:T(8,128)} %child_translate.3.rest_0_), custom_call_target="tpu_custom_call", output_to_operand_aliasing={{}: (4, {})} | custom-call | flops 50331648 | bytes 9437184 | tf_op jit(solution)/shard_map/child_translate/pallas_call | solution.py:150
  53.6 0.0 copy-done.1
  53.6 0.0 collective-permute-done.3
  53.7 0.0 collective-permute-done.2
  53.7 0.2 maximum_maximum_fusion
  53.8 1.1 copy.21
  55.0 52.8 %parent_level.1 = f32[30,104,128]{2,1,0:T(8,128)} custom-call(s32[16,12]{1,0:T(8,128)} %source_ref.1, s32[16,12]{1,0:T(8,128)} %kind_ref.1, f32[2,4,24,96,128]{4,3,2,1,0:T(8,128)} %bitcast.13, f32[2,4,3,96,128]{4,3,2,1,0:T(8,128)} %bitcast.5.next_ref, f32[2,4,3,96,128]{4,3,2,1,0:T(8,128)} %bitcast.28, f32[2,4,30,8,128]{4,3,2,1,0:T(8,128)} %bitcast.20, ...), custom_call_target="tpu_custom_call" | custom-call | flops 20000000000 | bytes 18874368 | tf_op jit(solution)/shard_map/parent_level/pallas_call | solution.py:569
  107.8 1.0 fusion.2
  108.8 1.9 %collective-permute-start.4 = (f32[3,104,128]{2,1,0:T(8,128)S(1)}, f32[3,104,128]{2,1,0:T(8,128)S(1)}, u32[]{:S(2)}, u32[]{:S(2)}) collective-permute-start(f32[3,104,128]{2,1,0:T(8,128)S(1)} %get-tuple-element.45), channel_id=1, source_target_pairs={{0,4},{4,8},{8,12},{12,16},{16,20},{20,24},{24,28},{1,5},{5,9},{9,... | collective-permute-start | bytes 479240 | tf_op jit(solution)/shard_map/ppermute | solution.py:621
  110.8 0.0 copy-start
  110.8 4.7 %collective-permute-start.5 = (f32[3,104,128]{2,1,0:T(8,128)S(1)}, f32[3,104,128]{2,1,0:T(8,128)S(1)}, u32[]{:S(2)}, u32[]{:S(2)}) collective-permute-start(f32[3,104,128]{2,1,0:T(8,128)S(1)} %get-tuple-element.46), channel_id=1, source_target_pairs={{4,0},{8,4},{12,8},{16,12},{20,16},{24,20},{28,24},{5,1},{9,5},{13... | collective-permute-start | bytes 479240 | tf_op jit(solution)/shard_map/ppermute | solution.py:621
  115.4 6.7 %child_translate.5.local_ref = f32[1,2048,128]{2,1,0:T(8,128)} custom-call(s32[12,128]{1,0:T(8,128)} %bitcast.23, s32[12,128]{1,0:T(8,128)} %bitcast.26, f32[2,4,2304,128]{3,2,1,0:T(8,128)} %bitcast.14, f32[2,2304,128]{2,1,0:T(8,128)} %bitcast.17), custom_call_target="tpu_custom_call" | custom-call | flops 12582912 | bytes 2359296 | tf_op jit(solution)/shard_map/child_translate/pallas_call | solution.py:150
  122.1 0.0 collective-permute-done.4
  122.1 0.0 collective-permute-done.5
  122.1 0.0 copy-done
  122.1 0.1 pad_add_fusion
  122.3 0.1 collective-permute-start.6
  122.4 2.1 %collective-permute-start.7 = (f32[24,2,128]{2,1,0:T(2,128)S(1)}, f32[24,2,128]{2,1,0:T(2,128)S(1)}, u32[]{:S(2)}, u32[]{:S(2)}) collective-permute-start(f32[24,2,128]{2,1,0:T(2,128)S(1)} %slice.58), channel_id=1, source_target_pairs={{1,0},{2,1},{3,2},{0,3},{5,4},{6,5},{7,6},{4,7},{9,8},{10,9},{11,1... | collective-permute-start | bytes 73736 | tf_op jit(solution)/shard_map/ppermute | solution.py:621
  124.4 3.6 %collective-permute-done.7 = f32[24,2,128]{2,1,0:T(2,128)S(1)} collective-permute-done((f32[24,2,128]{2,1,0:T(2,128)S(1)}, f32[24,2,128]{2,1,0:T(2,128)S(1)}, u32[]{:S(2)}, u32[]{:S(2)}) %collective-permute-start.7) | collective-permute-done | bytes 24608 | tf_op jit(solution)/shard_map/ppermute | solution.py:621
  128.0 0.0 collective-permute-done.6
  128.0 1.3 fusion
  129.3 11.6 %final_sum.2.rest_0_ = f32[2,4,2304,128]{3,2,1,0:T(8,128)} custom-call(s32[128]{0:T(128)} %slot_ref.3, f32[2,8192,128]{2,1,0:T(8,128)} %child_translate.4.local_ref, f32[2304,128]{1,0:T(8,128)} %bitcast.18, f32[16,18,128]{2,1,0:T(8,128)} %get-tuple-element.41.phase_ref), custom_call_target="tpu_custom_call" | custom-call | flops 8388608 | bytes 18874368 | tf_op jit(solution)/shard_map/final_sum/pallas_call | solution.py:226
  140.9 3.9 %final_sum.3 = f32[2,4,2304,128]{3,2,1,0:T(8,128)} custom-call(s32[128]{0:T(128)} %slot_ref.3, f32[1,2048,128]{2,1,0:T(8,128)} %child_translate.5.local_ref, f32[2304,128]{1,0:T(8,128)} %bitcast.19, f32[16,18,128]{2,1,0:T(8,128)} %get-tuple-element.41.phase_ref, f32[2,4,2304,128]{3,2,1,0:T(8,128)} %final_sum.2.rest_0_), custom_call_target="tpu_custom_call", output_to_operand_aliasing={{}: (4, {})} | custom-call | flops 1048576 | bytes 2359296 | tf_op jit(solution)/shard_map/final_sum/pallas_call | solution.py:226
  (11 shorter events, 0.1 us)
Async XLA Ops:
  1.8 28.2 %collective-permute-start.1 = (f32[8,3,96,128]{3,2,1,0:T(8,128)S(1)}, f32[8,3,96,128]{3,2,1,0:T(8,128)S(1)}, u32[]{:S(2)}, u32[]{:S(2)}) collective-permute-start(f32[8,3,96,128]{3,2,1,0:T(8,128)S(1)} %get-tuple-element.43), channel_id=1, source_target_pairs={{0,4},{4,8},{8,12},{12,16},{16,20},{20,24},{24,28},{1,5},{5,9},{9,... | collective-permute-start | bytes 3538952 | tf_op jit(solution)/shard_map/ppermute | solution.py:621
  3.7 27.2 %collective-permute-start = (f32[8,3,96,128]{3,2,1,0:T(8,128)S(1)}, f32[8,3,96,128]{3,2,1,0:T(8,128)}, u32[]{:S(2)}, u32[]{:S(2)}) collective-permute-start(f32[8,3,96,128]{3,2,1,0:T(8,128)S(1)} %get-tuple-element.44), channel_id=1, source_target_pairs={{4,0},{8,4},{12,8},{16,12},{20,16},{24,20},{28,24},{5,1},{9,5},{13... | collective-permute-start | bytes 3538952 | tf_op jit(solution)/shard_map/ppermute | solution.py:621
  30.1 23.6 %copy-start.1 = (f32[8,3,96,128]{3,2,1,0:T(8,128)}, f32[8,3,96,128]{3,2,1,0:T(8,128)S(1)}, u32[]{:S(2)}) copy-start(f32[8,3,96,128]{3,2,1,0:T(8,128)S(1)} %collective-permute-done.1) | copy-start | bytes 3538948
  32.9 20.7 %collective-permute-start.2 = (f32[8,30,3,128]{3,0,2,1:T(8,128)S(1)}, f32[8,30,3,128]{3,0,2,1:T(8,128)S(1)}, u32[]{:S(2)}, u32[]{:S(2)}) collective-permute-start(f32[8,30,3,128]{3,0,2,1:T(8,128)S(1)} %pad_maximum_fusion), channel_id=1, source_target_pairs={{1,0},{2,1},{3,2},{0,3},{5,4},{6,5},{7,6},{4,7},{9,8},{10,9},{11,1... | collective-permute-start | bytes 1105928 | tf_op jit(solution)/shard_map/ppermute | solution.py:621
  33.4 20.2 %collective-permute-start.3 = (f32[8,30,2,128]{3,0,2,1:T(8,128)S(1)}, f32[8,30,2,128]{3,0,2,1:T(8,128)S(1)}, u32[]{:S(2)}, u32[]{:S(2)}) collective-permute-start(f32[8,30,2,128]{3,0,2,1:T(8,128)S(1)} %pad_maximum_fusion.1), channel_id=1, source_target_pairs={{0,1},{1,2},{2,3},{3,0},{4,5},{5,6},{6,7},{7,4},{8,9},{9,10},{10,1... | collective-permute-start | bytes 737288 | tf_op jit(solution)/shard_map/ppermute | solution.py:621
  108.8 13.3 %collective-permute-start.4 = (f32[3,104,128]{2,1,0:T(8,128)S(1)}, f32[3,104,128]{2,1,0:T(8,128)S(1)}, u32[]{:S(2)}, u32[]{:S(2)}) collective-permute-start(f32[3,104,128]{2,1,0:T(8,128)S(1)} %get-tuple-element.45), channel_id=1, source_target_pairs={{0,4},{4,8},{8,12},{12,16},{16,20},{20,24},{24,28},{1,5},{5,9},{9,... | collective-permute-start | bytes 479240 | tf_op jit(solution)/shard_map/ppermute | solution.py:621
  110.8 11.4 %copy-start = (f32[30,104,128]{2,1,0:T(8,128)S(1)}, f32[30,104,128]{2,1,0:T(8,128)}, u32[]{:S(2)}) copy-start(f32[30,104,128]{2,1,0:T(8,128)} %parent_level.1) | copy-start | bytes 4792324
  110.8 11.4 %collective-permute-start.5 = (f32[3,104,128]{2,1,0:T(8,128)S(1)}, f32[3,104,128]{2,1,0:T(8,128)S(1)}, u32[]{:S(2)}, u32[]{:S(2)}) collective-permute-start(f32[3,104,128]{2,1,0:T(8,128)S(1)} %get-tuple-element.46), channel_id=1, source_target_pairs={{4,0},{8,4},{12,8},{16,12},{20,16},{24,20},{28,24},{5,1},{9,5},{13... | collective-permute-start | bytes 479240 | tf_op jit(solution)/shard_map/ppermute | solution.py:621
  122.3 5.8 %collective-permute-start.6 = (f32[24,3,128]{2,1,0:T(4,128)S(1)}, f32[24,3,128]{2,1,0:T(4,128)S(1)}, u32[]{:S(2)}, u32[]{:S(2)}) collective-permute-start(f32[24,3,128]{2,1,0:T(4,128)S(1)} %slice.57), channel_id=1, source_target_pairs={{0,1},{1,2},{2,3},{3,0},{4,5},{5,6},{6,7},{7,4},{8,9},{9,10},{10,1... | collective-permute-start | bytes 110600 | tf_op jit(solution)/shard_map/ppermute | solution.py:621
  122.4 5.7 %collective-permute-start.7 = (f32[24,2,128]{2,1,0:T(2,128)S(1)}, f32[24,2,128]{2,1,0:T(2,128)S(1)}, u32[]{:S(2)}, u32[]{:S(2)}) collective-permute-start(f32[24,2,128]{2,1,0:T(2,128)S(1)} %slice.58), channel_id=1, source_target_pairs={{1,0},{2,1},{3,2},{0,3},{5,4},{6,5},{7,6},{4,7},{9,8},{10,9},{11,1... | collective-permute-start | bytes 73736 | tf_op jit(solution)/shard_map/ppermute | solution.py:621

commit v6 on v5

--- a/solution.py
+++ b/solution.py
@@ -164,7 +164,7 @@
 
 
 def sum_kernel(packed, rows, parents, slot_ref, local_ref, lowered_ref, phase_ref, *rest):
-    out_ref, lowered, total = rest[-3:]
+    out_ref, lowered, total, phase = rest[-4:]
     groups, per = 4 // packed, 8 // packed
     tile = 16 * groups
     pitch = tile + 8
@@ -173,7 +173,10 @@
     @pl.when(step == 0)
     def _():
         for row in range(rows):
-            lowered[pl.ds(row, LANES, stride=8), :] = lowered_ref[row * LANES : (row + 1) * LANES].T
+            lowered[pl.ds(row, LANES, stride=per), :] = lowered_ref[row * LANES : (row + 1) * LANES].T
+        for octant in range(8):
+            for part in range(2):
+                phase[2 * octant + part] = jnp.concatenate([phase_ref[8 * part + octant, :per]] * packed, axis=0)
 
     @pl.when(step < 2)
     def _():
@@ -182,16 +185,15 @@
         def one_box(i, carry):
             slot = slot_ref[step * half + i]
             octant = slot // parents
-            cosine, sine = phase_ref[octant][:per], phase_ref[8 + octant][:per]
-            x = lowered[pl.ds(pl.multiple_of(slot % parents * 64, 64), 64), :]
+            cosine, sine = phase[2 * octant], phase[2 * octant + 1]
+            x = lowered[pl.ds(pl.multiple_of(slot % parents * tile, tile), tile), :]
             local = local_ref[0, pl.ds(pl.multiple_of(i * tile, tile), tile), :]
-            for c in range(4):
-                real, imag = x[c * 8 : c * 8 + per], x[(4 + c) * 8 : (4 + c) * 8 + per]
-                at = c // packed * 8 + c % packed * per
-                here = pl.multiple_of((step * half + i) * pitch, 8)
-                total[pl.ds(here + at, per), :] = local[at : at + per] + (real * cosine + imag * sine)
-                at += groups * 8
-                total[pl.ds(here + at, per), :] = local[at : at + per] + (imag * cosine - real * sine)
+            here = pl.multiple_of((step * half + i) * pitch, 8)
+            for g in range(groups):
+                at, to = slice(g * 8, g * 8 + 8), slice((groups + g) * 8, (groups + g) * 8 + 8)
+                real, imag = x[at], x[to]
+                total[pl.ds(here + g * 8, 8), :] = local[at] + (real * cosine + imag * sine)
+                total[pl.ds(here + (groups + g) * 8, 8), :] = local[to] + (imag * cosine - real * sine)
             return carry
 
         lax.fori_loop(0, half, one_box, 0, unroll=4)
@@ -230,7 +232,11 @@
         out_specs=pl.BlockSpec((2, 2, 8 * LANES, LANES), lambda i, s: (0, jnp.maximum(s - 2, 0), first + i, 0)),
         out_shape=jax.ShapeDtypeStruct(shape, F32),
         input_output_aliases=aliases,
-        scratch_shapes=[pltpu.VMEM((8 * LANES, LANES), F32), pltpu.VMEM((LANES * (tile + 8), LANES), F32)],
+        scratch_shapes=[
+            pltpu.VMEM((LANES * (8 // packed), LANES), F32),
+            pltpu.VMEM((LANES * (tile + 8), LANES), F32),
+            pltpu.VMEM((16, 8, LANES), F32),
+        ],
         compiler_params=pltpu.CompilerParams(vmem_limit_bytes=60 * MIB),
         cost_estimate=pl.CostEstimate(flops=work * 32, bytes_accessed=work * 72, transcendentals=0),
         name="final_sum",
@@ -349,7 +355,8 @@
     azimuth_down_ref,
     phase_ref,
     out_ref,
-    wide,
+    wide_even,
+    wide_odd,
     rows_done,
     table_by_kind,
     parent_out,
@@ -358,7 +365,7 @@
     lowered,
 ):
     (rows, columns, rows_up, columns_up, parents, entries, table_steps, table_rows) = sizes
-    pitch, f_pad = wide.shape[1] // 128, wide.shape[2]
+    pitch, f_pad = wide_even.shape[1] // 128, wide_even.shape[2]
     t_pad = pitch - 8
     p_pad, q_pad = phase_ref.shape[1], phase_ref.shape[2]
     row_tiles, lane_tiles = p_pad // 8, q_pad // LANES
@@ -370,7 +377,8 @@
     def _():
         for part in range(2):
             for t in range(rows + 6, t_pad):
-                wide[part, pl.ds(t, 128, stride=pitch), :] = jnp.zeros((128, f_pad), F32)
+                for wide in (wide_even, wide_odd):
+                    wide[part, pl.ds(t, 128, stride=pitch), :] = jnp.zeros((128, f_pad), F32)
         for part in range(2):
             for p in range(rows_up, p_pad):
                 for lane_tile in range(lane_tiles):
@@ -386,93 +394,107 @@
         high, low = split(x)
         return jnp.concatenate([high, low], axis=1)
 
-    def turn(pieces):
+    def turn(rows_here, wide):
+        pieces = [(part,) + row for row in rows_here for part in range(2)]
+        for i in range(0, len(pieces), 2):
+            both = jnp.concatenate([samples(*piece) for piece in pieces[i : i + 2]], axis=0)
+            turned = dot_transposed(combine, both)
+            for j, piece in enumerate(pieces[i : i + 2]):
+                at = pl.ds(piece[3], 128, stride=pitch)
+                wide[piece[0], at, :] = turned[:, j * f_pad : (j + 1) * f_pad]
+
+    def turn_table(r):
+        p = table_first + r
+        at = pl.ds(p % 8, 128, stride=8)
         for part in range(2):
-            for i in range(0, len(pieces), 2):
-                both = jnp.concatenate([samples(part, *piece) for piece in pieces[i : i + 2]], axis=0)
-                turned = dot_transposed(combine, both)
-                for j, piece in enumerate(pieces[i : i + 2]):
-                    at = pl.ds(piece[2], 128, stride=pitch)
-                    wide[part, at, :] = turned[:, j * f_pad : (j + 1) * f_pad]
-
-    per_turn = next(n for n in (4, 3, 2, 1) if rows % n == 0)
-
-    turns = rows // per_turn
-    table_per_turn = -(-table_rows // turns)
-
-    def main_rows(i, carry):
-        turn([(child_ref, per_turn * i + r, per_turn * i + r) for r in range(per_turn)])
-        for j in range(table_per_turn):
-            r = jnp.minimum(i * table_per_turn + j, table_rows - 1)
-            for part in range(2):
-                x = table_ref[part, r]
-                if q_pad > columns_up:
-                    x = jnp.concatenate([x, jnp.zeros((q_pad - columns_up, LANES), F32)], axis=0)
-                for lane in range(0, q_pad, LANES):
-                    turned = x[lane : lane + LANES].T
-                    p = table_first + r
-                    at = pl.ds(p % 8, 128, stride=8)
-                    table_by_kind[lane // LANES * row_tiles + p // 8, part, at, :] = turned
-        return carry
-
-    lax.fori_loop(0, turns, main_rows, 0)
-    turn([(next_ref, r, rows + r) for r in range(3)] + [(previous_ref, r, rows + 3 + r) for r in range(3)])
-
-    polar = []
-    for sign in (-1.0, 1.0):
-        both = jnp.concatenate([polar_cos_ref[...], sign * polar_sin_ref[...]], axis=1)
-        high, low = split(both)
-        polar.append(jnp.concatenate([high, high, low], axis=1))
-    azimuth = azimuth_up_ref[...]
+            x = table_ref[part, r]
+            if q_pad > columns_up:
+                x = jnp.concatenate([x, jnp.zeros((q_pad - columns_up, LANES), F32)], axis=0)
+            for lane_tile in range(lane_tiles):
+                turned = x[lane_tile * LANES : (lane_tile + 1) * LANES].T
+                table_by_kind[lane_tile * row_tiles + p // 8, part, at, :] = turned
+
+    def shares(count):
+        pairs = -(-count // 2)
+        sizes_here = [(pairs + 3 - i) // 4 for i in range(4)]
+        return [(2 * sum(sizes_here[:i]), sizes_here[i]) for i in range(4)]
+
     per = 4
-    for target in range(2):
-        for difference in range(2):
-            part = target if difference == 0 else 1 - target
-
-            def one_kind(kind, carry, part=part, difference=difference):
-                first = (kind * 2 + difference) * parents
-                for pair in range(parents // 2):
-                    stacked = []
-                    for source, offset in ((part, 0), (1 - part, half)):
-                        at = (offset + first + 2 * pair) * pitch
-                        stacked.append(
-                            jnp.concatenate(
-                                [wide[source, pl.ds(pl.multiple_of(at + i * pitch, 8), t_pad), :] for i in range(2)],
-                                axis=1,
-                            )
-                        )
-                    high, low = split(jnp.concatenate(stacked, axis=0))
-                    result = dot(polar[part], jnp.concatenate([high, low, high], axis=0))
-                    high, low = split(result)
-                    for i in range(2):
-                        lanes = slice(i * f_pad, (i + 1) * f_pad)
-                        rows_done[kind * 2 + difference, pl.ds((2 * pair + i) * p_pad, p_pad), :] = jnp.concatenate(
-                            [high[:, lanes], low[:, lanes], high[:, lanes]], axis=1
-                        )
+
+    def channel(read, write):
+        if write is not None:
+            turn(
+                [(next_ref, r, rows + r) for r in range(3)] + [(previous_ref, r, rows + 3 + r) for r in range(3)],
+                write,
+            )
+        if read is not None:
+            polar = []
+            for sign in (-1.0, 1.0):
+                high, low = split(jnp.concatenate([polar_cos_ref[...], sign * polar_sin_ref[...]], axis=1))
+                polar.append(jnp.concatenate([high, high, low], axis=1))
+        for target in range(2):
+            for difference in range(2):
+                part = target if difference == 0 else 1 - target
+                loop = 2 * target + difference
+
+                def one_kind(kind, carry, part=part, difference=difference, loop=loop):
+                    if write is not None:
+                        first, count = shares(rows)[loop]
+                        here = [jnp.minimum(first + kind * count + j, rows - 1) for j in range(count)]
+                        turn([(child_ref, r, r) for r in here], write)
+                        first, count = shares(table_rows)[loop]
+                        for j in range(count):
+                            turn_table(jnp.minimum(first + kind * count + j, table_rows - 1))
+                    if read is not None:
+                        first = (kind * 2 + difference) * parents
+                        for pair in range(parents // 2):
+                            stacked = []
+                            for source, offset in ((part, 0), (1 - part, half)):
+                                at = (offset + first + 2 * pair) * pitch
+                                both = [
+                                    read[source, pl.ds(pl.multiple_of(at + i * pitch, 8), t_pad), :] for i in range(2)
+                                ]
+                                stacked.append(jnp.concatenate(both, axis=1))
+                            high, low = split(jnp.concatenate(stacked, axis=0))
+                            result = dot(polar[part], jnp.concatenate([high, low, high], axis=0))
+                            high, low = split(result)
+                            for i in range(2):
+                                lanes = slice(i * f_pad, (i + 1) * f_pad)
+                                rows_done[kind * 2 + difference, pl.ds((2 * pair + i) * p_pad, p_pad), :] = (
+                                    jnp.concatenate([high[:, lanes], low[:, lanes], high[:, lanes]], axis=1)
+                                )
+                    return carry
+
+                lax.fori_loop(0, 2, one_kind, 0)
+
+            if read is None:
+                continue
+
+            def one_group(group, carry, target=target):
+                at = pl.ds(pl.multiple_of(group * per * p_pad, 16), per * p_pad)
+                y = dot(jnp.concatenate([rows_done[k, at, :] for k in range(4)], axis=0), azimuth_up_ref[...])
+                for i in range(per):
+                    terms = [y[(k * per + i) * p_pad : (k * per + i + 1) * p_pad] * phase_ref[k] for k in range(4)]
+                    if target == 0:
+                        value = (terms[0] - terms[1]) + (terms[2] - terms[3])
+                    else:
+                        value = (terms[0] + terms[1]) + (terms[2] + terms[3])
+                    at = pl.ds(pl.multiple_of((group * per + i) * 64 + target * 32 + (step - 1) * 8, 8), 8)
+                    for lane_tile in range(lane_tiles):
+                        lanes = slice(lane_tile * LANES, (lane_tile + 1) * LANES)
+                        for row_tile in range(row_tiles):
+                            tile = value[row_tile * 8 : row_tile * 8 + 8, lanes]
+                            parent_out[lane_tile * row_tiles + row_tile, at, :] = tile
                 return carry
 
-            lax.fori_loop(0, 2, one_kind, 0)
-
-        def one_group(group, carry, target=target):
-            at = pl.ds(pl.multiple_of(group * per * p_pad, 16), per * p_pad)
-            y = dot(jnp.concatenate([rows_done[k, at, :] for k in range(4)], axis=0), azimuth)
-            for i in range(per):
-                terms = [y[(k * per + i) * p_pad : (k * per + i + 1) * p_pad] * phase_ref[k] for k in range(4)]
-                if target == 0:
-                    value = (terms[0] - terms[1]) + (terms[2] - terms[3])
-                else:
-                    value = (terms[0] + terms[1]) + (terms[2] + terms[3])
-                at = pl.ds(pl.multiple_of((group * per + i) * 64 + target * 32 + step * 8, 8), 8)
-                for lane_tile in range(lane_tiles):
-                    lanes = slice(lane_tile * LANES, (lane_tile + 1) * LANES)
-                    for row_tile in range(row_tiles):
-                        tile = value[row_tile * 8 : row_tile * 8 + 8, lanes]
-                        parent_out[lane_tile * row_tiles + row_tile, at, :] = tile
-            return carry
-
-        lax.fori_loop(0, parents // per, one_group, 0)
-
-    @pl.when(step == 3)
+            lax.fori_loop(0, parents // per, one_group, 0)
+
+    pl.when(step == 0)(lambda: channel(None, wide_even))
+    pl.when((step == 1) | (step == 3))(lambda: channel(wide_even, wide_odd))
+    pl.when(step == 2)(lambda: channel(wide_odd, wide_even))
+    pl.when(step == 4)(lambda: channel(wide_odd, None))
+
+    @pl.when(step == 4)
     def _():
         def one_tile(tile, carry):
             box = tile // (p_pad // 16)
@@ -562,7 +584,7 @@
         return pl.BlockSpec(array.shape, lambda g: (0,) * array.ndim)
 
     def channel(shape):
-        return pl.BlockSpec((2, 1) + shape, lambda g: (0, g, 0, 0, 0))
+        return pl.BlockSpec((2, 1) + shape, lambda g: (0, jnp.minimum(g, 3), 0, 0, 0))
 
     smem = pl.BlockSpec(memory_space=pltpu.SMEM)
     constants = [combine, polar_cos, polar_sin, azimuth_three, polar_down, azimuth_down, phase]
@@ -570,7 +592,7 @@
         functools.partial(
             parent_kernel, (rows, columns, rows_up, columns_up, parents, entries, table_steps, table_rows)
         ),
-        grid=(4,),
+        grid=(5,),
         in_specs=[
             smem,
             smem,
@@ -586,6 +608,7 @@
         out_specs=pl.BlockSpec((rows + 6, columns + 8, 8 * parents), lambda g: (0, 0, 0)),
         out_shape=jax.ShapeDtypeStruct((rows + 6, columns + 8, 8 * parents), F32),
         scratch_shapes=[
+            pltpu.VMEM((2, 128 * (t_pad + 8), f_pad), F32),
             pltpu.VMEM((2, 128 * (t_pad + 8), f_pad), F32),
             pltpu.VMEM((4, parents * p_pad, 3 * f_pad), BF16),
             pltpu.VMEM((q_pad // LANES * (p_pad // 8), 2, translators * 8, LANES), F32),
@@ -665,7 +688,9 @@
 
     after = plain(send(plain(child_out[:, :3]), "theta", False))
     before = plain(send(plain(child_out[:, rows - 3 :]), "theta", True))
-    translate_next(flat_child)
+    first_child, made = barrier((flat_child, (combine, polar_cos, polar_sin, phase, phase_child)))
+    combine, polar_cos, polar_sin, phase, phase_child = made
+    translate_next(first_child)
     after, before, local = barrier((after, before, local))
 
     low, high = (

time: 146 us -> 143 us (0.979)
  Pallas kernels: 107 us -> 105 us
  waiting for transfers between devices: 8.68 us -> 6.88 us
    ppermute x8, waiting for transfers between devices: 8.68 us -> 6.88 us  [send(): lax.ppermute(block, axis, pairs if up else [(b, a) for a, b in pairs])]
where the time goes in v6:
time: 143 us; the launch traced here: 142 us
  Pallas kernels  105 us (73%)
  starting transfers between devices  19.1 us (13%)
  local copies, waits for them, and re-layouts  8.56 us (6%)
  waiting for transfers between devices  6.88 us (5%)
  other arithmetic  1.59 us (1%)
    pallas_call x1, Pallas kernels, parent_level(): pl.pallas_call(functools.partial(parent_kernel, (rows, columns, rows_up,...  51.9 us
    pallas_call x3, Pallas kernels, child_translate(): pl.pallas_call(functools.partial(translate_kernel, packed, rows), grid=(4...  36.6 us
    ppermute x8, starting transfers between devices, send(): lax.ppermute(block, axis, pairs if up else [(b, a) for a, b in pairs])  19.1 us
    pallas_call x2, Pallas kernels, final_sum(): pl.pallas_call(functools.partial(sum_kernel, packed, rows, LANES // 8), g...  15.2 us
    ppermute x8, waiting for transfers between devices, send(): lax.ppermute(block, axis, pairs if up else [(b, a) for a, b in pairs])  6.88 us
    slice x10, local copies, waits for them, and re-layouts, per_device(): edge[:, :, at]  4.26 us
  transfers between devices with their start and end apart: 8, of which 3 were waited for; matrix products, arithmetic and copies ran while one was open for 2% of the time, Pallas kernels for 27%

profile of v6, /device:TPU:28, one launch (start us, length us, event | category | flops | bytes accessed | tf_op | source)
XLA Modules:
  0.0 141.8 jit_solution(707942409755549917)
XLA Ops:
  0.0 1.8 %fusion.1 = (f32[8,3,96,128]{3,2,1,0:T(8,128)S(1)}, f32[8,3,96,128]{3,2,1,0:T(8,128)S(1)}) fusion(f32[8,24,96,128]{3,2,1,0:T(8,128)} %param.12), kind=kLoop, calls=%fused_computation.6 | loop fusion | bytes 4718592 | tf_op jit(solution)/shard_map/slice | solution.py:690
  1.8 1.9 %collective-permute-start.1 = (f32[8,3,96,128]{3,2,1,0:T(8,128)S(1)}, f32[8,3,96,128]{3,2,1,0:T(8,128)S(1)}, u32[]{:S(2)}, u32[]{:S(2)}) collective-permute-start(f32[8,3,96,128]{3,2,1,0:T(8,128)S(1)} %get-tuple-element.55), channel_id=1, source_target_pairs={{0,4},{4,8},{8,12},{12,16},{16,20},{20,24},{24,28},{1,5},{5,9},{9,... | collective-permute-start | bytes 3538952 | tf_op jit(solution)/shard_map/ppermute | solution.py:644
  3.7 4.5 %collective-permute-start = (f32[8,3,96,128]{3,2,1,0:T(8,128)S(1)}, f32[8,3,96,128]{3,2,1,0:T(8,128)}, u32[]{:S(2)}, u32[]{:S(2)}) collective-permute-start(f32[8,3,96,128]{3,2,1,0:T(8,128)S(1)} %get-tuple-element.56), channel_id=1, source_target_pairs={{4,0},{8,4},{12,8},{16,12},{20,16},{24,20},{28,24},{5,1},{9,5},{13... | collective-permute-start | bytes 3538952 | tf_op jit(solution)/shard_map/ppermute | solution.py:644
  8.3 1.2 slice.47
  9.5 1.2 slice.42
  10.7 0.1 copy.23
  10.8 0.2 copy.22
  11.0 1.8 %tables.1 = (bf16[128,256]{1,0:T(8,128)(2,1)}, f32[48,32]{1,0:T(8,128)}, f32[48,32]{1,0:T(8,128)}, f32[4,48,256]{2,1,0:T(8,128)}, f32[16,18,128]{2,1,0:T(8,128)}) custom-call(s32[1,128]{1,0:T(1,128)} %bitcast.27, f32[48,32]{1,0:T(8,128)} %constant.12.clone.polar_up_ref), custom_call_target="tpu_custom_call" | custom-call | tf_op jit(solution)/shard_map/tables/pallas_call | solution.py:327
  12.8 15.0 %child_translate.3.rest_0_ = f32[2,8192,128]{2,1,0:T(8,128)} custom-call(s32[12,128]{1,0:T(8,128)} %bitcast.21, s32[12,128]{1,0:T(8,128)} %bitcast.24, f32[2,4,2304,128]{3,2,1,0:T(8,128)} %bitcast.11, f32[2,2304,128]{2,1,0:T(8,128)} %bitcast.15), custom_call_target="tpu_custom_call" | custom-call | flops 50331648 | bytes 9437184 | tf_op jit(solution)/shard_map/child_translate/pallas_call | solution.py:150
  27.7 2.3 %collective-permute-done.1 = f32[8,3,96,128]{3,2,1,0:T(8,128)S(1)} collective-permute-done((f32[8,3,96,128]{3,2,1,0:T(8,128)S(1)}, f32[8,3,96,128]{3,2,1,0:T(8,128)S(1)}, u32[]{:S(2)}, u32[]{:S(2)}) %collective-permute-start.1) | collective-permute-done | bytes 1179680 | tf_op jit(solution)/shard_map/ppermute | solution.py:644
  30.1 0.0 copy-start.1
  30.1 0.9 collective-permute-done
  31.0 0.9 slice.48
  31.9 0.9 slice.45
  32.9 0.5 collective-permute-start.2
  33.4 3.4 %collective-permute-start.3 = (f32[8,30,2,128]{3,0,2,1:T(8,128)S(1)}, f32[8,30,2,128]{3,0,2,1:T(8,128)S(1)}, u32[]{:S(2)}, u32[]{:S(2)}) collective-permute-start(f32[8,30,2,128]{3,0,2,1:T(8,128)S(1)} %pad_maximum_fusion.1), channel_id=1, source_target_pairs={{0,1},{1,2},{2,3},{3,0},{4,5},{5,6},{6,7},{7,4},{8,9},{9,10},{10,1... | collective-permute-start | bytes 737288 | tf_op jit(solution)/shard_map/ppermute | solution.py:644
  36.8 0.1 pad.22.clone
  36.9 15.0 %child_translate.4.local_ref = f32[2,8192,128]{2,1,0:T(8,128)} custom-call(s32[12,128]{1,0:T(8,128)} %bitcast.22, s32[12,128]{1,0:T(8,128)} %bitcast.25, f32[2,4,2304,128]{3,2,1,0:T(8,128)} %bitcast.12, f32[2,2304,128]{2,1,0:T(8,128)} %bitcast.16, f32[2,8192,128]{2,1,0:T(8,128)} %child_translate.3.rest_0_), custom_call_target="tpu_custom_call", output_to_operand_aliasing={{}: (4, {})} | custom-call | flops 50331648 | bytes 9437184 | tf_op jit(solution)/shard_map/child_translate/pallas_call | solution.py:150
  51.9 0.0 copy-done.1
  51.9 0.0 collective-permute-done.3
  51.9 0.0 collective-permute-done.2
  51.9 0.2 maximum_maximum_fusion
  52.1 1.1 copy.21
  53.2 51.9 %parent_level.1 = f32[30,104,128]{2,1,0:T(8,128)} custom-call(s32[16,12]{1,0:T(8,128)} %source_ref.1, s32[16,12]{1,0:T(8,128)} %kind_ref.1, f32[2,4,24,96,128]{4,3,2,1,0:T(8,128)} %bitcast.13, f32[2,4,3,96,128]{4,3,2,1,0:T(8,128)} %bitcast.6.next_ref, f32[2,4,3,96,128]{4,3,2,1,0:T(8,128)} %bitcast.28, f32[2,4,30,8,128]{4,3,2,1,0:T(8,128)} %bitcast.20, ...), custom_call_target="tpu_custom_call" | custom-call | flops 20000000000 | bytes 18874368 | tf_op jit(solution)/shard_map/parent_level/pallas_call | solution.py:591
  105.1 1.0 fusion.2
  106.1 1.9 %collective-permute-start.4 = (f32[3,104,128]{2,1,0:T(8,128)S(1)}, f32[3,104,128]{2,1,0:T(8,128)S(1)}, u32[]{:S(2)}, u32[]{:S(2)}) collective-permute-start(f32[3,104,128]{2,1,0:T(8,128)S(1)} %get-tuple-element.57), channel_id=1, source_target_pairs={{0,4},{4,8},{8,12},{12,16},{16,20},{20,24},{24,28},{1,5},{5,9},{9,... | collective-permute-start | bytes 479240 | tf_op jit(solution)/shard_map/ppermute | solution.py:644
  108.0 0.0 copy-start
  108.0 4.7 %collective-permute-start.5 = (f32[3,104,128]{2,1,0:T(8,128)S(1)}, f32[3,104,128]{2,1,0:T(8,128)S(1)}, u32[]{:S(2)}, u32[]{:S(2)}) collective-permute-start(f32[3,104,128]{2,1,0:T(8,128)S(1)} %get-tuple-element.58), channel_id=1, source_target_pairs={{4,0},{8,4},{12,8},{16,12},{20,16},{24,20},{28,24},{5,1},{9,5},{13... | collective-permute-start | bytes 479240 | tf_op jit(solution)/shard_map/ppermute | solution.py:644
  112.7 6.7 %child_translate.5.local_ref = f32[1,2048,128]{2,1,0:T(8,128)} custom-call(s32[12,128]{1,0:T(8,128)} %bitcast.23, s32[12,128]{1,0:T(8,128)} %bitcast.26, f32[2,4,2304,128]{3,2,1,0:T(8,128)} %bitcast.14, f32[2,2304,128]{2,1,0:T(8,128)} %bitcast.17), custom_call_target="tpu_custom_call" | custom-call | flops 12582912 | bytes 2359296 | tf_op jit(solution)/shard_map/child_translate/pallas_call | solution.py:150
  119.4 0.0 collective-permute-done.4
  119.4 0.0 collective-permute-done.5
  119.4 0.0 copy-done
  119.4 0.1 pad_add_fusion
  119.5 0.1 collective-permute-start.6
  119.6 2.1 %collective-permute-start.7 = (f32[24,2,128]{2,1,0:T(2,128)S(1)}, f32[24,2,128]{2,1,0:T(2,128)S(1)}, u32[]{:S(2)}, u32[]{:S(2)}) collective-permute-start(f32[24,2,128]{2,1,0:T(2,128)S(1)} %slice.58), channel_id=1, source_target_pairs={{1,0},{2,1},{3,2},{0,3},{5,4},{6,5},{7,6},{4,7},{9,8},{10,9},{11,1... | collective-permute-start | bytes 73736 | tf_op jit(solution)/shard_map/ppermute | solution.py:644
  121.7 3.6 %collective-permute-done.7 = f32[24,2,128]{2,1,0:T(2,128)S(1)} collective-permute-done((f32[24,2,128]{2,1,0:T(2,128)S(1)}, f32[24,2,128]{2,1,0:T(2,128)S(1)}, u32[]{:S(2)}, u32[]{:S(2)}) %collective-permute-start.7) | collective-permute-done | bytes 24608 | tf_op jit(solution)/shard_map/ppermute | solution.py:644
  125.3 0.0 collective-permute-done.6
  125.3 1.3 fusion
  126.6 11.5 %final_sum.2.rest_0_ = f32[2,4,2304,128]{3,2,1,0:T(8,128)} custom-call(s32[128]{0:T(128)} %slot_ref.3, f32[2,8192,128]{2,1,0:T(8,128)} %child_translate.4.local_ref, f32[2304,128]{1,0:T(8,128)} %bitcast.18, f32[16,18,128]{2,1,0:T(8,128)} %get-tuple-element.53.phase_ref), custom_call_target="tpu_custom_call" | custom-call | flops 8388608 | bytes 18874368 | tf_op jit(solution)/shard_map/final_sum/pallas_call | solution.py:228
  138.1 3.7 %final_sum.3 = f32[2,4,2304,128]{3,2,1,0:T(8,128)} custom-call(s32[128]{0:T(128)} %slot_ref.3, f32[1,2048,128]{2,1,0:T(8,128)} %child_translate.5.local_ref, f32[2304,128]{1,0:T(8,128)} %bitcast.19, f32[16,18,128]{2,1,0:T(8,128)} %get-tuple-element.53.phase_ref, f32[2,4,2304,128]{3,2,1,0:T(8,128)} %final_sum.2.rest_0_), custom_call_target="tpu_custom_call", output_to_operand_aliasing={{}: (4, {})} | custom-call | flops 1048576 | bytes 2359296 | tf_op jit(solution)/shard_map/final_sum/pallas_call | solution.py:228
  (11 shorter events, 0.1 us)
Async XLA Ops:
  1.8 28.2 %collective-permute-start.1 = (f32[8,3,96,128]{3,2,1,0:T(8,128)S(1)}, f32[8,3,96,128]{3,2,1,0:T(8,128)S(1)}, u32[]{:S(2)}, u32[]{:S(2)}) collective-permute-start(f32[8,3,96,128]{3,2,1,0:T(8,128)S(1)} %get-tuple-element.55), channel_id=1, source_target_pairs={{0,4},{4,8},{8,12},{12,16},{16,20},{20,24},{24,28},{1,5},{5,9},{9,... | collective-permute-start | bytes 3538952 | tf_op jit(solution)/shard_map/ppermute | solution.py:644
  3.7 27.2 %collective-permute-start = (f32[8,3,96,128]{3,2,1,0:T(8,128)S(1)}, f32[8,3,96,128]{3,2,1,0:T(8,128)}, u32[]{:S(2)}, u32[]{:S(2)}) collective-permute-start(f32[8,3,96,128]{3,2,1,0:T(8,128)S(1)} %get-tuple-element.56), channel_id=1, source_target_pairs={{4,0},{8,4},{12,8},{16,12},{20,16},{24,20},{28,24},{5,1},{9,5},{13... | collective-permute-start | bytes 3538952 | tf_op jit(solution)/shard_map/ppermute | solution.py:644
  30.1 21.8 %copy-start.1 = (f32[8,3,96,128]{3,2,1,0:T(8,128)}, f32[8,3,96,128]{3,2,1,0:T(8,128)S(1)}, u32[]{:S(2)}) copy-start(f32[8,3,96,128]{3,2,1,0:T(8,128)S(1)} %collective-permute-done.1) | copy-start | bytes 3538948
  32.9 19.0 %collective-permute-start.2 = (f32[8,30,3,128]{3,0,2,1:T(8,128)S(1)}, f32[8,30,3,128]{3,0,2,1:T(8,128)S(1)}, u32[]{:S(2)}, u32[]{:S(2)}) collective-permute-start(f32[8,30,3,128]{3,0,2,1:T(8,128)S(1)} %pad_maximum_fusion), channel_id=1, source_target_pairs={{1,0},{2,1},{3,2},{0,3},{5,4},{6,5},{7,6},{4,7},{9,8},{10,9},{11,1... | collective-permute-start | bytes 1105928 | tf_op jit(solution)/shard_map/ppermute | solution.py:644
  33.4 18.5 %collective-permute-start.3 = (f32[8,30,2,128]{3,0,2,1:T(8,128)S(1)}, f32[8,30,2,128]{3,0,2,1:T(8,128)S(1)}, u32[]{:S(2)}, u32[]{:S(2)}) collective-permute-start(f32[8,30,2,128]{3,0,2,1:T(8,128)S(1)} %pad_maximum_fusion.1), channel_id=1, source_target_pairs={{0,1},{1,2},{2,3},{3,0},{4,5},{5,6},{6,7},{7,4},{8,9},{9,10},{10,1... | collective-permute-start | bytes 737288 | tf_op jit(solution)/shard_map/ppermute | solution.py:644
  106.1 13.3 %collective-permute-start.4 = (f32[3,104,128]{2,1,0:T(8,128)S(1)}, f32[3,104,128]{2,1,0:T(8,128)S(1)}, u32[]{:S(2)}, u32[]{:S(2)}) collective-permute-start(f32[3,104,128]{2,1,0:T(8,128)S(1)} %get-tuple-element.57), channel_id=1, source_target_pairs={{0,4},{4,8},{8,12},{12,16},{16,20},{20,24},{24,28},{1,5},{5,9},{9,... | collective-permute-start | bytes 479240 | tf_op jit(solution)/shard_map/ppermute | solution.py:644
  108.0 11.4 %copy-start = (f32[30,104,128]{2,1,0:T(8,128)S(1)}, f32[30,104,128]{2,1,0:T(8,128)}, u32[]{:S(2)}) copy-start(f32[30,104,128]{2,1,0:T(8,128)} %parent_level.1) | copy-start | bytes 4792324
  108.0 11.4 %collective-permute-start.5 = (f32[3,104,128]{2,1,0:T(8,128)S(1)}, f32[3,104,128]{2,1,0:T(8,128)S(1)}, u32[]{:S(2)}, u32[]{:S(2)}) collective-permute-start(f32[3,104,128]{2,1,0:T(8,128)S(1)} %get-tuple-element.58), channel_id=1, source_target_pairs={{4,0},{8,4},{12,8},{16,12},{20,16},{24,20},{28,24},{5,1},{9,5},{13... | collective-permute-start | bytes 479240 | tf_op jit(solution)/shard_map/ppermute | solution.py:644
  119.5 5.8 %collective-permute-start.6 = (f32[24,3,128]{2,1,0:T(4,128)S(1)}, f32[24,3,128]{2,1,0:T(4,128)S(1)}, u32[]{:S(2)}, u32[]{:S(2)}) collective-permute-start(f32[24,3,128]{2,1,0:T(4,128)S(1)} %slice.57), channel_id=1, source_target_pairs={{0,1},{1,2},{2,3},{3,0},{4,5},{5,6},{6,7},{7,4},{8,9},{9,10},{10,1... | collective-permute-start | bytes 110600 | tf_op jit(solution)/shard_map/ppermute | solution.py:644
  119.6 5.7 %collective-permute-start.7 = (f32[24,2,128]{2,1,0:T(2,128)S(1)}, f32[24,2,128]{2,1,0:T(2,128)S(1)}, u32[]{:S(2)}, u32[]{:S(2)}) collective-permute-start(f32[24,2,128]{2,1,0:T(2,128)S(1)} %slice.58), channel_id=1, source_target_pairs={{1,0},{2,1},{3,2},{0,3},{5,4},{6,5},{7,6},{4,7},{9,8},{10,9},{11,1... | collective-permute-start | bytes 73736 | tf_op jit(solution)/shard_map/ppermute | solution.py:644

commit v7 on v6

--- a/solution.py
+++ b/solution.py
@@ -91,8 +91,8 @@
     @pl.when(step == 0)
     def _():
         for row in range(rows):
-            for part in range(2):
-                turned = table_ref[part, row * LANES : (row + 1) * LANES].T
+            real, imag = (table_ref[part, row * LANES : (row + 1) * LANES].T for part in range(2))
+            for part, turned in enumerate((real, imag - real, real + imag)):
                 for c in range(packed):
                     table[part, pl.ds(c * per + row, LANES, stride=8), :] = turned
 
@@ -112,17 +112,18 @@
 
         def one_box(i, carry):
             box = (step - 2) * half + i
-            total = [None] * (2 * groups)
+            sums = [[None] * groups for _ in range(3)]
             for entry in range(entries):
                 x = pattern[pl.ds(pl.multiple_of(source_ref[entry, box] * pitch, 8), tile), :]
                 kind = pl.ds(pl.multiple_of(kind_ref[entry, box] * 8, 8), 8)
-                real, imag = table[0, kind, :], table[1, kind, :]
+                factors = [table[part, kind, :] for part in range(3)]
                 for g in range(groups):
                     xr, xi = x[g * 8 : g * 8 + 8], x[(groups + g) * 8 : (groups + g) * 8 + 8]
-                    re = xr * real - xi * imag
-                    im = xr * imag + xi * real
-                    total[g] = re if entry == 0 else total[g] + re
-                    total[groups + g] = im if entry == 0 else total[groups + g] + im
+                    for part, term in enumerate((xr + xi, xr, xi)):
+                        product = term * factors[part]
+                        sums[part][g] = product if entry == 0 else sums[part][g] + product
+            total = [sums[0][g] - sums[2][g] for g in range(groups)]
+            total += [sums[0][g] + sums[1][g] for g in range(groups)]
             for g in range(2 * groups):
                 out_ref[0, pl.ds(pl.multiple_of(i * tile, tile) + g * 8, 8), :] = total[g]
             return carry
@@ -154,7 +155,7 @@
         out_specs=pl.BlockSpec((1, LANES // 2 * tile, LANES), lambda s: (chunk, jnp.maximum(s - 2, 0), 0)),
         out_shape=jax.ShapeDtypeStruct((count, LANES * tile, LANES), F32),
         input_output_aliases=aliases,
-        scratch_shapes=[pltpu.VMEM((LANES * (tile + 8), LANES), F32), pltpu.VMEM((2, LANES * 8, LANES), F32)],
+        scratch_shapes=[pltpu.VMEM((LANES * (tile + 8), LANES), F32), pltpu.VMEM((3, LANES * 8, LANES), F32)],
         compiler_params=pltpu.CompilerParams(vmem_limit_bytes=60 * MIB),
         cost_estimate=pl.CostEstimate(
             flops=work * sources.shape[0] * 32, bytes_accessed=work * 72, transcendentals=0
@@ -184,9 +185,9 @@
 
         def one_box(i, carry):
             slot = slot_ref[step * half + i]
-            octant = slot // parents
+            octant = slot >> (parents.bit_length() - 1)
             cosine, sine = phase[2 * octant], phase[2 * octant + 1]
-            x = lowered[pl.ds(pl.multiple_of(slot % parents * tile, tile), tile), :]
+            x = lowered[pl.ds(pl.multiple_of((slot & (parents - 1)) * tile, tile), tile), :]
             local = local_ref[0, pl.ds(pl.multiple_of(i * tile, tile), tile), :]
             here = pl.multiple_of((step * half + i) * pitch, 8)
             for g in range(groups):
@@ -405,14 +406,14 @@
 
     def turn_table(r):
         p = table_first + r
-        at = pl.ds(p % 8, 128, stride=8)
+        at = pl.ds(p & 7, 128, stride=8)
         for part in range(2):
             x = table_ref[part, r]
             if q_pad > columns_up:
                 x = jnp.concatenate([x, jnp.zeros((q_pad - columns_up, LANES), F32)], axis=0)
             for lane_tile in range(lane_tiles):
                 turned = x[lane_tile * LANES : (lane_tile + 1) * LANES].T
-                table_by_kind[lane_tile * row_tiles + p // 8, part, at, :] = turned
+                table_by_kind[lane_tile * row_tiles + (p >> 3), part, at, :] = turned
 
     def shares(count):
         pairs = -(-count // 2)
@@ -679,9 +680,9 @@
     local = [None] * len(pieces)
     chunks = [(n, i) for n, piece in enumerate(pieces) for i in range(piece[1])]
 
-    def translate_next(child):
+    def translate_next(child, last=False):
         if chunks:
-            n, i = chunks.pop(0)
+            n, i = chunks.pop(-1 if last else 0)
             local[n] = child_translate(
                 child, flat_table, sources_child.T, kinds_child.T, pieces[n], i, local[n]
             )
@@ -691,6 +692,8 @@
     first_child, made = barrier((flat_child, (combine, polar_cos, polar_sin, phase, phase_child)))
     combine, polar_cos, polar_sin, phase, phase_child = made
     translate_next(first_child)
+    if len(chunks) > 1:
+        translate_next(first_child, last=True)
     after, before, local = barrier((after, before, local))
 
     low, high = (
@@ -700,8 +703,7 @@
     low, high, later_child = barrier((low, high, flat_child))
     right = send(low, "phi", False)
     left = send(high, "phi", True)
-    if len(chunks) > 1:
-        translate_next(later_child)
+    translate_next(later_child)
     right, left, local = barrier((right, left, local))
     side = jnp.concatenate([right, left, jnp.zeros((8, rows + 6, 3, boxes), F32)], axis=2)
 

time: 143 us -> 141 us (0.986)
  Pallas kernels: 105 us -> 101 us
  waiting for transfers between devices: 6.88 us -> 10.2 us
  starting transfers between devices: 19.1 us -> 15.9 us
  local copies, waits for them, and re-layouts: 8.56 us -> 10.3 us
    ppermute x8, waiting for transfers between devices: 6.88 us -> 10.2 us  [send(): lax.ppermute(block, axis, pairs if up else [(b, a) for a, b in pairs])]
    ppermute x8, starting transfers between devices: 19.1 us -> 15.9 us  [send(): lax.ppermute(block, axis, pairs if up else [(b, a) for a, b in pairs])]
    pallas_call x3, Pallas kernels: 36.6 us -> 33.9 us  [child_translate(): pl.pallas_call(functools.partial(translate_kernel, packed, rows), grid=(4...]
    slice x10, local copies, waits for them, and re-layouts: 4.26 us -> 6.03 us  [per_device(): edge[:, :, at]]
  transfers between devices with their start and end apart: 8 -> 8, of which waited for: 3 -> 4; matrix products, arithmetic and copies ran while one was open for 2% -> 2% of each run, Pallas kernels for 27% -> 25%
where the time goes in v7:
time: 141 us
  Pallas kernels  101 us (72%)
  starting transfers between devices  15.9 us (11%)
  local copies, waits for them, and re-layouts  10.3 us (7%)
  waiting for transfers between devices  10.2 us (7%)
  other arithmetic  2.86 us (2%)
    pallas_call x1, Pallas kernels, parent_level(): pl.pallas_call(functools.partial(parent_kernel, (rows, columns, rows_up,...  51.7 us
    pallas_call x3, Pallas kernels, child_translate(): pl.pallas_call(functools.partial(translate_kernel, packed, rows), grid=(4...  33.9 us
    ppermute x8, starting transfers between devices, send(): lax.ppermute(block, axis, pairs if up else [(b, a) for a, b in pairs])  15.9 us
    pallas_call x2, Pallas kernels, final_sum(): pl.pallas_call(functools.partial(sum_kernel, packed, rows, LANES // 8), g...  13.9 us
    ppermute x8, waiting for transfers between devices, send(): lax.ppermute(block, axis, pairs if up else [(b, a) for a, b in pairs])  10.2 us
    slice x10, local copies, waits for them, and re-layouts, per_device(): edge[:, :, at]  6.03 us
  transfers between devices with their start and end apart: 8, of which 4 were waited for; matrix products, arithmetic and copies ran while one was open for 2% of the time, Pallas kernels for 25%

profile of v7, /device:TPU:28, one launch (start us, length us, event | category | flops | bytes accessed | tf_op | source)
XLA Modules:
  0.0 140.8 jit_solution(6803806804732772593)
XLA Ops:
  0.0 1.8 %fusion.1 = (f32[8,3,96,128]{3,2,1,0:T(8,128)S(1)}, f32[8,3,96,128]{3,2,1,0:T(8,128)S(1)}) fusion(f32[8,24,96,128]{3,2,1,0:T(8,128)} %param.12), kind=kLoop, calls=%fused_computation.6 | loop fusion | bytes 4718592 | tf_op jit(solution)/shard_map/slice | solution.py:691
  1.8 2.8 %collective-permute-start = (f32[8,3,96,128]{3,2,1,0:T(8,128)S(1)}, f32[8,3,96,128]{3,2,1,0:T(8,128)}, u32[]{:S(2)}, u32[]{:S(2)}) collective-permute-start(f32[8,3,96,128]{3,2,1,0:T(8,128)S(1)} %get-tuple-element.58), channel_id=1, source_target_pairs={{4,0},{8,4},{12,8},{16,12},{20,16},{24,20},{28,24},{5,1},{9,5},{13... | collective-permute-start | bytes 3538952 | tf_op jit(solution)/shard_map/ppermute | solution.py:645
  4.6 1.9 %collective-permute-start.1 = (f32[8,3,96,128]{3,2,1,0:T(8,128)S(1)}, f32[8,3,96,128]{3,2,1,0:T(8,128)}, u32[]{:S(2)}, u32[]{:S(2)}) collective-permute-start(f32[8,3,96,128]{3,2,1,0:T(8,128)S(1)} %get-tuple-element.57), channel_id=1, source_target_pairs={{0,4},{4,8},{8,12},{12,16},{16,20},{20,24},{24,28},{1,5},{5,9},{9,... | collective-permute-start | bytes 3538952 | tf_op jit(solution)/shard_map/ppermute | solution.py:645
  6.5 1.2 slice.42
  7.7 1.2 slice.47
  8.9 1.8 %tables.1 = (bf16[128,256]{1,0:T(8,128)(2,1)}, f32[48,32]{1,0:T(8,128)}, f32[48,32]{1,0:T(8,128)}, f32[4,48,256]{2,1,0:T(8,128)}, f32[16,18,128]{2,1,0:T(8,128)}) custom-call(s32[1,128]{1,0:T(1,128)} %bitcast.27, f32[48,32]{1,0:T(8,128)} %constant.12.clone.polar_up_ref), custom_call_target="tpu_custom_call" | custom-call | tf_op jit(solution)/shard_map/tables/pallas_call | solution.py:328
  10.8 0.2 copy.22
  11.0 0.1 copy.23
  11.0 6.8 %child_translate.4.local_ref = f32[1,2048,128]{2,1,0:T(8,128)} custom-call(s32[12,128]{1,0:T(8,128)} %bitcast.21, s32[12,128]{1,0:T(8,128)} %bitcast.24, f32[2,4,2304,128]{3,2,1,0:T(8,128)} %bitcast.11, f32[2,2304,128]{2,1,0:T(8,128)} %bitcast.15), custom_call_target="tpu_custom_call" | custom-call | flops 12582912 | bytes 2359296 | tf_op jit(solution)/shard_map/child_translate/pallas_call | solution.py:151
  17.8 13.5 %child_translate.3.rest_0_ = f32[2,8192,128]{2,1,0:T(8,128)} custom-call(s32[12,128]{1,0:T(8,128)} %bitcast.22, s32[12,128]{1,0:T(8,128)} %bitcast.25, f32[2,4,2304,128]{3,2,1,0:T(8,128)} %bitcast.12, f32[2,2304,128]{2,1,0:T(8,128)} %bitcast.16), custom_call_target="tpu_custom_call" | custom-call | flops 50331648 | bytes 9437184 | tf_op jit(solution)/shard_map/child_translate/pallas_call | solution.py:151
  31.4 0.0 collective-permute-done
  31.4 0.7 collective-permute-done.1
  32.1 0.9 slice.46
  33.0 0.9 slice.49
  33.9 0.9 slice.45
  34.8 0.9 slice.48
  35.8 0.5 collective-permute-start.2
  36.3 3.4 %collective-permute-start.3 = (f32[8,30,2,128]{3,0,2,1:T(8,128)S(1)}, f32[8,30,2,128]{3,0,2,1:T(8,128)S(1)}, u32[]{:S(2)}, u32[]{:S(2)}) collective-permute-start(f32[8,30,2,128]{3,0,2,1:T(8,128)S(1)} %pad_maximum_fusion.1), channel_id=1, source_target_pairs={{0,1},{1,2},{2,3},{3,0},{4,5},{5,6},{6,7},{7,4},{8,9},{9,10},{10,1... | collective-permute-start | bytes 737288 | tf_op jit(solution)/shard_map/ppermute | solution.py:645
  39.7 0.1 pad.22.clone
  39.8 13.6 %child_translate.5.local_ref = f32[2,8192,128]{2,1,0:T(8,128)} custom-call(s32[12,128]{1,0:T(8,128)} %bitcast.23, s32[12,128]{1,0:T(8,128)} %bitcast.26, f32[2,4,2304,128]{3,2,1,0:T(8,128)} %bitcast.13, f32[2,2304,128]{2,1,0:T(8,128)} %bitcast.17, f32[2,8192,128]{2,1,0:T(8,128)} %child_translate.3.rest_0_), custom_call_target="tpu_custom_call", output_to_operand_aliasing={{}: (4, {})} | custom-call | flops 50331648 | bytes 9437184 | tf_op jit(solution)/shard_map/child_translate/pallas_call | solution.py:151
  53.3 0.0 collective-permute-done.3
  53.3 0.0 collective-permute-done.2
  53.3 0.2 maximum_maximum_fusion
  53.5 1.1 copy.21
  54.7 51.7 %parent_level.1 = f32[30,104,128]{2,1,0:T(8,128)} custom-call(s32[16,12]{1,0:T(8,128)} %source_ref.1, s32[16,12]{1,0:T(8,128)} %kind_ref.1, f32[2,4,24,96,128]{4,3,2,1,0:T(8,128)} %bitcast.14, f32[2,4,3,96,128]{4,3,2,1,0:T(8,128)} %bitcast.6.next_ref, f32[2,4,3,96,128]{4,3,2,1,0:T(8,128)} %bitcast.7.previous_ref, f32[2,4,30,8,128]{4,3,2,1,0:T(8,128)} %bitcast.20, ...), custom_call_target="tpu_custom_call" | custom-call | flops 20000000000 | bytes 18874368 | tf_op jit(solution)/shard_map/parent_level/pallas_call | solution.py:592
  106.4 1.0 fusion.2
  107.4 3.3 %collective-permute-start.5 = (f32[3,104,128]{2,1,0:T(8,128)S(1)}, f32[3,104,128]{2,1,0:T(8,128)S(1)}, u32[]{:S(2)}, u32[]{:S(2)}) collective-permute-start(f32[3,104,128]{2,1,0:T(8,128)S(1)} %get-tuple-element.60), channel_id=1, source_target_pairs={{4,0},{8,4},{12,8},{16,12},{20,16},{24,20},{28,24},{5,1},{9,5},{13... | collective-permute-start | bytes 479240 | tf_op jit(solution)/shard_map/ppermute | solution.py:645
  110.7 1.9 %collective-permute-start.4 = (f32[3,104,128]{2,1,0:T(8,128)S(1)}, f32[3,104,128]{2,1,0:T(8,128)S(1)}, u32[]{:S(2)}, u32[]{:S(2)}) collective-permute-start(f32[3,104,128]{2,1,0:T(8,128)S(1)} %get-tuple-element.59), channel_id=1, source_target_pairs={{0,4},{4,8},{8,12},{12,16},{16,20},{20,24},{24,28},{1,5},{5,9},{9,... | collective-permute-start | bytes 479240 | tf_op jit(solution)/shard_map/ppermute | solution.py:645
  112.6 1.0 collective-permute-done.5
  113.6 4.6 %collective-permute-done.4 = f32[3,104,128]{2,1,0:T(8,128)S(1)} collective-permute-done((f32[3,104,128]{2,1,0:T(8,128)S(1)}, f32[3,104,128]{2,1,0:T(8,128)S(1)}, u32[]{:S(2)}, u32[]{:S(2)}) %collective-permute-start.4) | collective-permute-done | bytes 159776 | tf_op jit(solution)/shard_map/ppermute | solution.py:645
  118.2 1.4 pad_add_fusion
  119.6 0.3 collective-permute-start.6
  120.0 1.8 %collective-permute-start.7 = (f32[24,2,128]{2,1,0:T(2,128)S(1)}, f32[24,2,128]{2,1,0:T(2,128)S(1)}, u32[]{:S(2)}, u32[]{:S(2)}) collective-permute-start(f32[24,2,128]{2,1,0:T(2,128)S(1)} %slice.58), channel_id=1, source_target_pairs={{1,0},{2,1},{3,2},{0,3},{5,4},{6,5},{7,6},{4,7},{9,8},{10,9},{11,1... | collective-permute-start | bytes 73736 | tf_op jit(solution)/shard_map/ppermute | solution.py:645
  121.8 3.9 %collective-permute-done.7 = f32[24,2,128]{2,1,0:T(2,128)S(1)} collective-permute-done((f32[24,2,128]{2,1,0:T(2,128)S(1)}, f32[24,2,128]{2,1,0:T(2,128)S(1)}, u32[]{:S(2)}, u32[]{:S(2)}) %collective-permute-start.7) | collective-permute-done | bytes 24608 | tf_op jit(solution)/shard_map/ppermute | solution.py:645
  125.6 0.0 collective-permute-done.6
  125.6 1.2 fusion
  126.9 10.8 %final_sum.2.rest_0_ = f32[2,4,2304,128]{3,2,1,0:T(8,128)} custom-call(s32[128]{0:T(128)} %slot_ref.3, f32[2,8192,128]{2,1,0:T(8,128)} %child_translate.5.local_ref, f32[2304,128]{1,0:T(8,128)} %bitcast.18, f32[16,18,128]{2,1,0:T(8,128)} %get-tuple-element.55.phase_ref), custom_call_target="tpu_custom_call" | custom-call | flops 8388608 | bytes 18874368 | tf_op jit(solution)/shard_map/final_sum/pallas_call | solution.py:229
  137.6 3.2 %final_sum.3 = f32[2,4,2304,128]{3,2,1,0:T(8,128)} custom-call(s32[128]{0:T(128)} %slot_ref.3, f32[1,2048,128]{2,1,0:T(8,128)} %child_translate.4.local_ref, f32[2304,128]{1,0:T(8,128)} %bitcast.19, f32[16,18,128]{2,1,0:T(8,128)} %get-tuple-element.55.phase_ref, f32[2,4,2304,128]{3,2,1,0:T(8,128)} %final_sum.2.rest_0_), custom_call_target="tpu_custom_call", output_to_operand_aliasing={{}: (4, {})} | custom-call | flops 1048576 | bytes 2359296 | tf_op jit(solution)/shard_map/final_sum/pallas_call | solution.py:229
  (9 shorter events, 0.1 us)
Async XLA Ops:
  1.8 29.6 %collective-permute-start = (f32[8,3,96,128]{3,2,1,0:T(8,128)S(1)}, f32[8,3,96,128]{3,2,1,0:T(8,128)}, u32[]{:S(2)}, u32[]{:S(2)}) collective-permute-start(f32[8,3,96,128]{3,2,1,0:T(8,128)S(1)} %get-tuple-element.58), channel_id=1, source_target_pairs={{4,0},{8,4},{12,8},{16,12},{20,16},{24,20},{28,24},{5,1},{9,5},{13... | collective-permute-start | bytes 3538952 | tf_op jit(solution)/shard_map/ppermute | solution.py:645
  4.6 27.5 %collective-permute-start.1 = (f32[8,3,96,128]{3,2,1,0:T(8,128)S(1)}, f32[8,3,96,128]{3,2,1,0:T(8,128)}, u32[]{:S(2)}, u32[]{:S(2)}) collective-permute-start(f32[8,3,96,128]{3,2,1,0:T(8,128)S(1)} %get-tuple-element.57), channel_id=1, source_target_pairs={{0,4},{4,8},{8,12},{12,16},{16,20},{20,24},{24,28},{1,5},{5,9},{9,... | collective-permute-start | bytes 3538952 | tf_op jit(solution)/shard_map/ppermute | solution.py:645
  35.8 17.5 %collective-permute-start.2 = (f32[8,30,3,128]{3,0,2,1:T(8,128)S(1)}, f32[8,30,3,128]{3,0,2,1:T(8,128)S(1)}, u32[]{:S(2)}, u32[]{:S(2)}) collective-permute-start(f32[8,30,3,128]{3,0,2,1:T(8,128)S(1)} %pad_maximum_fusion), channel_id=1, source_target_pairs={{1,0},{2,1},{3,2},{0,3},{5,4},{6,5},{7,6},{4,7},{9,8},{10,9},{11,1... | collective-permute-start | bytes 1105928 | tf_op jit(solution)/shard_map/ppermute | solution.py:645
  36.3 17.0 %collective-permute-start.3 = (f32[8,30,2,128]{3,0,2,1:T(8,128)S(1)}, f32[8,30,2,128]{3,0,2,1:T(8,128)S(1)}, u32[]{:S(2)}, u32[]{:S(2)}) collective-permute-start(f32[8,30,2,128]{3,0,2,1:T(8,128)S(1)} %pad_maximum_fusion.1), channel_id=1, source_target_pairs={{0,1},{1,2},{2,3},{3,0},{4,5},{5,6},{6,7},{7,4},{8,9},{9,10},{10,1... | collective-permute-start | bytes 737288 | tf_op jit(solution)/shard_map/ppermute | solution.py:645
  107.4 6.2 %collective-permute-start.5 = (f32[3,104,128]{2,1,0:T(8,128)S(1)}, f32[3,104,128]{2,1,0:T(8,128)S(1)}, u32[]{:S(2)}, u32[]{:S(2)}) collective-permute-start(f32[3,104,128]{2,1,0:T(8,128)S(1)} %get-tuple-element.60), channel_id=1, source_target_pairs={{4,0},{8,4},{12,8},{16,12},{20,16},{24,20},{28,24},{5,1},{9,5},{13... | collective-permute-start | bytes 479240 | tf_op jit(solution)/shard_map/ppermute | solution.py:645
  110.7 7.5 %collective-permute-start.4 = (f32[3,104,128]{2,1,0:T(8,128)S(1)}, f32[3,104,128]{2,1,0:T(8,128)S(1)}, u32[]{:S(2)}, u32[]{:S(2)}) collective-permute-start(f32[3,104,128]{2,1,0:T(8,128)S(1)} %get-tuple-element.59), channel_id=1, source_target_pairs={{0,4},{4,8},{8,12},{12,16},{16,20},{20,24},{24,28},{1,5},{5,9},{9,... | collective-permute-start | bytes 479240 | tf_op jit(solution)/shard_map/ppermute | solution.py:645
  119.6 6.0 %collective-permute-start.6 = (f32[24,3,128]{2,1,0:T(4,128)S(1)}, f32[24,3,128]{2,1,0:T(4,128)S(1)}, u32[]{:S(2)}, u32[]{:S(2)}) collective-permute-start(f32[24,3,128]{2,1,0:T(4,128)S(1)} %slice.57), channel_id=1, source_target_pairs={{0,1},{1,2},{2,3},{3,0},{4,5},{5,6},{6,7},{7,4},{8,9},{9,10},{10,1... | collective-permute-start | bytes 110600 | tf_op jit(solution)/shard_map/ppermute | solution.py:645
  120.0 5.7 %collective-permute-start.7 = (f32[24,2,128]{2,1,0:T(2,128)S(1)}, f32[24,2,128]{2,1,0:T(2,128)S(1)}, u32[]{:S(2)}, u32[]{:S(2)}) collective-permute-start(f32[24,2,128]{2,1,0:T(2,128)S(1)} %slice.58), channel_id=1, source_target_pairs={{1,0},{2,1},{3,2},{0,3},{5,4},{6,5},{7,6},{4,7},{9,8},{10,9},{11,1... | collective-permute-start | bytes 73736 | tf_op jit(solution)/shard_map/ppermute | solution.py:645

commit v8 on v7

--- a/solution.py
+++ b/solution.py
@@ -480,12 +480,20 @@
                         value = (terms[0] - terms[1]) + (terms[2] - terms[3])
                     else:
                         value = (terms[0] + terms[1]) + (terms[2] + terms[3])
-                    at = pl.ds(pl.multiple_of((group * per + i) * 64 + target * 32 + (step - 1) * 8, 8), 8)
+                    at, to, both = (
+                        pl.ds(pl.multiple_of((group * per + i) * 96 + part * 32 + (step - 1) * 8, 8), 8)
+                        for part in range(3)
+                    )
                     for lane_tile in range(lane_tiles):
                         lanes = slice(lane_tile * LANES, (lane_tile + 1) * LANES)
                         for row_tile in range(row_tiles):
                             tile = value[row_tile * 8 : row_tile * 8 + 8, lanes]
-                            parent_out[lane_tile * row_tiles + row_tile, at, :] = tile
+                            where = lane_tile * row_tiles + row_tile
+                            if target == 0:
+                                parent_out[where, at, :] = tile
+                            else:
+                                parent_out[where, to, :] = tile
+                                parent_out[where, both, :] = parent_out[where, at, :] + tile
                 return carry
 
             lax.fori_loop(0, parents // per, one_group, 0)
@@ -500,22 +508,23 @@
         def one_tile(tile, carry):
             box = tile // (p_pad // 16)
             row_pair = tile % (p_pad // 16)
-            sources = [pl.ds(pl.multiple_of(source_ref[box, e] * 64, 64), 64) for e in range(entries)]
+            sources = [pl.ds(pl.multiple_of(source_ref[box, e] * 96, 32), 96) for e in range(entries)]
             kinds = [pl.ds(pl.multiple_of(kind_ref[box, e] * 8, 8), 8) for e in range(entries)]
             for lane_tile in range(lane_tiles):
                 halves = []
                 for i in range(2):
                     where = lane_tile * row_tiles + 2 * row_pair + i
-                    total = [None] * 8
+                    sums = [[None] * 4 for _ in range(3)]
                     for e in range(entries):
                         x = parent_out[where, sources[e], :]
                         real, imag = (table_by_kind[where, part, kinds[e], :] for part in range(2))
+                        factors = (imag - real, real + imag, real)
                         for c in range(4):
-                            xr, xi = x[c * 8 : c * 8 + 8], x[(4 + c) * 8 : (4 + c) * 8 + 8]
-                            re = xr * real - xi * imag
-                            im = xr * imag + xi * real
-                            total[c] = re if e == 0 else total[c] + re
-                            total[4 + c] = im if e == 0 else total[4 + c] + im
+                            for part in range(3):
+                                product = x[(4 * part + c) * 8 : (4 * part + c) * 8 + 8] * factors[part]
+                                sums[part][c] = product if e == 0 else sums[part][c] + product
+                    total = [sums[2][c] - sums[1][c] for c in range(4)]
+                    total += [sums[2][c] + sums[0][c] for c in range(4)]
                     halves.append(total)
                 for c in range(8):
                     high, low = split(jnp.concatenate([halves[0][c], halves[1][c]], axis=0))
@@ -613,7 +622,7 @@
             pltpu.VMEM((2, 128 * (t_pad + 8), f_pad), F32),
             pltpu.VMEM((4, parents * p_pad, 3 * f_pad), BF16),
             pltpu.VMEM((q_pad // LANES * (p_pad // 8), 2, translators * 8, LANES), F32),
-            pltpu.VMEM((q_pad // LANES * (p_pad // 8), parents * 64, LANES), F32),
+            pltpu.VMEM((q_pad // LANES * (p_pad // 8), parents * 96, LANES), F32),
             pltpu.VMEM((8 * parents * p_pad, q_pad), BF16),
             pltpu.VMEM((8 * parents * p_pad, q_pad), BF16),
             pltpu.VMEM((8 * parents * (t_pad + 8), f_pad), F32),
@@ -680,9 +689,9 @@
     local = [None] * len(pieces)
     chunks = [(n, i) for n, piece in enumerate(pieces) for i in range(piece[1])]
 
-    def translate_next(child, last=False):
+    def translate_next(child):
         if chunks:
-            n, i = chunks.pop(-1 if last else 0)
+            n, i = chunks.pop(0)
             local[n] = child_translate(
                 child, flat_table, sources_child.T, kinds_child.T, pieces[n], i, local[n]
             )
@@ -692,8 +701,6 @@
     first_child, made = barrier((flat_child, (combine, polar_cos, polar_sin, phase, phase_child)))
     combine, polar_cos, polar_sin, phase, phase_child = made
     translate_next(first_child)
-    if len(chunks) > 1:
-        translate_next(first_child, last=True)
     after, before, local = barrier((after, before, local))
 
     low, high = (
@@ -703,7 +710,8 @@
     low, high, later_child = barrier((low, high, flat_child))
     right = send(low, "phi", False)
     left = send(high, "phi", True)
-    translate_next(later_child)
+    if len(chunks) > 1:
+        translate_next(later_child)
     right, left, local = barrier((right, left, local))
     side = jnp.concatenate([right, left, jnp.zeros((8, rows + 6, 3, boxes), F32)], axis=2)
 

time: 141 us -> 140 us (level)
  starting transfers between devices: 15.9 us -> 19.1 us
  waiting for transfers between devices: 10.2 us -> 8.36 us
  local copies, waits for them, and re-layouts: 10.3 us -> 8.56 us
    ppermute x8, starting transfers between devices: 15.9 us -> 19.1 us  [send(): lax.ppermute(block, axis, pairs if up else [(b, a) for a, b in pairs])]
    ppermute x8, waiting for transfers between devices: 10.2 us -> 8.36 us  [send(): lax.ppermute(block, axis, pairs if up else [(b, a) for a, b in pairs])]
    slice x10, local copies, waits for them, and re-layouts: 6.03 us -> 4.26 us  [per_device(): edge[:, :, at]]
  transfers between devices with their start and end apart: 8 -> 8, of which waited for: 4 -> 3; matrix products, arithmetic and copies ran while one was open for 2% -> 2% of each run, Pallas kernels for 25% -> 26%
where the time goes in v8:
time: 140 us; the launch traced here: 139 us
  Pallas kernels  101 us (72%)
  starting transfers between devices  19.1 us (14%)
  local copies, waits for them, and re-layouts  8.56 us (6%)
  waiting for transfers between devices  8.36 us (6%)
  other arithmetic  1.59 us (1%)
    pallas_call x1, Pallas kernels, parent_level(): pl.pallas_call(functools.partial(parent_kernel, (rows, columns, rows_up,...  51.7 us
    pallas_call x3, Pallas kernels, child_translate(): pl.pallas_call(functools.partial(translate_kernel, packed, rows), grid=(4...  33.8 us
    ppermute x8, starting transfers between devices, send(): lax.ppermute(block, axis, pairs if up else [(b, a) for a, b in pairs])  19.1 us
    pallas_call x2, Pallas kernels, final_sum(): pl.pallas_call(functools.partial(sum_kernel, packed, rows, LANES // 8), g...  13.9 us
    ppermute x8, waiting for transfers between devices, send(): lax.ppermute(block, axis, pairs if up else [(b, a) for a, b in pairs])  8.36 us
    slice x10, local copies, waits for them, and re-layouts, per_device(): edge[:, :, at]  4.26 us
  transfers between devices with their start and end apart: 8, of which 3 were waited for; matrix products, arithmetic and copies ran while one was open for 2% of the time, Pallas kernels for 26%

profile of v8, /device:TPU:28, one launch (start us, length us, event | category | flops | bytes accessed | tf_op | source)
XLA Modules:
  0.0 139.0 jit_solution(15685282373594299246)
XLA Ops:
  0.0 1.8 %fusion.1 = (f32[8,3,96,128]{3,2,1,0:T(8,128)S(1)}, f32[8,3,96,128]{3,2,1,0:T(8,128)S(1)}) fusion(f32[8,24,96,128]{3,2,1,0:T(8,128)} %param.12), kind=kLoop, calls=%fused_computation.6 | loop fusion | bytes 4718592 | tf_op jit(solution)/shard_map/slice | solution.py:700
  1.8 1.9 %collective-permute-start.1 = (f32[8,3,96,128]{3,2,1,0:T(8,128)S(1)}, f32[8,3,96,128]{3,2,1,0:T(8,128)S(1)}, u32[]{:S(2)}, u32[]{:S(2)}) collective-permute-start(f32[8,3,96,128]{3,2,1,0:T(8,128)S(1)} %get-tuple-element.55), channel_id=1, source_target_pairs={{0,4},{4,8},{8,12},{12,16},{16,20},{20,24},{24,28},{1,5},{5,9},{9,... | collective-permute-start | bytes 3538952 | tf_op jit(solution)/shard_map/ppermute | solution.py:654
  3.7 4.5 %collective-permute-start = (f32[8,3,96,128]{3,2,1,0:T(8,128)S(1)}, f32[8,3,96,128]{3,2,1,0:T(8,128)}, u32[]{:S(2)}, u32[]{:S(2)}) collective-permute-start(f32[8,3,96,128]{3,2,1,0:T(8,128)S(1)} %get-tuple-element.56), channel_id=1, source_target_pairs={{4,0},{8,4},{12,8},{16,12},{20,16},{24,20},{28,24},{5,1},{9,5},{13... | collective-permute-start | bytes 3538952 | tf_op jit(solution)/shard_map/ppermute | solution.py:654
  8.3 1.2 slice.47
  9.5 1.2 slice.42
  10.7 0.1 copy.23
  10.8 0.2 copy.22
  11.0 1.8 %tables.1 = (bf16[128,256]{1,0:T(8,128)(2,1)}, f32[48,32]{1,0:T(8,128)}, f32[48,32]{1,0:T(8,128)}, f32[4,48,256]{2,1,0:T(8,128)}, f32[16,18,128]{2,1,0:T(8,128)}) custom-call(s32[1,128]{1,0:T(1,128)} %bitcast.27, f32[48,32]{1,0:T(8,128)} %constant.12.clone.polar_up_ref), custom_call_target="tpu_custom_call" | custom-call | tf_op jit(solution)/shard_map/tables/pallas_call | solution.py:328
  12.8 13.5 %child_translate.3.rest_0_ = f32[2,8192,128]{2,1,0:T(8,128)} custom-call(s32[12,128]{1,0:T(8,128)} %bitcast.21, s32[12,128]{1,0:T(8,128)} %bitcast.24, f32[2,4,2304,128]{3,2,1,0:T(8,128)} %bitcast.11, f32[2,2304,128]{2,1,0:T(8,128)} %bitcast.15), custom_call_target="tpu_custom_call" | custom-call | flops 50331648 | bytes 9437184 | tf_op jit(solution)/shard_map/child_translate/pallas_call | solution.py:151
  26.2 3.8 %collective-permute-done.1 = f32[8,3,96,128]{3,2,1,0:T(8,128)S(1)} collective-permute-done((f32[8,3,96,128]{3,2,1,0:T(8,128)S(1)}, f32[8,3,96,128]{3,2,1,0:T(8,128)S(1)}, u32[]{:S(2)}, u32[]{:S(2)}) %collective-permute-start.1) | collective-permute-done | bytes 1179680 | tf_op jit(solution)/shard_map/ppermute | solution.py:654
  30.1 0.0 copy-start.1
  30.1 0.9 collective-permute-done
  31.0 0.9 slice.48
  31.9 0.9 slice.45
  32.9 0.5 collective-permute-start.2
  33.4 3.4 %collective-permute-start.3 = (f32[8,30,2,128]{3,0,2,1:T(8,128)S(1)}, f32[8,30,2,128]{3,0,2,1:T(8,128)S(1)}, u32[]{:S(2)}, u32[]{:S(2)}) collective-permute-start(f32[8,30,2,128]{3,0,2,1:T(8,128)S(1)} %pad_maximum_fusion.1), channel_id=1, source_target_pairs={{0,1},{1,2},{2,3},{3,0},{4,5},{5,6},{6,7},{7,4},{8,9},{9,10},{10,1... | collective-permute-start | bytes 737288 | tf_op jit(solution)/shard_map/ppermute | solution.py:654
  36.8 0.1 pad.22.clone
  36.9 13.5 %child_translate.4.local_ref = f32[2,8192,128]{2,1,0:T(8,128)} custom-call(s32[12,128]{1,0:T(8,128)} %bitcast.22, s32[12,128]{1,0:T(8,128)} %bitcast.25, f32[2,4,2304,128]{3,2,1,0:T(8,128)} %bitcast.12, f32[2,2304,128]{2,1,0:T(8,128)} %bitcast.16, f32[2,8192,128]{2,1,0:T(8,128)} %child_translate.3.rest_0_), custom_call_target="tpu_custom_call", output_to_operand_aliasing={{}: (4, {})} | custom-call | flops 50331648 | bytes 9437184 | tf_op jit(solution)/shard_map/child_translate/pallas_call | solution.py:151
  50.4 0.0 copy-done.1
  50.4 0.0 collective-permute-done.3
  50.4 0.0 collective-permute-done.2
  50.4 0.2 maximum_maximum_fusion
  50.6 1.1 copy.21
  51.7 51.7 %parent_level.1 = f32[30,104,128]{2,1,0:T(8,128)} custom-call(s32[16,12]{1,0:T(8,128)} %source_ref.1, s32[16,12]{1,0:T(8,128)} %kind_ref.1, f32[2,4,24,96,128]{4,3,2,1,0:T(8,128)} %bitcast.13, f32[2,4,3,96,128]{4,3,2,1,0:T(8,128)} %bitcast.6.next_ref, f32[2,4,3,96,128]{4,3,2,1,0:T(8,128)} %bitcast.28, f32[2,4,30,8,128]{4,3,2,1,0:T(8,128)} %bitcast.20, ...), custom_call_target="tpu_custom_call" | custom-call | flops 20000000000 | bytes 18874368 | tf_op jit(solution)/shard_map/parent_level/pallas_call | solution.py:601
  103.5 1.0 fusion.2
  104.5 1.9 %collective-permute-start.4 = (f32[3,104,128]{2,1,0:T(8,128)S(1)}, f32[3,104,128]{2,1,0:T(8,128)S(1)}, u32[]{:S(2)}, u32[]{:S(2)}) collective-permute-start(f32[3,104,128]{2,1,0:T(8,128)S(1)} %get-tuple-element.57), channel_id=1, source_target_pairs={{0,4},{4,8},{8,12},{12,16},{16,20},{20,24},{24,28},{1,5},{5,9},{9,... | collective-permute-start | bytes 479240 | tf_op jit(solution)/shard_map/ppermute | solution.py:654
  106.4 0.0 copy-start
  106.4 4.7 %collective-permute-start.5 = (f32[3,104,128]{2,1,0:T(8,128)S(1)}, f32[3,104,128]{2,1,0:T(8,128)S(1)}, u32[]{:S(2)}, u32[]{:S(2)}) collective-permute-start(f32[3,104,128]{2,1,0:T(8,128)S(1)} %get-tuple-element.58), channel_id=1, source_target_pairs={{4,0},{8,4},{12,8},{16,12},{20,16},{24,20},{28,24},{5,1},{9,5},{13... | collective-permute-start | bytes 479240 | tf_op jit(solution)/shard_map/ppermute | solution.py:654
  111.1 6.8 %child_translate.5.local_ref = f32[1,2048,128]{2,1,0:T(8,128)} custom-call(s32[12,128]{1,0:T(8,128)} %bitcast.23, s32[12,128]{1,0:T(8,128)} %bitcast.26, f32[2,4,2304,128]{3,2,1,0:T(8,128)} %bitcast.14, f32[2,2304,128]{2,1,0:T(8,128)} %bitcast.17), custom_call_target="tpu_custom_call" | custom-call | flops 12582912 | bytes 2359296 | tf_op jit(solution)/shard_map/child_translate/pallas_call | solution.py:151
  117.9 0.0 collective-permute-done.4
  117.9 0.0 collective-permute-done.5
  117.9 0.0 copy-done
  117.9 0.1 pad_add_fusion
  118.1 0.1 collective-permute-start.6
  118.2 2.1 %collective-permute-start.7 = (f32[24,2,128]{2,1,0:T(2,128)S(1)}, f32[24,2,128]{2,1,0:T(2,128)S(1)}, u32[]{:S(2)}, u32[]{:S(2)}) collective-permute-start(f32[24,2,128]{2,1,0:T(2,128)S(1)} %slice.58), channel_id=1, source_target_pairs={{1,0},{2,1},{3,2},{0,3},{5,4},{6,5},{7,6},{4,7},{9,8},{10,9},{11,1... | collective-permute-start | bytes 73736 | tf_op jit(solution)/shard_map/ppermute | solution.py:654
  120.2 3.6 %collective-permute-done.7 = f32[24,2,128]{2,1,0:T(2,128)S(1)} collective-permute-done((f32[24,2,128]{2,1,0:T(2,128)S(1)}, f32[24,2,128]{2,1,0:T(2,128)S(1)}, u32[]{:S(2)}, u32[]{:S(2)}) %collective-permute-start.7) | collective-permute-done | bytes 24608 | tf_op jit(solution)/shard_map/ppermute | solution.py:654
  123.8 0.0 collective-permute-done.6
  123.8 1.3 fusion
  125.1 10.8 %final_sum.2.rest_0_ = f32[2,4,2304,128]{3,2,1,0:T(8,128)} custom-call(s32[128]{0:T(128)} %slot_ref.3, f32[2,8192,128]{2,1,0:T(8,128)} %child_translate.4.local_ref, f32[2304,128]{1,0:T(8,128)} %bitcast.18, f32[16,18,128]{2,1,0:T(8,128)} %get-tuple-element.53.phase_ref), custom_call_target="tpu_custom_call" | custom-call | flops 8388608 | bytes 18874368 | tf_op jit(solution)/shard_map/final_sum/pallas_call | solution.py:229
  135.9 3.2 %final_sum.3 = f32[2,4,2304,128]{3,2,1,0:T(8,128)} custom-call(s32[128]{0:T(128)} %slot_ref.3, f32[1,2048,128]{2,1,0:T(8,128)} %child_translate.5.local_ref, f32[2304,128]{1,0:T(8,128)} %bitcast.19, f32[16,18,128]{2,1,0:T(8,128)} %get-tuple-element.53.phase_ref, f32[2,4,2304,128]{3,2,1,0:T(8,128)} %final_sum.2.rest_0_), custom_call_target="tpu_custom_call", output_to_operand_aliasing={{}: (4, {})} | custom-call | flops 1048576 | bytes 2359296 | tf_op jit(solution)/shard_map/final_sum/pallas_call | solution.py:229
  (11 shorter events, 0.1 us)
Async XLA Ops:
  1.8 28.2 %collective-permute-start.1 = (f32[8,3,96,128]{3,2,1,0:T(8,128)S(1)}, f32[8,3,96,128]{3,2,1,0:T(8,128)S(1)}, u32[]{:S(2)}, u32[]{:S(2)}) collective-permute-start(f32[8,3,96,128]{3,2,1,0:T(8,128)S(1)} %get-tuple-element.55), channel_id=1, source_target_pairs={{0,4},{4,8},{8,12},{12,16},{16,20},{20,24},{24,28},{1,5},{5,9},{9,... | collective-permute-start | bytes 3538952 | tf_op jit(solution)/shard_map/ppermute | solution.py:654
  3.7 27.2 %collective-permute-start = (f32[8,3,96,128]{3,2,1,0:T(8,128)S(1)}, f32[8,3,96,128]{3,2,1,0:T(8,128)}, u32[]{:S(2)}, u32[]{:S(2)}) collective-permute-start(f32[8,3,96,128]{3,2,1,0:T(8,128)S(1)} %get-tuple-element.56), channel_id=1, source_target_pairs={{4,0},{8,4},{12,8},{16,12},{20,16},{24,20},{28,24},{5,1},{9,5},{13... | collective-permute-start | bytes 3538952 | tf_op jit(solution)/shard_map/ppermute | solution.py:654
  30.1 20.4 %copy-start.1 = (f32[8,3,96,128]{3,2,1,0:T(8,128)}, f32[8,3,96,128]{3,2,1,0:T(8,128)S(1)}, u32[]{:S(2)}) copy-start(f32[8,3,96,128]{3,2,1,0:T(8,128)S(1)} %collective-permute-done.1) | copy-start | bytes 3538948
  32.9 17.5 %collective-permute-start.2 = (f32[8,30,3,128]{3,0,2,1:T(8,128)S(1)}, f32[8,30,3,128]{3,0,2,1:T(8,128)S(1)}, u32[]{:S(2)}, u32[]{:S(2)}) collective-permute-start(f32[8,30,3,128]{3,0,2,1:T(8,128)S(1)} %pad_maximum_fusion), channel_id=1, source_target_pairs={{1,0},{2,1},{3,2},{0,3},{5,4},{6,5},{7,6},{4,7},{9,8},{10,9},{11,1... | collective-permute-start | bytes 1105928 | tf_op jit(solution)/shard_map/ppermute | solution.py:654
  33.4 17.0 %collective-permute-start.3 = (f32[8,30,2,128]{3,0,2,1:T(8,128)S(1)}, f32[8,30,2,128]{3,0,2,1:T(8,128)S(1)}, u32[]{:S(2)}, u32[]{:S(2)}) collective-permute-start(f32[8,30,2,128]{3,0,2,1:T(8,128)S(1)} %pad_maximum_fusion.1), channel_id=1, source_target_pairs={{0,1},{1,2},{2,3},{3,0},{4,5},{5,6},{6,7},{7,4},{8,9},{9,10},{10,1... | collective-permute-start | bytes 737288 | tf_op jit(solution)/shard_map/ppermute | solution.py:654
  104.5 13.4 %collective-permute-start.4 = (f32[3,104,128]{2,1,0:T(8,128)S(1)}, f32[3,104,128]{2,1,0:T(8,128)S(1)}, u32[]{:S(2)}, u32[]{:S(2)}) collective-permute-start(f32[3,104,128]{2,1,0:T(8,128)S(1)} %get-tuple-element.57), channel_id=1, source_target_pairs={{0,4},{4,8},{8,12},{12,16},{16,20},{20,24},{24,28},{1,5},{5,9},{9,... | collective-permute-start | bytes 479240 | tf_op jit(solution)/shard_map/ppermute | solution.py:654
  106.4 11.5 %copy-start = (f32[30,104,128]{2,1,0:T(8,128)S(1)}, f32[30,104,128]{2,1,0:T(8,128)}, u32[]{:S(2)}) copy-start(f32[30,104,128]{2,1,0:T(8,128)} %parent_level.1) | copy-start | bytes 4792324
  106.4 11.5 %collective-permute-start.5 = (f32[3,104,128]{2,1,0:T(8,128)S(1)}, f32[3,104,128]{2,1,0:T(8,128)S(1)}, u32[]{:S(2)}, u32[]{:S(2)}) collective-permute-start(f32[3,104,128]{2,1,0:T(8,128)S(1)} %get-tuple-element.58), channel_id=1, source_target_pairs={{4,0},{8,4},{12,8},{16,12},{20,16},{24,20},{28,24},{5,1},{9,5},{13... | collective-permute-start | bytes 479240 | tf_op jit(solution)/shard_map/ppermute | solution.py:654
  118.1 5.8 %collective-permute-start.6 = (f32[24,3,128]{2,1,0:T(4,128)S(1)}, f32[24,3,128]{2,1,0:T(4,128)S(1)}, u32[]{:S(2)}, u32[]{:S(2)}) collective-permute-start(f32[24,3,128]{2,1,0:T(4,128)S(1)} %slice.57), channel_id=1, source_target_pairs={{0,1},{1,2},{2,3},{3,0},{4,5},{5,6},{6,7},{7,4},{8,9},{9,10},{10,1... | collective-permute-start | bytes 110600 | tf_op jit(solution)/shard_map/ppermute | solution.py:654
  118.2 5.7 %collective-permute-start.7 = (f32[24,2,128]{2,1,0:T(2,128)S(1)}, f32[24,2,128]{2,1,0:T(2,128)S(1)}, u32[]{:S(2)}, u32[]{:S(2)}) collective-permute-start(f32[24,2,128]{2,1,0:T(2,128)S(1)} %slice.58), channel_id=1, source_target_pairs={{1,0},{2,1},{3,2},{0,3},{5,4},{6,5},{7,6},{4,7},{9,8},{10,9},{11,1... | collective-permute-start | bytes 73736 | tf_op jit(solution)/shard_map/ppermute | solution.py:654

commit v9 on v8

--- a/solution.py
+++ b/solution.py
@@ -128,7 +128,7 @@
                 out_ref[0, pl.ds(pl.multiple_of(i * tile, tile) + g * 8, 8), :] = total[g]
             return carry
 
-        lax.fori_loop(0, half, one_box, 0, unroll=2)
+        lax.fori_loop(0, half, one_box, 0, unroll=4)
 
 
 def child_translate(child, table, sources, kinds, segment, chunk, onto):
@@ -197,7 +197,7 @@
                 total[pl.ds(here + (groups + g) * 8, 8), :] = local[to] + (imag * cosine - real * sine)
             return carry
 
-        lax.fori_loop(0, half, one_box, 0, unroll=4)
+        lax.fori_loop(0, half, one_box, 0, unroll=8)
 
     @pl.when(step >= 2)
     def _():

time: 140 us -> 139 us (level)
  no operation moved by 1% of the time
where the time goes in v9:
time: 139 us; the launch traced here: 138 us
  Pallas kernels  101 us (73%)
  starting transfers between devices  19.1 us (14%)
  local copies, waits for them, and re-layouts  8.56 us (6%)
  waiting for transfers between devices  8.37 us (6%)
  other arithmetic  1.59 us (1%)
    pallas_call x1, Pallas kernels, parent_level(): pl.pallas_call(functools.partial(parent_kernel, (rows, columns, rows_up,...  51.7 us
    pallas_call x3, Pallas kernels, child_translate(): pl.pallas_call(functools.partial(translate_kernel, packed, rows), grid=(4...  33.6 us
    ppermute x8, starting transfers between devices, send(): lax.ppermute(block, axis, pairs if up else [(b, a) for a, b in pairs])  19.1 us
    pallas_call x2, Pallas kernels, final_sum(): pl.pallas_call(functools.partial(sum_kernel, packed, rows, LANES // 8), g...  13.6 us
    ppermute x8, waiting for transfers between devices, send(): lax.ppermute(block, axis, pairs if up else [(b, a) for a, b in pairs])  8.37 us
    slice x10, local copies, waits for them, and re-layouts, per_device(): edge[:, :, at]  4.26 us
  transfers between devices with their start and end apart: 8, of which 3 were waited for; matrix products, arithmetic and copies ran while one was open for 2% of the time, Pallas kernels for 26%

profile of v9, /device:TPU:28, one launch (start us, length us, event | category | flops | bytes accessed | tf_op | source)
XLA Modules:
  0.0 138.4 jit_solution(2041308164792972349)
XLA Ops:
  0.0 1.8 %fusion.1 = (f32[8,3,96,128]{3,2,1,0:T(8,128)S(1)}, f32[8,3,96,128]{3,2,1,0:T(8,128)S(1)}) fusion(f32[8,24,96,128]{3,2,1,0:T(8,128)} %param.12), kind=kLoop, calls=%fused_computation.6 | loop fusion | bytes 4718592 | tf_op jit(solution)/shard_map/slice | solution.py:700
  1.8 1.9 %collective-permute-start.1 = (f32[8,3,96,128]{3,2,1,0:T(8,128)S(1)}, f32[8,3,96,128]{3,2,1,0:T(8,128)S(1)}, u32[]{:S(2)}, u32[]{:S(2)}) collective-permute-start(f32[8,3,96,128]{3,2,1,0:T(8,128)S(1)} %get-tuple-element.55), channel_id=1, source_target_pairs={{0,4},{4,8},{8,12},{12,16},{16,20},{20,24},{24,28},{1,5},{5,9},{9,... | collective-permute-start | bytes 3538952 | tf_op jit(solution)/shard_map/ppermute | solution.py:654
  3.7 4.5 %collective-permute-start = (f32[8,3,96,128]{3,2,1,0:T(8,128)S(1)}, f32[8,3,96,128]{3,2,1,0:T(8,128)}, u32[]{:S(2)}, u32[]{:S(2)}) collective-permute-start(f32[8,3,96,128]{3,2,1,0:T(8,128)S(1)} %get-tuple-element.56), channel_id=1, source_target_pairs={{4,0},{8,4},{12,8},{16,12},{20,16},{24,20},{28,24},{5,1},{9,5},{13... | collective-permute-start | bytes 3538952 | tf_op jit(solution)/shard_map/ppermute | solution.py:654
  8.3 1.2 slice.47
  9.5 1.2 slice.42
  10.7 0.1 copy.23
  10.8 0.2 copy.22
  11.0 1.8 %tables.1 = (bf16[128,256]{1,0:T(8,128)(2,1)}, f32[48,32]{1,0:T(8,128)}, f32[48,32]{1,0:T(8,128)}, f32[4,48,256]{2,1,0:T(8,128)}, f32[16,18,128]{2,1,0:T(8,128)}) custom-call(s32[1,128]{1,0:T(1,128)} %bitcast.27, f32[48,32]{1,0:T(8,128)} %constant.12.clone.polar_up_ref), custom_call_target="tpu_custom_call" | custom-call | tf_op jit(solution)/shard_map/tables/pallas_call | solution.py:328
  12.8 13.5 %child_translate.3.rest_0_ = f32[2,8192,128]{2,1,0:T(8,128)} custom-call(s32[12,128]{1,0:T(8,128)} %bitcast.21, s32[12,128]{1,0:T(8,128)} %bitcast.24, f32[2,4,2304,128]{3,2,1,0:T(8,128)} %bitcast.11, f32[2,2304,128]{2,1,0:T(8,128)} %bitcast.15), custom_call_target="tpu_custom_call" | custom-call | flops 50331648 | bytes 9437184 | tf_op jit(solution)/shard_map/child_translate/pallas_call | solution.py:151
  26.2 3.8 %collective-permute-done.1 = f32[8,3,96,128]{3,2,1,0:T(8,128)S(1)} collective-permute-done((f32[8,3,96,128]{3,2,1,0:T(8,128)S(1)}, f32[8,3,96,128]{3,2,1,0:T(8,128)S(1)}, u32[]{:S(2)}, u32[]{:S(2)}) %collective-permute-start.1) | collective-permute-done | bytes 1179680 | tf_op jit(solution)/shard_map/ppermute | solution.py:654
  30.1 0.0 copy-start.1
  30.1 0.9 collective-permute-done
  31.0 0.9 slice.48
  31.9 0.9 slice.45
  32.9 0.5 collective-permute-start.2
  33.4 3.4 %collective-permute-start.3 = (f32[8,30,2,128]{3,0,2,1:T(8,128)S(1)}, f32[8,30,2,128]{3,0,2,1:T(8,128)S(1)}, u32[]{:S(2)}, u32[]{:S(2)}) collective-permute-start(f32[8,30,2,128]{3,0,2,1:T(8,128)S(1)} %pad_maximum_fusion.1), channel_id=1, source_target_pairs={{0,1},{1,2},{2,3},{3,0},{4,5},{5,6},{6,7},{7,4},{8,9},{9,10},{10,1... | collective-permute-start | bytes 737288 | tf_op jit(solution)/shard_map/ppermute | solution.py:654
  36.8 0.1 pad.22.clone
  36.9 13.5 %child_translate.4.local_ref = f32[2,8192,128]{2,1,0:T(8,128)} custom-call(s32[12,128]{1,0:T(8,128)} %bitcast.22, s32[12,128]{1,0:T(8,128)} %bitcast.25, f32[2,4,2304,128]{3,2,1,0:T(8,128)} %bitcast.12, f32[2,2304,128]{2,1,0:T(8,128)} %bitcast.16, f32[2,8192,128]{2,1,0:T(8,128)} %child_translate.3.rest_0_), custom_call_target="tpu_custom_call", output_to_operand_aliasing={{}: (4, {})} | custom-call | flops 50331648 | bytes 9437184 | tf_op jit(solution)/shard_map/child_translate/pallas_call | solution.py:151
  50.4 0.0 copy-done.1
  50.4 0.0 collective-permute-done.3
  50.4 0.0 collective-permute-done.2
  50.4 0.2 maximum_maximum_fusion
  50.6 1.1 copy.21
  51.7 51.7 %parent_level.1 = f32[30,104,128]{2,1,0:T(8,128)} custom-call(s32[16,12]{1,0:T(8,128)} %source_ref.1, s32[16,12]{1,0:T(8,128)} %kind_ref.1, f32[2,4,24,96,128]{4,3,2,1,0:T(8,128)} %bitcast.13, f32[2,4,3,96,128]{4,3,2,1,0:T(8,128)} %bitcast.6.next_ref, f32[2,4,3,96,128]{4,3,2,1,0:T(8,128)} %bitcast.28, f32[2,4,30,8,128]{4,3,2,1,0:T(8,128)} %bitcast.20, ...), custom_call_target="tpu_custom_call" | custom-call | flops 20000000000 | bytes 18874368 | tf_op jit(solution)/shard_map/parent_level/pallas_call | solution.py:601
  103.4 1.0 fusion.2
  104.4 1.9 %collective-permute-start.4 = (f32[3,104,128]{2,1,0:T(8,128)S(1)}, f32[3,104,128]{2,1,0:T(8,128)S(1)}, u32[]{:S(2)}, u32[]{:S(2)}) collective-permute-start(f32[3,104,128]{2,1,0:T(8,128)S(1)} %get-tuple-element.57), channel_id=1, source_target_pairs={{0,4},{4,8},{8,12},{12,16},{16,20},{20,24},{24,28},{1,5},{5,9},{9,... | collective-permute-start | bytes 479240 | tf_op jit(solution)/shard_map/ppermute | solution.py:654
  106.4 0.0 copy-start
  106.4 4.7 %collective-permute-start.5 = (f32[3,104,128]{2,1,0:T(8,128)S(1)}, f32[3,104,128]{2,1,0:T(8,128)S(1)}, u32[]{:S(2)}, u32[]{:S(2)}) collective-permute-start(f32[3,104,128]{2,1,0:T(8,128)S(1)} %get-tuple-element.58), channel_id=1, source_target_pairs={{4,0},{8,4},{12,8},{16,12},{20,16},{24,20},{28,24},{5,1},{9,5},{13... | collective-permute-start | bytes 479240 | tf_op jit(solution)/shard_map/ppermute | solution.py:654
  111.1 6.6 %child_translate.5.local_ref = f32[1,2048,128]{2,1,0:T(8,128)} custom-call(s32[12,128]{1,0:T(8,128)} %bitcast.23, s32[12,128]{1,0:T(8,128)} %bitcast.26, f32[2,4,2304,128]{3,2,1,0:T(8,128)} %bitcast.14, f32[2,2304,128]{2,1,0:T(8,128)} %bitcast.17), custom_call_target="tpu_custom_call" | custom-call | flops 12582912 | bytes 2359296 | tf_op jit(solution)/shard_map/child_translate/pallas_call | solution.py:151
  117.7 0.0 collective-permute-done.4
  117.7 0.0 collective-permute-done.5
  117.7 0.0 copy-done
  117.7 0.1 pad_add_fusion
  117.8 0.1 collective-permute-start.6
  117.9 2.1 %collective-permute-start.7 = (f32[24,2,128]{2,1,0:T(2,128)S(1)}, f32[24,2,128]{2,1,0:T(2,128)S(1)}, u32[]{:S(2)}, u32[]{:S(2)}) collective-permute-start(f32[24,2,128]{2,1,0:T(2,128)S(1)} %slice.58), channel_id=1, source_target_pairs={{1,0},{2,1},{3,2},{0,3},{5,4},{6,5},{7,6},{4,7},{9,8},{10,9},{11,1... | collective-permute-start | bytes 73736 | tf_op jit(solution)/shard_map/ppermute | solution.py:654
  120.0 3.6 %collective-permute-done.7 = f32[24,2,128]{2,1,0:T(2,128)S(1)} collective-permute-done((f32[24,2,128]{2,1,0:T(2,128)S(1)}, f32[24,2,128]{2,1,0:T(2,128)S(1)}, u32[]{:S(2)}, u32[]{:S(2)}) %collective-permute-start.7) | collective-permute-done | bytes 24608 | tf_op jit(solution)/shard_map/ppermute | solution.py:654
  123.6 0.0 collective-permute-done.6
  123.6 1.3 fusion
  124.9 10.5 %final_sum.2.rest_0_ = f32[2,4,2304,128]{3,2,1,0:T(8,128)} custom-call(s32[128]{0:T(128)} %slot_ref.3, f32[2,8192,128]{2,1,0:T(8,128)} %child_translate.4.local_ref, f32[2304,128]{1,0:T(8,128)} %bitcast.18, f32[16,18,128]{2,1,0:T(8,128)} %get-tuple-element.53.phase_ref), custom_call_target="tpu_custom_call" | custom-call | flops 8388608 | bytes 18874368 | tf_op jit(solution)/shard_map/final_sum/pallas_call | solution.py:229
  135.4 3.0 %final_sum.3 = f32[2,4,2304,128]{3,2,1,0:T(8,128)} custom-call(s32[128]{0:T(128)} %slot_ref.3, f32[1,2048,128]{2,1,0:T(8,128)} %child_translate.5.local_ref, f32[2304,128]{1,0:T(8,128)} %bitcast.19, f32[16,18,128]{2,1,0:T(8,128)} %get-tuple-element.53.phase_ref, f32[2,4,2304,128]{3,2,1,0:T(8,128)} %final_sum.2.rest_0_), custom_call_target="tpu_custom_call", output_to_operand_aliasing={{}: (4, {})} | custom-call | flops 1048576 | bytes 2359296 | tf_op jit(solution)/shard_map/final_sum/pallas_call | solution.py:229
  (11 shorter events, 0.1 us)
Async XLA Ops:
  1.8 28.2 %collective-permute-start.1 = (f32[8,3,96,128]{3,2,1,0:T(8,128)S(1)}, f32[8,3,96,128]{3,2,1,0:T(8,128)S(1)}, u32[]{:S(2)}, u32[]{:S(2)}) collective-permute-start(f32[8,3,96,128]{3,2,1,0:T(8,128)S(1)} %get-tuple-element.55), channel_id=1, source_target_pairs={{0,4},{4,8},{8,12},{12,16},{16,20},{20,24},{24,28},{1,5},{5,9},{9,... | collective-permute-start | bytes 3538952 | tf_op jit(solution)/shard_map/ppermute | solution.py:654
  3.7 27.2 %collective-permute-start = (f32[8,3,96,128]{3,2,1,0:T(8,128)S(1)}, f32[8,3,96,128]{3,2,1,0:T(8,128)}, u32[]{:S(2)}, u32[]{:S(2)}) collective-permute-start(f32[8,3,96,128]{3,2,1,0:T(8,128)S(1)} %get-tuple-element.56), channel_id=1, source_target_pairs={{4,0},{8,4},{12,8},{16,12},{20,16},{24,20},{28,24},{5,1},{9,5},{13... | collective-permute-start | bytes 3538952 | tf_op jit(solution)/shard_map/ppermute | solution.py:654
  30.1 20.3 %copy-start.1 = (f32[8,3,96,128]{3,2,1,0:T(8,128)}, f32[8,3,96,128]{3,2,1,0:T(8,128)S(1)}, u32[]{:S(2)}) copy-start(f32[8,3,96,128]{3,2,1,0:T(8,128)S(1)} %collective-permute-done.1) | copy-start | bytes 3538948
  32.9 17.5 %collective-permute-start.2 = (f32[8,30,3,128]{3,0,2,1:T(8,128)S(1)}, f32[8,30,3,128]{3,0,2,1:T(8,128)S(1)}, u32[]{:S(2)}, u32[]{:S(2)}) collective-permute-start(f32[8,30,3,128]{3,0,2,1:T(8,128)S(1)} %pad_maximum_fusion), channel_id=1, source_target_pairs={{1,0},{2,1},{3,2},{0,3},{5,4},{6,5},{7,6},{4,7},{9,8},{10,9},{11,1... | collective-permute-start | bytes 1105928 | tf_op jit(solution)/shard_map/ppermute | solution.py:654
  33.4 17.0 %collective-permute-start.3 = (f32[8,30,2,128]{3,0,2,1:T(8,128)S(1)}, f32[8,30,2,128]{3,0,2,1:T(8,128)S(1)}, u32[]{:S(2)}, u32[]{:S(2)}) collective-permute-start(f32[8,30,2,128]{3,0,2,1:T(8,128)S(1)} %pad_maximum_fusion.1), channel_id=1, source_target_pairs={{0,1},{1,2},{2,3},{3,0},{4,5},{5,6},{6,7},{7,4},{8,9},{9,10},{10,1... | collective-permute-start | bytes 737288 | tf_op jit(solution)/shard_map/ppermute | solution.py:654
  104.4 13.2 %collective-permute-start.4 = (f32[3,104,128]{2,1,0:T(8,128)S(1)}, f32[3,104,128]{2,1,0:T(8,128)S(1)}, u32[]{:S(2)}, u32[]{:S(2)}) collective-permute-start(f32[3,104,128]{2,1,0:T(8,128)S(1)} %get-tuple-element.57), channel_id=1, source_target_pairs={{0,4},{4,8},{8,12},{12,16},{16,20},{20,24},{24,28},{1,5},{5,9},{9,... | collective-permute-start | bytes 479240 | tf_op jit(solution)/shard_map/ppermute | solution.py:654
  106.4 11.3 %copy-start = (f32[30,104,128]{2,1,0:T(8,128)S(1)}, f32[30,104,128]{2,1,0:T(8,128)}, u32[]{:S(2)}) copy-start(f32[30,104,128]{2,1,0:T(8,128)} %parent_level.1) | copy-start | bytes 4792324
  106.4 11.3 %collective-permute-start.5 = (f32[3,104,128]{2,1,0:T(8,128)S(1)}, f32[3,104,128]{2,1,0:T(8,128)S(1)}, u32[]{:S(2)}, u32[]{:S(2)}) collective-permute-start(f32[3,104,128]{2,1,0:T(8,128)S(1)} %get-tuple-element.58), channel_id=1, source_target_pairs={{4,0},{8,4},{12,8},{16,12},{20,16},{24,20},{28,24},{5,1},{9,5},{13... | collective-permute-start | bytes 479240 | tf_op jit(solution)/shard_map/ppermute | solution.py:654
  117.8 5.8 %collective-permute-start.6 = (f32[24,3,128]{2,1,0:T(4,128)S(1)}, f32[24,3,128]{2,1,0:T(4,128)S(1)}, u32[]{:S(2)}, u32[]{:S(2)}) collective-permute-start(f32[24,3,128]{2,1,0:T(4,128)S(1)} %slice.57), channel_id=1, source_target_pairs={{0,1},{1,2},{2,3},{3,0},{4,5},{5,6},{6,7},{7,4},{8,9},{9,10},{10,1... | collective-permute-start | bytes 110600 | tf_op jit(solution)/shard_map/ppermute | solution.py:654
  117.9 5.7 %collective-permute-start.7 = (f32[24,2,128]{2,1,0:T(2,128)S(1)}, f32[24,2,128]{2,1,0:T(2,128)S(1)}, u32[]{:S(2)}, u32[]{:S(2)}) collective-permute-start(f32[24,2,128]{2,1,0:T(2,128)S(1)} %slice.58), channel_id=1, source_target_pairs={{1,0},{2,1},{3,2},{0,3},{5,4},{6,5},{7,6},{4,7},{9,8},{10,9},{11,1... | collective-permute-start | bytes 73736 | tf_op jit(solution)/shard_map/ppermute | solution.py:654

commit v10 on v9

--- a/solution.py
+++ b/solution.py
@@ -155,7 +155,10 @@
         out_specs=pl.BlockSpec((1, LANES // 2 * tile, LANES), lambda s: (chunk, jnp.maximum(s - 2, 0), 0)),
         out_shape=jax.ShapeDtypeStruct((count, LANES * tile, LANES), F32),
         input_output_aliases=aliases,
-        scratch_shapes=[pltpu.VMEM((LANES * (tile + 8), LANES), F32), pltpu.VMEM((3, LANES * 8, LANES), F32)],
+        scratch_shapes=[
+            pltpu.VMEM((LANES * (tile + 8) + tile + 8, LANES), F32),
+            pltpu.VMEM((3, LANES * 8 + 8, LANES), F32),
+        ],
         compiler_params=pltpu.CompilerParams(vmem_limit_bytes=60 * MIB),
         cost_estimate=pl.CostEstimate(
             flops=work * sources.shape[0] * 32, bytes_accessed=work * 72, transcendentals=0
@@ -234,8 +237,8 @@
         out_shape=jax.ShapeDtypeStruct(shape, F32),
         input_output_aliases=aliases,
         scratch_shapes=[
-            pltpu.VMEM((LANES * (8 // packed), LANES), F32),
-            pltpu.VMEM((LANES * (tile + 8), LANES), F32),
+            pltpu.VMEM((LANES * (8 // packed) + 8, LANES), F32),
+            pltpu.VMEM((LANES * (tile + 8) + tile + 8, LANES), F32),
             pltpu.VMEM((16, 8, LANES), F32),
         ],
         compiler_params=pltpu.CompilerParams(vmem_limit_bytes=60 * MIB),
@@ -366,7 +369,7 @@
     lowered,
 ):
     (rows, columns, rows_up, columns_up, parents, entries, table_steps, table_rows) = sizes
-    pitch, f_pad = wide_even.shape[1] // 128, wide_even.shape[2]
+    pitch, f_pad = wide_even.shape[1] // 129, wide_even.shape[2]
     t_pad = pitch - 8
     p_pad, q_pad = phase_ref.shape[1], phase_ref.shape[2]
     row_tiles, lane_tiles = p_pad // 8, q_pad // LANES
@@ -618,14 +621,14 @@
         out_specs=pl.BlockSpec((rows + 6, columns + 8, 8 * parents), lambda g: (0, 0, 0)),
         out_shape=jax.ShapeDtypeStruct((rows + 6, columns + 8, 8 * parents), F32),
         scratch_shapes=[
-            pltpu.VMEM((2, 128 * (t_pad + 8), f_pad), F32),
-            pltpu.VMEM((2, 128 * (t_pad + 8), f_pad), F32),
+            pltpu.VMEM((2, 129 * (t_pad + 8), f_pad), F32),
+            pltpu.VMEM((2, 129 * (t_pad + 8), f_pad), F32),
             pltpu.VMEM((4, parents * p_pad, 3 * f_pad), BF16),
-            pltpu.VMEM((q_pad // LANES * (p_pad // 8), 2, translators * 8, LANES), F32),
+            pltpu.VMEM((q_pad // LANES * (p_pad // 8), 2, translators * 8 + 8, LANES), F32),
             pltpu.VMEM((q_pad // LANES * (p_pad // 8), parents * 96, LANES), F32),
             pltpu.VMEM((8 * parents * p_pad, q_pad), BF16),
             pltpu.VMEM((8 * parents * p_pad, q_pad), BF16),
-            pltpu.VMEM((8 * parents * (t_pad + 8), f_pad), F32),
+            pltpu.VMEM(((8 * parents + 1) * (t_pad + 8), f_pad), F32),
         ],
         compiler_params=pltpu.CompilerParams(vmem_limit_bytes=60 * MIB),
         cost_estimate=pl.CostEstimate(

time: 139 us -> 139 us (level)
  transfers between devices with their start and end apart: 8 -> 8, of which waited for: 3 -> 3; matrix products, arithmetic and copies ran while one was open for 2% -> 2% of each run, Pallas kernels for 26% -> 25%
where the time goes in v10:
time: 139 us; the launch traced here: 138 us
  Pallas kernels  99.9 us (72%)
  starting transfers between devices  19.1 us (14%)
  waiting for transfers between devices  8.91 us (6%)
  local copies, waits for them, and re-layouts  8.56 us (6%)
  other arithmetic  1.59 us (1%)
    pallas_call x1, Pallas kernels, parent_level(): pl.pallas_call(functools.partial(parent_kernel, (rows, columns, rows_up,...  51.6 us
    pallas_call x3, Pallas kernels, child_translate(): pl.pallas_call(functools.partial(translate_kernel, packed, rows), grid=(4...  32.7 us
    ppermute x8, starting transfers between devices, send(): lax.ppermute(block, axis, pairs if up else [(b, a) for a, b in pairs])  19.1 us
    pallas_call x2, Pallas kernels, final_sum(): pl.pallas_call(functools.partial(sum_kernel, packed, rows, LANES // 8), g...  13.8 us
    ppermute x8, waiting for transfers between devices, send(): lax.ppermute(block, axis, pairs if up else [(b, a) for a, b in pairs])  8.91 us
    slice x10, local copies, waits for them, and re-layouts, per_device(): edge[:, :, at]  4.26 us
  transfers between devices with their start and end apart: 8, of which 3 were waited for; matrix products, arithmetic and copies ran while one was open for 2% of the time, Pallas kernels for 25%

profile of v10, /device:TPU:28, one launch (start us, length us, event | category | flops | bytes accessed | tf_op | source)
XLA Modules:
  0.0 138.2 jit_solution(15728179902530756161)
XLA Ops:
  0.0 1.8 %fusion.1 = (f32[8,3,96,128]{3,2,1,0:T(8,128)S(1)}, f32[8,3,96,128]{3,2,1,0:T(8,128)S(1)}) fusion(f32[8,24,96,128]{3,2,1,0:T(8,128)} %param.12), kind=kLoop, calls=%fused_computation.6 | loop fusion | bytes 4718592 | tf_op jit(solution)/shard_map/slice | solution.py:703
  1.8 1.9 %collective-permute-start.1 = (f32[8,3,96,128]{3,2,1,0:T(8,128)S(1)}, f32[8,3,96,128]{3,2,1,0:T(8,128)S(1)}, u32[]{:S(2)}, u32[]{:S(2)}) collective-permute-start(f32[8,3,96,128]{3,2,1,0:T(8,128)S(1)} %get-tuple-element.55), channel_id=1, source_target_pairs={{0,4},{4,8},{8,12},{12,16},{16,20},{20,24},{24,28},{1,5},{5,9},{9,... | collective-permute-start | bytes 3538952 | tf_op jit(solution)/shard_map/ppermute | solution.py:657
  3.7 4.5 %collective-permute-start = (f32[8,3,96,128]{3,2,1,0:T(8,128)S(1)}, f32[8,3,96,128]{3,2,1,0:T(8,128)}, u32[]{:S(2)}, u32[]{:S(2)}) collective-permute-start(f32[8,3,96,128]{3,2,1,0:T(8,128)S(1)} %get-tuple-element.56), channel_id=1, source_target_pairs={{4,0},{8,4},{12,8},{16,12},{20,16},{24,20},{28,24},{5,1},{9,5},{13... | collective-permute-start | bytes 3538952 | tf_op jit(solution)/shard_map/ppermute | solution.py:657
  8.3 1.2 slice.47
  9.5 1.2 slice.42
  10.7 0.1 copy.23
  10.8 0.2 copy.22
  11.0 1.8 %tables.1 = (bf16[128,256]{1,0:T(8,128)(2,1)}, f32[48,32]{1,0:T(8,128)}, f32[48,32]{1,0:T(8,128)}, f32[4,48,256]{2,1,0:T(8,128)}, f32[16,18,128]{2,1,0:T(8,128)}) custom-call(s32[1,128]{1,0:T(1,128)} %bitcast.27, f32[48,32]{1,0:T(8,128)} %constant.12.clone.polar_up_ref), custom_call_target="tpu_custom_call" | custom-call | tf_op jit(solution)/shard_map/tables/pallas_call | solution.py:331
  12.8 13.1 %child_translate.3.rest_0_ = f32[2,8192,128]{2,1,0:T(8,128)} custom-call(s32[12,128]{1,0:T(8,128)} %bitcast.21, s32[12,128]{1,0:T(8,128)} %bitcast.24, f32[2,4,2304,128]{3,2,1,0:T(8,128)} %bitcast.11, f32[2,2304,128]{2,1,0:T(8,128)} %bitcast.15), custom_call_target="tpu_custom_call" | custom-call | flops 50331648 | bytes 9437184 | tf_op jit(solution)/shard_map/child_translate/pallas_call | solution.py:151
  25.8 4.2 %collective-permute-done.1 = f32[8,3,96,128]{3,2,1,0:T(8,128)S(1)} collective-permute-done((f32[8,3,96,128]{3,2,1,0:T(8,128)S(1)}, f32[8,3,96,128]{3,2,1,0:T(8,128)S(1)}, u32[]{:S(2)}, u32[]{:S(2)}) %collective-permute-start.1) | collective-permute-done | bytes 1179680 | tf_op jit(solution)/shard_map/ppermute | solution.py:657
  30.1 0.0 copy-start.1
  30.1 0.9 collective-permute-done
  31.0 0.9 slice.48
  31.9 0.9 slice.45
  32.9 0.5 collective-permute-start.2
  33.4 3.4 %collective-permute-start.3 = (f32[8,30,2,128]{3,0,2,1:T(8,128)S(1)}, f32[8,30,2,128]{3,0,2,1:T(8,128)S(1)}, u32[]{:S(2)}, u32[]{:S(2)}) collective-permute-start(f32[8,30,2,128]{3,0,2,1:T(8,128)S(1)} %pad_maximum_fusion.1), channel_id=1, source_target_pairs={{0,1},{1,2},{2,3},{3,0},{4,5},{5,6},{6,7},{7,4},{8,9},{9,10},{10,1... | collective-permute-start | bytes 737288 | tf_op jit(solution)/shard_map/ppermute | solution.py:657
  36.8 0.1 pad.22.clone
  36.9 13.1 %child_translate.4.local_ref = f32[2,8192,128]{2,1,0:T(8,128)} custom-call(s32[12,128]{1,0:T(8,128)} %bitcast.22, s32[12,128]{1,0:T(8,128)} %bitcast.25, f32[2,4,2304,128]{3,2,1,0:T(8,128)} %bitcast.12, f32[2,2304,128]{2,1,0:T(8,128)} %bitcast.16, f32[2,8192,128]{2,1,0:T(8,128)} %child_translate.3.rest_0_), custom_call_target="tpu_custom_call", output_to_operand_aliasing={{}: (4, {})} | custom-call | flops 50331648 | bytes 9437184 | tf_op jit(solution)/shard_map/child_translate/pallas_call | solution.py:151
  50.0 0.0 copy-done.1
  50.0 0.0 collective-permute-done.3
  50.0 0.0 collective-permute-done.2
  50.0 0.2 maximum_maximum_fusion
  50.2 1.1 copy.21
  51.3 51.6 %parent_level.1 = f32[30,104,128]{2,1,0:T(8,128)} custom-call(s32[16,12]{1,0:T(8,128)} %source_ref.1, s32[16,12]{1,0:T(8,128)} %kind_ref.1, f32[2,4,24,96,128]{4,3,2,1,0:T(8,128)} %bitcast.13, f32[2,4,3,96,128]{4,3,2,1,0:T(8,128)} %bitcast.6.next_ref, f32[2,4,3,96,128]{4,3,2,1,0:T(8,128)} %bitcast.28, f32[2,4,30,8,128]{4,3,2,1,0:T(8,128)} %bitcast.20, ...), custom_call_target="tpu_custom_call" | custom-call | flops 20000000000 | bytes 18874368 | tf_op jit(solution)/shard_map/parent_level/pallas_call | solution.py:604
  102.9 1.0 fusion.2
  104.0 1.9 %collective-permute-start.4 = (f32[3,104,128]{2,1,0:T(8,128)S(1)}, f32[3,104,128]{2,1,0:T(8,128)S(1)}, u32[]{:S(2)}, u32[]{:S(2)}) collective-permute-start(f32[3,104,128]{2,1,0:T(8,128)S(1)} %get-tuple-element.57), channel_id=1, source_target_pairs={{0,4},{4,8},{8,12},{12,16},{16,20},{20,24},{24,28},{1,5},{5,9},{9,... | collective-permute-start | bytes 479240 | tf_op jit(solution)/shard_map/ppermute | solution.py:657
  105.9 0.0 copy-start
  105.9 4.7 %collective-permute-start.5 = (f32[3,104,128]{2,1,0:T(8,128)S(1)}, f32[3,104,128]{2,1,0:T(8,128)S(1)}, u32[]{:S(2)}, u32[]{:S(2)}) collective-permute-start(f32[3,104,128]{2,1,0:T(8,128)S(1)} %get-tuple-element.58), channel_id=1, source_target_pairs={{4,0},{8,4},{12,8},{16,12},{20,16},{24,20},{28,24},{5,1},{9,5},{13... | collective-permute-start | bytes 479240 | tf_op jit(solution)/shard_map/ppermute | solution.py:657
  110.6 6.5 %child_translate.5.local_ref = f32[1,2048,128]{2,1,0:T(8,128)} custom-call(s32[12,128]{1,0:T(8,128)} %bitcast.23, s32[12,128]{1,0:T(8,128)} %bitcast.26, f32[2,4,2304,128]{3,2,1,0:T(8,128)} %bitcast.14, f32[2,2304,128]{2,1,0:T(8,128)} %bitcast.17), custom_call_target="tpu_custom_call" | custom-call | flops 12582912 | bytes 2359296 | tf_op jit(solution)/shard_map/child_translate/pallas_call | solution.py:151
  117.0 0.0 collective-permute-done.4
  117.0 0.0 collective-permute-done.5
  117.0 0.0 copy-done
  117.1 0.1 pad_add_fusion
  117.2 0.2 collective-permute-start.6
  117.4 1.9 %collective-permute-start.7 = (f32[24,2,128]{2,1,0:T(2,128)S(1)}, f32[24,2,128]{2,1,0:T(2,128)S(1)}, u32[]{:S(2)}, u32[]{:S(2)}) collective-permute-start(f32[24,2,128]{2,1,0:T(2,128)S(1)} %slice.58), channel_id=1, source_target_pairs={{1,0},{2,1},{3,2},{0,3},{5,4},{6,5},{7,6},{4,7},{9,8},{10,9},{11,1... | collective-permute-start | bytes 73736 | tf_op jit(solution)/shard_map/ppermute | solution.py:657
  119.3 3.8 %collective-permute-done.7 = f32[24,2,128]{2,1,0:T(2,128)S(1)} collective-permute-done((f32[24,2,128]{2,1,0:T(2,128)S(1)}, f32[24,2,128]{2,1,0:T(2,128)S(1)}, u32[]{:S(2)}, u32[]{:S(2)}) %collective-permute-start.7) | collective-permute-done | bytes 24608 | tf_op jit(solution)/shard_map/ppermute | solution.py:657
  123.1 0.0 collective-permute-done.6
  123.1 1.3 fusion
  124.4 10.8 %final_sum.2.rest_0_ = f32[2,4,2304,128]{3,2,1,0:T(8,128)} custom-call(s32[128]{0:T(128)} %slot_ref.3, f32[2,8192,128]{2,1,0:T(8,128)} %child_translate.4.local_ref, f32[2304,128]{1,0:T(8,128)} %bitcast.18, f32[16,18,128]{2,1,0:T(8,128)} %get-tuple-element.53.phase_ref), custom_call_target="tpu_custom_call" | custom-call | flops 8388608 | bytes 18874368 | tf_op jit(solution)/shard_map/final_sum/pallas_call | solution.py:232
  135.2 3.0 %final_sum.3 = f32[2,4,2304,128]{3,2,1,0:T(8,128)} custom-call(s32[128]{0:T(128)} %slot_ref.3, f32[1,2048,128]{2,1,0:T(8,128)} %child_translate.5.local_ref, f32[2304,128]{1,0:T(8,128)} %bitcast.19, f32[16,18,128]{2,1,0:T(8,128)} %get-tuple-element.53.phase_ref, f32[2,4,2304,128]{3,2,1,0:T(8,128)} %final_sum.2.rest_0_), custom_call_target="tpu_custom_call", output_to_operand_aliasing={{}: (4, {})} | custom-call | flops 1048576 | bytes 2359296 | tf_op jit(solution)/shard_map/final_sum/pallas_call | solution.py:232
  (11 shorter events, 0.1 us)
Async XLA Ops:
  1.8 28.2 %collective-permute-start.1 = (f32[8,3,96,128]{3,2,1,0:T(8,128)S(1)}, f32[8,3,96,128]{3,2,1,0:T(8,128)S(1)}, u32[]{:S(2)}, u32[]{:S(2)}) collective-permute-start(f32[8,3,96,128]{3,2,1,0:T(8,128)S(1)} %get-tuple-element.55), channel_id=1, source_target_pairs={{0,4},{4,8},{8,12},{12,16},{16,20},{20,24},{24,28},{1,5},{5,9},{9,... | collective-permute-start | bytes 3538952 | tf_op jit(solution)/shard_map/ppermute | solution.py:657
  3.7 27.2 %collective-permute-start = (f32[8,3,96,128]{3,2,1,0:T(8,128)S(1)}, f32[8,3,96,128]{3,2,1,0:T(8,128)}, u32[]{:S(2)}, u32[]{:S(2)}) collective-permute-start(f32[8,3,96,128]{3,2,1,0:T(8,128)S(1)} %get-tuple-element.56), channel_id=1, source_target_pairs={{4,0},{8,4},{12,8},{16,12},{20,16},{24,20},{28,24},{5,1},{9,5},{13... | collective-permute-start | bytes 3538952 | tf_op jit(solution)/shard_map/ppermute | solution.py:657
  30.1 20.0 %copy-start.1 = (f32[8,3,96,128]{3,2,1,0:T(8,128)}, f32[8,3,96,128]{3,2,1,0:T(8,128)S(1)}, u32[]{:S(2)}) copy-start(f32[8,3,96,128]{3,2,1,0:T(8,128)S(1)} %collective-permute-done.1) | copy-start | bytes 3538948
  32.9 17.1 %collective-permute-start.2 = (f32[8,30,3,128]{3,0,2,1:T(8,128)S(1)}, f32[8,30,3,128]{3,0,2,1:T(8,128)S(1)}, u32[]{:S(2)}, u32[]{:S(2)}) collective-permute-start(f32[8,30,3,128]{3,0,2,1:T(8,128)S(1)} %pad_maximum_fusion), channel_id=1, source_target_pairs={{1,0},{2,1},{3,2},{0,3},{5,4},{6,5},{7,6},{4,7},{9,8},{10,9},{11,1... | collective-permute-start | bytes 1105928 | tf_op jit(solution)/shard_map/ppermute | solution.py:657
  33.4 16.6 %collective-permute-start.3 = (f32[8,30,2,128]{3,0,2,1:T(8,128)S(1)}, f32[8,30,2,128]{3,0,2,1:T(8,128)S(1)}, u32[]{:S(2)}, u32[]{:S(2)}) collective-permute-start(f32[8,30,2,128]{3,0,2,1:T(8,128)S(1)} %pad_maximum_fusion.1), channel_id=1, source_target_pairs={{0,1},{1,2},{2,3},{3,0},{4,5},{5,6},{6,7},{7,4},{8,9},{9,10},{10,1... | collective-permute-start | bytes 737288 | tf_op jit(solution)/shard_map/ppermute | solution.py:657
  104.0 13.1 %collective-permute-start.4 = (f32[3,104,128]{2,1,0:T(8,128)S(1)}, f32[3,104,128]{2,1,0:T(8,128)S(1)}, u32[]{:S(2)}, u32[]{:S(2)}) collective-permute-start(f32[3,104,128]{2,1,0:T(8,128)S(1)} %get-tuple-element.57), channel_id=1, source_target_pairs={{0,4},{4,8},{8,12},{12,16},{16,20},{20,24},{24,28},{1,5},{5,9},{9,... | collective-permute-start | bytes 479240 | tf_op jit(solution)/shard_map/ppermute | solution.py:657
  105.9 11.2 %copy-start = (f32[30,104,128]{2,1,0:T(8,128)S(1)}, f32[30,104,128]{2,1,0:T(8,128)}, u32[]{:S(2)}) copy-start(f32[30,104,128]{2,1,0:T(8,128)} %parent_level.1) | copy-start | bytes 4792324
  105.9 11.2 %collective-permute-start.5 = (f32[3,104,128]{2,1,0:T(8,128)S(1)}, f32[3,104,128]{2,1,0:T(8,128)S(1)}, u32[]{:S(2)}, u32[]{:S(2)}) collective-permute-start(f32[3,104,128]{2,1,0:T(8,128)S(1)} %get-tuple-element.58), channel_id=1, source_target_pairs={{4,0},{8,4},{12,8},{16,12},{20,16},{24,20},{28,24},{5,1},{9,5},{13... | collective-permute-start | bytes 479240 | tf_op jit(solution)/shard_map/ppermute | solution.py:657
  117.2 5.9 %collective-permute-start.6 = (f32[24,3,128]{2,1,0:T(4,128)S(1)}, f32[24,3,128]{2,1,0:T(4,128)S(1)}, u32[]{:S(2)}, u32[]{:S(2)}) collective-permute-start(f32[24,3,128]{2,1,0:T(4,128)S(1)} %slice.57), channel_id=1, source_target_pairs={{0,1},{1,2},{2,3},{3,0},{4,5},{5,6},{6,7},{7,4},{8,9},{9,10},{10,1... | collective-permute-start | bytes 110600 | tf_op jit(solution)/shard_map/ppermute | solution.py:657
  117.4 5.7 %collective-permute-start.7 = (f32[24,2,128]{2,1,0:T(2,128)S(1)}, f32[24,2,128]{2,1,0:T(2,128)S(1)}, u32[]{:S(2)}, u32[]{:S(2)}) collective-permute-start(f32[24,2,128]{2,1,0:T(2,128)S(1)} %slice.58), channel_id=1, source_target_pairs={{1,0},{2,1},{3,2},{0,3},{5,4},{6,5},{7,6},{4,7},{9,8},{10,9},{11,1... | collective-permute-start | bytes 73736 | tf_op jit(solution)/shard_map/ppermute | solution.py:657
